TPU v7x, 32 devices: a whole 2x2x4 slice. The times are simulated.
32 devices in a mesh: dp: 8 (over z, y), seq: 4 (over x, core).
Axes of the slice: x: 2, y: 2, z: 4, core: 2. Of those that a mesh axis runs over, the one named last changes fastest.
Arguments:
- block_input: bfloat16 [16384, 768], P(('dp', 'seq')), may hold values from -6 to 6
- teacher: bfloat16 [16384, 768], P(('dp', 'seq')), may hold values from -6 to 6
- prev_logits: float32 [16384, 12], P(('dp', 'seq')), may hold values from -3 to 3
- valid_mask: int32 [16384], P(('dp', 'seq')), may hold values from 0 to 1, as said below
- segments: int32 [16384], P(('dp', 'seq')), may hold values from 0 to 256, as said below
- routes: int32 [16384, 2], P(('dp', 'seq')), may hold values from 0 to 11, all different within a row; in each aligned block of 512 rows (0 to 511, 512 to 1023, ...) at most 160 rows name the same one
- input_proj: bfloat16 [768, 2304], P(('dp', 'seq')), may hold values from -0.21875 to 0.21875
- output_proj: bfloat16 [768, 768], P(('dp', 'seq')), may hold values from -0.875 to 0.875
- attention_gain: bfloat16 [768], P(('dp', 'seq')), may hold values from 0.5 to 1.5
- mixture_gain: bfloat16 [768], P(('dp', 'seq')), may hold values from 0.5 to 1.5
- router: bfloat16 [768, 12], P(('dp', 'seq')), may hold values from -0.15625 to 0.15625
- const_mix: bfloat16 [768, 4], P(('dp', 'seq')), may hold values from -0.21875 to 0.21875
- const_vectors: bfloat16 [2, 768], P(None, ('dp', 'seq')), may hold values from -5 to 5
- expert_gate: bfloat16 [8, 768, 2048], P('seq', 'dp'), may hold values from -0.21875 to 0.21875
- expert_up: bfloat16 [8, 768, 2048], P('seq', 'dp'), may hold values from -0.21875 to 0.21875
- expert_down: bfloat16 [8, 2048, 768], P('seq', 'dp'), may hold values from -0.25 to 0.25
Outputs:
- block_output: bfloat16 [16384, 768], P(('dp', 'seq'))
- mean_loss: float32 [], replicated
- grad_input: float32 [16384, 768], P(('dp', 'seq'))
- grad_input_proj: float32 [768, 2304], P(('dp', 'seq'))
- grad_output_proj: float32 [768, 768], P(('dp', 'seq'))
- grad_attention_gain: float32 [768], P(('dp', 'seq'))
- grad_mixture_gain: float32 [768], P(('dp', 'seq'))
- grad_router: float32 [768, 12], P(('dp', 'seq'))
- grad_const_mix: float32 [768, 4], P(('dp', 'seq'))
- grad_const_vectors: float32 [2, 768], P(None, ('dp', 'seq'))
- grad_expert_gate: float32 [8, 768, 2048], P('seq', 'dp')
- grad_expert_up: float32 [8, 768, 2048], P('seq', 'dp')
- grad_expert_down: float32 [8, 2048, 768], P('seq', 'dp')
Inputs may be any that keep to these rules, and one draw needn't show every extreme that they name: `valid_mask`: each sequence of 2048 tokens is valid on a leading run of more than 1536 tokens and pad after it. `segments`: never falling within a sequence, starting at 0; one document of each sequence begins within its first 256 tokens and runs to the end of its valid tokens; trailing pad, where there is any, has the number 512 // 2 and every valid token a smaller one. A token's two routes differ; among the 512 rows of one device no expert is chosen by more than 160 rows.
All inputs are finite; a program needn't handle non-finite values.
Results may differ from a plain program's by a relative error of at most 0.0088.
Values may be sent and summed in bfloat16 or wider, within the bound.
No kernel may reach another device: no remote copies, remote signals or barrier semaphores. Data moves between devices by JAX's collectives and lax.ppermute only.
A program may use at most 192 MiB of HBM per device.

v0:
```python
import jax
import jax.numpy as jnp
from jax import lax
from jax.sharding import PartitionSpec as P

HEAD = 64
EXPERTS = 8
ROUTES = 12
CAP = 160


exact = lax.Precision.HIGHEST
epsilon = 1e-06
masked_out = -1e30


def rms_scale(values):
    return lax.rsqrt(jnp.mean(values * values, -1, keepdims=True) + epsilon)


def dot_rows(left, right, precision=None):
    return lax.dot_general(
        left,
        right,
        (((0,), (0,)), ((), ())),
        preferred_element_type=jnp.float32,
        precision=precision,
    )


def dot_last(left, right, precision=None):
    return lax.dot_general(
        left,
        right,
        (((1,), (1,)), ((), ())),
        preferred_element_type=jnp.float32,
        precision=precision,
    )


def body(
    block_input,
    teacher,
    prev_logits,
    valid_mask,
    segments,
    routes,
    input_proj,
    output_proj,
    attention_gain,
    mixture_gain,
    router,
    const_mix,
    const_vectors,
    expert_gate,
    expert_up,
    expert_down,
):
    tokens_here = block_input.shape[0]
    features = block_input.shape[1]
    devices_all = lax.axis_size("dp") * lax.axis_size("seq")

    def dense_weights():
        return (
            lax.all_gather(input_proj, ("dp", "seq"), axis=0, tiled=True),
            lax.all_gather(output_proj, ("dp", "seq"), axis=0, tiled=True),
            lax.all_gather(attention_gain, ("dp", "seq"), axis=0, tiled=True),
            lax.all_gather(mixture_gain, ("dp", "seq"), axis=0, tiled=True),
            lax.all_gather(router, ("dp", "seq"), axis=0, tiled=True),
            lax.all_gather(const_mix, ("dp", "seq"), axis=0, tiled=True),
            lax.all_gather(const_vectors, ("dp", "seq"), axis=1, tiled=True),
        )

    def expert_weights():
        return (
            lax.all_gather(expert_gate, "dp", axis=1, tiled=True),
            lax.all_gather(expert_up, "dp", axis=1, tiled=True),
            lax.all_gather(expert_down, "dp", axis=1, tiled=True),
        )

    full_in, full_out, gain_first, gain_second, full_router, full_mix, full_vectors = (
        dense_weights()
    )
    inputs_f = block_input.astype(jnp.float32)
    scale_first = rms_scale(inputs_f)
    unit_first = inputs_f * scale_first
    normed_first = (unit_first * gain_first.astype(jnp.float32)).astype(jnp.bfloat16)
    projected = jnp.dot(normed_first, full_in, preferred_element_type=jnp.float32).astype(
        jnp.bfloat16
    )
    query_heads, key_heads, value_heads = (
        lax.all_to_all(projected[:, :features], "seq", split_axis=1, concat_axis=0, tiled=True),
        lax.all_to_all(
            projected[:, features : 2 * features], "seq", split_axis=1, concat_axis=0, tiled=True
        ),
        lax.all_to_all(
            projected[:, 2 * features :], "seq", split_axis=1, concat_axis=0, tiled=True
        ),
    )
    seq_segments = lax.all_gather(segments, "seq", axis=0, tiled=True)
    length = query_heads.shape[0]
    heads_here = query_heads.shape[1] // HEAD
    query_three = query_heads.reshape(length, heads_here, HEAD)
    key_three = key_heads.reshape(length, heads_here, HEAD)
    value_three = value_heads.reshape(length, heads_here, HEAD)
    block_rows = min(512, length)
    block_count = length // block_rows
    scaling = HEAD ** (-0.5)
    key_positions = jnp.arange(length)

    def block_scores(block_id):
        first_row = block_id * block_rows
        query_block = lax.dynamic_slice_in_dim(query_three, first_row, block_rows, 0)
        segment_block = lax.dynamic_slice_in_dim(seq_segments, first_row, block_rows, 0)
        scores = (
            jnp.einsum("qhd,khd->hqk", query_block, key_three, preferred_element_type=jnp.float32)
            * scaling
        )
        allowed = (seq_segments[None, :] == segment_block[:, None]) & (
            key_positions[None, :] <= first_row + jnp.arange(block_rows)[:, None]
        )
        return (query_block, jnp.where(allowed[None], scores, masked_out))

    def forward_block(block_id):
        query_block, scores = block_scores(block_id)
        row_max = jnp.max(scores, -1, keepdims=True)
        expo = jnp.exp(scores - row_max)
        row_total = jnp.sum(expo, -1, keepdims=True)
        weights = (expo / row_total).astype(jnp.bfloat16)
        attended = jnp.einsum(
            "hqk,khd->qhd", weights, value_three, preferred_element_type=jnp.float32
        )
        return (attended.astype(jnp.bfloat16), (row_max + jnp.log(row_total))[..., 0])

    attended_blocks, log_totals = lax.map(forward_block, jnp.arange(block_count))
    attended_heads = attended_blocks.reshape(length, heads_here * HEAD)
    attended_tok = lax.all_to_all(attended_heads, "seq", split_axis=0, concat_axis=1, tiled=True)
    residual_mid = inputs_f + jnp.dot(attended_tok, full_out, preferred_element_type=jnp.float32)
    scale_second = rms_scale(residual_mid)
    unit_second = residual_mid * scale_second
    gain_mid = gain_second.astype(jnp.float32)
    normed = unit_second * gain_mid
    router_f = full_router.astype(jnp.float32)
    route_probs = jax.nn.softmax(jnp.dot(normed, router_f, precision=exact) + prev_logits, -1)
    onehot = (routes[:, :, None] == jnp.arange(ROUTES, dtype=jnp.int32)[None, None, :]).astype(
        jnp.float32
    )
    picked = jnp.sum(onehot * route_probs[:, None, :], -1)
    picked_sum = jnp.sum(picked, -1, keepdims=True)
    gate_weights = picked / picked_sum
    weights_all = jnp.sum(gate_weights[:, :, None] * onehot, 1)
    mix_f = full_mix.astype(jnp.float32)
    vectors_f = full_vectors.astype(jnp.float32)
    mix_weights = jax.nn.softmax(
        jnp.dot(normed, mix_f, precision=exact).reshape(tokens_here, 2, 2), -1
    )
    const_out = mix_weights[..., 0:1] * normed[:, None, :] + mix_weights[..., 1:2] * vectors_f[None]
    copy_weight = weights_all[:, EXPERTS + 1 : EXPERTS + 2]
    const_weight = weights_all[:, EXPERTS + 2 : EXPERTS + 4]
    local_terms = copy_weight * normed + jnp.sum(const_weight[:, :, None] * const_out, 1)
    flat_routes = routes.reshape(-1)
    onehot_e = (flat_routes[:, None] == jnp.arange(EXPERTS, dtype=jnp.int32)[None, :]).astype(
        jnp.int32
    )
    slot_rank = jnp.sum((jnp.cumsum(onehot_e, 0) - onehot_e) * onehot_e, -1)
    slot_dest = jnp.where(flat_routes < EXPERTS, flat_routes * CAP + slot_rank, EXPERTS * CAP)
    slot_source = (
        jnp.full((EXPERTS * CAP + 1,), 2 * tokens_here, jnp.int32)
        .at[slot_dest]
        .set(jnp.arange(2 * tokens_here, dtype=jnp.int32))[: EXPERTS * CAP]
    )
    normed_pad = jnp.concatenate(
        [normed.astype(jnp.bfloat16), jnp.zeros((1, features), jnp.bfloat16)], 0
    )
    send_rows = normed_pad[slot_source // 2].reshape(EXPERTS, CAP, features)
    recv_rows = lax.all_to_all(send_rows, "seq", split_axis=0, concat_axis=1, tiled=True)
    gate_full, up_full, down_full = expert_weights()
    gate_part = jnp.einsum("erd,edf->erf", recv_rows, gate_full, preferred_element_type=jnp.float32)
    up_part = jnp.einsum("erd,edf->erf", recv_rows, up_full, preferred_element_type=jnp.float32)
    hidden = (jax.nn.silu(gate_part) * up_part).astype(jnp.bfloat16)
    result_rows = jnp.einsum(
        "erf,efd->erd", hidden, down_full, preferred_element_type=jnp.float32
    ).astype(jnp.bfloat16)
    back_rows = lax.all_to_all(result_rows, "seq", split_axis=1, concat_axis=0, tiled=True)
    back_pad = jnp.concatenate(
        [back_rows.reshape(-1, features), jnp.zeros((1, features), jnp.bfloat16)], 0
    )
    expert_terms = back_pad[slot_dest].astype(jnp.float32).reshape(tokens_here, 2, features)
    full_output = residual_mid + local_terms + jnp.sum(gate_weights[:, :, None] * expert_terms, 1)
    valid_f = valid_mask.astype(jnp.float32)
    differ = full_output - teacher.astype(jnp.float32)
    valid_count, squared = lax.psum(
        (jnp.sum(valid_f), jnp.sum(valid_f[:, None] * differ * differ)), ("dp", "seq")
    )
    mean_loss = squared / (2.0 * features * valid_count)
    grad_full = valid_f[:, None] * differ * (tokens_here * devices_all / valid_count)
    full_in, full_out, gain_first, gain_second, full_router, full_mix, full_vectors = (
        dense_weights()
    )
    gate_full, up_full, down_full = expert_weights()
    gates_pad = jnp.concatenate([gate_weights.reshape(-1), jnp.zeros((1,), jnp.float32)], 0)
    grad_pad = jnp.concatenate([grad_full, jnp.zeros((1, features), jnp.float32)], 0)
    grad_send = (
        (gates_pad[slot_source][:, None] * grad_pad[slot_source // 2])
        .astype(jnp.bfloat16)
        .reshape(EXPERTS, CAP, features)
    )
    grad_recv = lax.all_to_all(grad_send, "seq", split_axis=0, concat_axis=1, tiled=True)
    gate_part = jnp.einsum("erd,edf->erf", recv_rows, gate_full, preferred_element_type=jnp.float32)
    up_part = jnp.einsum("erd,edf->erf", recv_rows, up_full, preferred_element_type=jnp.float32)
    sigmoid_gate = jax.nn.sigmoid(gate_part)
    silu_gate = gate_part * sigmoid_gate
    hidden = (silu_gate * up_part).astype(jnp.bfloat16)
    grad_hidden = jnp.einsum(
        "erd,efd->erf", grad_recv, down_full, preferred_element_type=jnp.float32
    )
    grad_gate_part = (
        grad_hidden * up_part * sigmoid_gate * (1.0 + gate_part * (1.0 - sigmoid_gate))
    ).astype(jnp.bfloat16)
    grad_up_part = (grad_hidden * silu_gate).astype(jnp.bfloat16)
    grad_rows = (
        jnp.einsum("erf,edf->erd", grad_gate_part, gate_full, preferred_element_type=jnp.float32)
        + jnp.einsum("erf,edf->erd", grad_up_part, up_full, preferred_element_type=jnp.float32)
    ).astype(jnp.bfloat16)
    grad_back = lax.all_to_all(grad_rows, "seq", split_axis=1, concat_axis=0, tiled=True)
    grad_back_pad = jnp.concatenate(
        [grad_back.reshape(-1, features), jnp.zeros((1, features), jnp.bfloat16)], 0
    )
    grad_down = jnp.einsum("erf,erd->efd", hidden, grad_recv, preferred_element_type=jnp.float32)
    grad_gate_w = jnp.einsum(
        "erd,erf->edf", recv_rows, grad_gate_part, preferred_element_type=jnp.float32
    )
    grad_up_w = jnp.einsum(
        "erd,erf->edf", recv_rows, grad_up_part, preferred_element_type=jnp.float32
    )
    grad_expert_gate, grad_expert_up, grad_expert_down = (
        lax.psum_scatter(grad_gate_w, "dp", scatter_dimension=1, tiled=True),
        lax.psum_scatter(grad_up_w, "dp", scatter_dimension=1, tiled=True),
        lax.psum_scatter(grad_down, "dp", scatter_dimension=1, tiled=True),
    )
    expert_dot = jnp.sum(grad_full[:, None, :] * expert_terms, -1)
    copy_dot = jnp.sum(grad_full * normed, -1)
    const_dot = jnp.sum(grad_full[:, None, :] * const_out, -1)
    grad_gates = (
        expert_dot
        + onehot[:, :, EXPERTS + 1] * copy_dot[:, None]
        + jnp.sum(onehot[:, :, EXPERTS + 2 : EXPERTS + 4] * const_dot[:, None, :], -1)
    )
    grad_picked = (grad_gates - jnp.sum(gate_weights * grad_gates, -1, keepdims=True)) / picked_sum
    grad_probs = jnp.sum(grad_picked[:, :, None] * onehot, 1)
    grad_logits = route_probs * (grad_probs - jnp.sum(route_probs * grad_probs, -1, keepdims=True))
    grad_router = dot_rows(normed, grad_logits, exact)
    router_f = full_router.astype(jnp.float32)
    mix_f = full_mix.astype(jnp.float32)
    vectors_f = full_vectors.astype(jnp.float32)
    grad_const = const_weight[:, :, None] * grad_full[:, None, :]
    grad_mix = jnp.stack(
        [jnp.sum(grad_const * normed[:, None, :], -1), jnp.sum(grad_const * vectors_f[None], -1)],
        -1,
    )
    grad_z = (
        mix_weights * (grad_mix - jnp.sum(mix_weights * grad_mix, -1, keepdims=True))
    ).reshape(tokens_here, 4)
    grad_const_mix = dot_rows(normed, grad_z, exact)
    grad_const_vectors = jnp.sum(mix_weights[..., 1:2] * grad_const, 0)
    grad_normed = copy_weight * grad_full + dot_last(grad_logits, router_f, exact)
    grad_normed = (
        grad_normed
        + jnp.sum(mix_weights[..., 0:1] * grad_const, 1)
        + dot_last(grad_z, mix_f, exact)
    )
    grad_normed = grad_normed + jnp.sum(
        grad_back_pad[slot_dest].astype(jnp.float32).reshape(tokens_here, 2, features), 1
    )
    grad_mixture_gain = jnp.sum(grad_normed * unit_second, 0)
    gain_mid = gain_second.astype(jnp.float32)
    grad_hat = grad_normed * gain_mid
    grad_mid = grad_full + scale_second * (
        grad_hat - unit_second * jnp.mean(grad_hat * unit_second, -1, keepdims=True)
    )
    grad_branch = grad_mid.astype(jnp.bfloat16)
    grad_output_proj = dot_rows(attended_tok, grad_branch)
    grad_attended = dot_last(grad_branch, full_out).astype(jnp.bfloat16)
    grad_heads = lax.all_to_all(grad_attended, "seq", split_axis=1, concat_axis=0, tiled=True)
    grad_three = grad_heads.reshape(length, heads_here, HEAD)

    def backward_block(carry, block_id):
        grad_key, grad_value = carry
        first_row = block_id * block_rows
        query_block, scores = block_scores(block_id)
        probs_block = jnp.exp(scores - log_totals[block_id][..., None])
        grad_block = lax.dynamic_slice_in_dim(grad_three, first_row, block_rows, 0)
        grad_value = grad_value + jnp.einsum(
            "hqk,qhd->khd",
            probs_block.astype(jnp.bfloat16),
            grad_block,
            preferred_element_type=jnp.float32,
        )
        grad_prob = jnp.einsum(
            "qhd,khd->hqk", grad_block, value_three, preferred_element_type=jnp.float32
        )
        inner = jnp.sum(probs_block * grad_prob, -1, keepdims=True)
        grad_scores = (probs_block * (grad_prob - inner)).astype(jnp.bfloat16)
        grad_query = (
            jnp.einsum("hqk,khd->qhd", grad_scores, key_three, preferred_element_type=jnp.float32)
            * scaling
        )
        grad_key = (
            grad_key
            + jnp.einsum(
                "hqk,qhd->khd", grad_scores, query_block, preferred_element_type=jnp.float32
            )
            * scaling
        )
        return ((grad_key, grad_value), grad_query.astype(jnp.bfloat16))

    zeros_heads = jnp.zeros((length, heads_here, HEAD), jnp.float32)
    (grad_key, grad_value), grad_queries = lax.scan(
        backward_block, (zeros_heads, zeros_heads), jnp.arange(block_count)
    )
    grad_query_tok, grad_key_tok, grad_value_tok = (
        lax.all_to_all(
            grad_queries.reshape(length, heads_here * HEAD),
            "seq",
            split_axis=0,
            concat_axis=1,
            tiled=True,
        ),
        lax.all_to_all(
            grad_key.astype(jnp.bfloat16).reshape(length, heads_here * HEAD),
            "seq",
            split_axis=0,
            concat_axis=1,
            tiled=True,
        ),
        lax.all_to_all(
            grad_value.astype(jnp.bfloat16).reshape(length, heads_here * HEAD),
            "seq",
            split_axis=0,
            concat_axis=1,
            tiled=True,
        ),
    )
    grad_projected = jnp.concatenate([grad_query_tok, grad_key_tok, grad_value_tok], 1)
    grad_input_proj = dot_rows(normed_first, grad_projected)
    grad_normed_first = dot_last(grad_projected, full_in)
    grad_attention_gain = jnp.sum(grad_normed_first * unit_first, 0)
    grad_hat_first = grad_normed_first * gain_first.astype(jnp.float32)
    grad_input = grad_mid + scale_first * (
        grad_hat_first - unit_first * jnp.mean(grad_hat_first * unit_first, -1, keepdims=True)
    )
    dense_out = (
        lax.psum_scatter(grad_input_proj, ("dp", "seq"), scatter_dimension=0, tiled=True),
        lax.psum_scatter(grad_output_proj, ("dp", "seq"), scatter_dimension=0, tiled=True),
        lax.psum_scatter(grad_attention_gain, ("dp", "seq"), scatter_dimension=0, tiled=True),
        lax.psum_scatter(grad_mixture_gain, ("dp", "seq"), scatter_dimension=0, tiled=True),
        lax.psum_scatter(grad_router, ("dp", "seq"), scatter_dimension=0, tiled=True),
        lax.psum_scatter(grad_const_mix, ("dp", "seq"), scatter_dimension=0, tiled=True),
        lax.psum_scatter(grad_const_vectors, ("dp", "seq"), scatter_dimension=1, tiled=True),
    )
    return (
        full_output.astype(jnp.bfloat16),
        mean_loss,
        grad_input,
        dense_out[0],
        dense_out[1],
        dense_out[2],
        dense_out[3],
        dense_out[4],
        dense_out[5],
        dense_out[6],
        grad_expert_gate,
        grad_expert_up,
        grad_expert_down,
    )


def solution(mesh):
    return jax.shard_map(
        body,
        mesh=mesh,
        in_specs=(
            P(("dp", "seq"), None),
            P(("dp", "seq"), None),
            P(("dp", "seq"), None),
            P(("dp", "seq")),
            P(("dp", "seq")),
            P(("dp", "seq"), None),
            P(("dp", "seq"), None),
            P(("dp", "seq"), None),
            P(("dp", "seq")),
            P(("dp", "seq")),
            P(("dp", "seq"), None),
            P(("dp", "seq"), None),
            P(None, ("dp", "seq")),
            P("seq", "dp", None),
            P("seq", "dp", None),
            P("seq", "dp", None),
        ),
        out_specs=(
            P(("dp", "seq"), None),
            P(),
            P(("dp", "seq"), None),
            P(("dp", "seq"), None),
            P(("dp", "seq"), None),
            P(("dp", "seq")),
            P(("dp", "seq")),
            P(("dp", "seq"), None),
            P(("dp", "seq"), None),
            P(None, ("dp", "seq")),
            P("seq", "dp", None),
            P("seq", "dp", None),
            P("seq", "dp", None),
        ),
        check_vma=False,
    )
```

profile of v0, /device:TPU:2, one launch (start us, length us, event | category | flops | bytes accessed | tf_op | source)
XLA Modules:
  0.0 1694.9 jit_solution(26431627287732722)
XLA Ops:
  11.7 41.5 %all-reduce.12 = (bf16[768]{0:T(1024)(128)(2,1)S(1)}, bf16[768]{0:T(1024)(128)(2,1)S(1)}) all-reduce(bf16[768]{0:T(1024)(128)(2,1)S(1)} %dynamic-update-slice.1, bf16[768]{0:T(1024)(128)(2,1)S(1)} %dynamic-update-slice), channel_id=1, replica_groups=mesh['dp'=8,'seq'=4] {'dp','seq'}, use_global_device_ids=true, to_apply=%add.5 | all-reduce | flops 1536 | bytes 6144
  54.5 17.8 %all-gather.10.cloned.1.call-done = bf16[768,2304]{1,0:T(8,128)(2,1)} async-done(((bf16[24,2304]{1,0:T(8,128)(2,1)}), bf16[768,2304]{1,0:T(8,128)(2,1)}) %all-gather.10.cloned.1.call-update) | async-done | bytes 3538960 | tf_op jit(solution)/shard_map/all_gather | solution.py:65
  114.2 47.7 %psum.15 = f32[]{:T(128)} all-reduce(f32[]{:T(128)} %convert_reduce_fusion), channel_id=1, replica_groups=mesh['dp'=8,'seq'=4] {'dp','seq'}, use_global_device_ids=true, to_apply=%region_22.23 | all-reduce | flops 1 | bytes 8 | tf_op jit(solution)/shard_map/psum | solution.py:192
  162.6 36.4 %all-gather.2 = bf16[32,24,4]{1,2,0:T(4,128)(2,1)S(1)} all-gather(bf16[1,24,4]{1,2,0:T(4,128)(2,1)S(1)} %bitcast.264), channel_id=1, replica_groups=mesh['dp'=8,'seq'=4] {'dp','seq'}, dimensions={0}, use_global_device_ids=true | all-gather | bytes 6336 | tf_op jit(solution)/shard_map/all_gather | solution.py:70
  199.8 40.9 %all-gather.1 = bf16[32,24,12]{1,2,0:T(8,128)(2,1)S(1)} all-gather(bf16[1,24,12]{1,2,0:T(8,128)(2,1)S(1)} %bitcast.262), channel_id=1, replica_groups=mesh['dp'=8,'seq'=4] {'dp','seq'}, dimensions={0}, use_global_device_ids=true | all-gather | bytes 19008 | tf_op jit(solution)/shard_map/all_gather | solution.py:69
  241.5 36.6 %all-gather.3 = bf16[32,24,2]{1,2,0:T(2,128)(2,1)S(1)} all-gather(bf16[1,24,2]{1,2,0:T(2,128)(2,1)S(1)} %bitcast.265), channel_id=1, replica_groups=mesh['dp'=8,'seq'=4] {'dp','seq'}, dimensions={0}, use_global_device_ids=true | all-gather | bytes 3168 | tf_op jit(solution)/shard_map/all_gather | solution.py:71
  299.2 91.4 %while.28 = (s32[]{:T(128)}, bf16[4,512,3,64]{1,3,2,0:T(8,128)(2,1)S(1)}, f32[4,3,512]{2,1,0:T(4,128)}, s32[2048]{0:T(1024)S(1)}, s32[4]{0:T(128)S(1)}, /*index=...) while((s32[]{:T(128)}, ...), condition=%wide.region_4.5_spmd.clone, body=%wide.region_1.4_spmd.clone.sunk | while | flops 846298112 | bytes 43983552 | solution.py:135
  430.7 14.6 all-to-all-done.4
  448.3 11.6 fusion.99
  459.9 12.1 multiply_convert_fusion.3
  533.0 16.4 multiply_reduce_fusion.3
  567.1 18.6 %fusion.46 = (f32[512,2]{1,0:T(8,128)}, f32[512,2]{1,0:T(8,128)}, f32[2,768]{1,0:T(2,128)}, f32[512,768]{1,0:T(8,128)}, f32[512,2]{1,0:T(8,128)}, /*index=5*/f32[512,2]{1,0:T(8,128)}) fusion(f32[512,768]{1,0:T(8,128)S(1)} %copy-done.10, f32[512,768]{1,0:T(8,128)} %get-tuple-element.256, f32[512,2]{1,0:T(8,128)} %copy.165, f32[2,768]{1,0:T(2,128)S(1)} %bitcast.255, ...), kind=kLoop, calls=%fused_computation.72 | loop fusion | flops 12184064 | bytes 7905280 | tf_op jit(solution)/shard_map/reduce_sum | solution.py:258
  592.7 15.3 multiply_convert_fusion.1
  640.3 15.7 all-to-all-done.7
  706.2 177.1 %while.29 = (s32[]{:T(128)}, f32[2048,3,64]{0,2,1:T(8,128)}, f32[2048,3,64]{0,2,1:T(8,128)}, bf16[4,512,3,64]{1,3,2,0:T(8,128)(2,1)}, s32[4]{0:T(128)S(1)}, /*in...) while((s32[]{:T(128)}, f32[2048,3,64]{0,2,1:T(8,128)}, ...), condition=%wide.region_38.39_spmd.clone, body=%wide.region_36.38_spmd.clone.sunk | while | flops 2065759232 | bytes 200537168 | solution.py:318
  902.1 14.1 all_to_all.206
  916.2 14.1 all_to_all.207
  938.3 11.6 fusion.103
  962.5 10.7 fusion.102
  984.9 41.8 %all-reduce.11 = (f32[]{:T(128)}, f32[768]{0:T(1024)S(1)}, f32[768]{0:T(1024)S(1)}, f32[768,12]{0,1:T(8,128)S(1)}, f32[768,4]{0,1:T(4,128)S(1)}, /*index=5*/f32[2,768]{1,0:T(2,128)S(1)}) all-reduce(f32[]{:T(128)} %get-tuple-element.258, f32[768]{0:T(1024)S(1)} %get-tuple-element.190, ...), channel_id=1, replica_groups=mesh['dp'=8,'seq'=4] {'dp','seq'}, use_global_device_ids=true, to_apply=%region_20.21 | all-reduce | flops 15361 | bytes 122888 | tf_op jit(solution)/shard_map/psum | solution.py:192
  1033.5 21.3 %reduce-scatter.9.cloned.1.call-done = f32[24,2304]{1,0:T(8,128)} async-done(((f32[768,2304]{1,0:T(8,128)}), f32[24,2304]{1,0:T(8,128)}) %reduce-scatter.9.cloned.1.call-update) | async-done | bytes 221200 | tf_op jit(solution)/shard_map/reduce_scatter | solution.py:353
  1054.8 210.8 %reduce-scatter.17.cloned.1.call-done = f32[2,256,768]{2,1,0:T(8,128)} async-done(((f32[2,2048,768]{2,1,0:T(8,128)}), f32[2,256,768]{2,1,0:T(8,128)}) %reduce-scatter.17.cloned.1.call-update) | async-done | bytes 1572880 | tf_op jit(solution)/shard_map/reduce_scatter | solution.py:239
  1265.6 210.6 %reduce-scatter.13.cloned.1.call-done = f32[2,96,2048]{2,1,0:T(8,128)} async-done(((f32[2,768,2048]{2,1,0:T(8,128)}), f32[2,96,2048]{2,1,0:T(8,128)}) %reduce-scatter.13.cloned.1.call-update) | async-done | bytes 1572880 | tf_op jit(solution)/shard_map/reduce_scatter | solution.py:237
  1476.2 210.5 %reduce-scatter.15.cloned.1.call-done = f32[2,96,2048]{2,1,0:T(8,128)} async-done(((f32[2,768,2048]{2,1,0:T(8,128)}), f32[2,96,2048]{2,1,0:T(8,128)}) %reduce-scatter.15.cloned.1.call-update) | async-done | bytes 1572880 | tf_op jit(solution)/shard_map/reduce_scatter | solution.py:238
  (532 shorter events, 591.9 us)
Async XLA Ops:
  7.2 65.1 %all-gather.10.cloned.1.call-start = ((), (), s32[]{:S(2)}) async-start(), calls=%async_computation.17 | async-start | bytes 3649536 | tf_op jit(solution)/shard_map/all_gather | solution.py:65
  7.9 391.6 %all-gather.12.cloned.1.call-start = ((), (), s32[]{:S(2)}) async-start(), calls=%async_computation.18 | async-start | bytes 1216512 | tf_op jit(solution)/shard_map/all_gather | solution.py:66
  8.7 439.6 %all-gather.14.cloned.1.call-start = ((), (), s32[]{:S(2)}) async-start(), calls=%async_computation.19 | async-start | bytes 7077888 | tf_op jit(solution)/shard_map/all_gather | solution.py:76
  9.4 450.5 %all-gather.16.cloned.1.call-start = ((), (), s32[]{:S(2)}) async-start(), calls=%async_computation.20 | async-start | bytes 7077888 | tf_op jit(solution)/shard_map/all_gather | solution.py:77
  78.0 14.4 all-to-all-start
  82.2 389.8 %all-gather.18.cloned.1.call-start = ((), (), s32[]{:S(2)}) async-start(), calls=%async_computation.21 | async-start | bytes 7077888 | tf_op jit(solution)/shard_map/all_gather | solution.py:78
  92.4 192.6 %copy-start.89 = (s32[512]{0:T(512)S(1)}, s32[512]{0:T(512)}, u32[]{:S(2)}) copy-start(s32[512]{0:T(512)} %param.24) | copy-start | bytes 6148
  92.4 16.3 all-to-all-start.1
  108.8 189.2 %all-to-all-start.2 = ((bf16[512,4,192]{0,2,1:T(8,128)(2,1)}), bf16[512,4,192]{0,2,1:T(8,128)(2,1)S(1)}, u32[]{:S(2)}, u32[]{:S(2)}) async-start(bf16[512,4,192]{0,2,1:T(8,128)(2,1)} %bitcast.6), calls=%async_computation.2 | async-start | bytes 1572864 | tf_op jit(solution)/shard_map/all_to_all | solution.py:96
  162.6 517.7 %copy-start.45 = (f32[768]{0:T(1024)}, f32[768]{0:T(1024)S(1)}, u32[]{:S(2)}) copy-start(f32[768]{0:T(1024)S(1)} %convert_element_type.122) | copy-start | bytes 9220
  391.5 15.3 all-to-all-start.3
  409.6 270.7 %copy-start.48 = (f32[512]{0:T(512)}, f32[512]{0:T(512)S(1)}, u32[]{:S(2)}) copy-start(f32[512]{0:T(512)S(1)} %add_rsqrt_fusion) | copy-start | bytes 6148
  416.3 28.9 %all-to-all-start.4 = ((bf16[8,160,768]{2,1,0:T(8,128)(2,1)}), bf16[8,160,768]{2,1,0:T(8,128)(2,1)}, u32[]{:S(2)}, u32[]{:S(2)}) async-start(bf16[8,160,768]{2,1,0:T(8,128)(2,1)} %bitcast.228), calls=%async_computation.4 | async-start | bytes 3932160 | tf_op jit(solution)/shard_map/all_to_all | solution.py:176
  424.2 214.1 %copy-start.41 = (f32[512,12]{0,1:T(8,128)}, f32[512,12]{0,1:T(8,128)S(1)}, u32[]{:S(2)}) copy-start(f32[512,12]{0,1:T(8,128)S(1)} %fusion.81) | copy-start | bytes 73732
  483.9 33.5 %all-to-all-start.5 = ((bf16[2,640,768]{2,0,1:T(2,128)(2,1)}), bf16[2,640,768]{2,0,1:T(2,128)(2,1)}, u32[]{:S(2)}, u32[]{:S(2)}) async-start(bf16[2,640,768]{2,0,1:T(2,128)(2,1)} %copy.176), calls=%async_computation.5 | async-start | bytes 3932160 | tf_op jit(solution)/shard_map/all_to_all | solution.py:184
  562.1 27.7 %all-to-all-start.6 = ((bf16[8,160,768]{2,1,0:T(8,128)(2,1)}), bf16[8,160,768]{2,1,0:T(8,128)(2,1)}, u32[]{:S(2)}, u32[]{:S(2)}) async-start(bf16[8,160,768]{2,1,0:T(8,128)(2,1)} %multiply_convert_fusion.4), calls=%async_computation.6 | async-start | bytes 3932160 | tf_op jit(solution)/shard_map/all_to_all | solution.py:208
  626.9 29.1 %all-to-all-start.7 = ((bf16[2,640,768]{2,0,1:T(2,128)(2,1)}), bf16[2,640,768]{2,0,1:T(2,128)(2,1)}, u32[]{:S(2)}, u32[]{:S(2)}) async-start(bf16[2,640,768]{2,0,1:T(2,128)(2,1)} %copy.182), calls=%async_computation.7 | async-start | bytes 3932160 | tf_op jit(solution)/shard_map/all_to_all | solution.py:225
  686.1 15.9 all-to-all-start.8
  691.9 341.6 %reduce-scatter.11.cloned.1.call-start = ((), (), s32[]{:S(2)}) async-start(), calls=%async_computation.23 | async-start | bytes 2433024 | tf_op jit(solution)/shard_map/reduce_scatter | solution.py:354
  886.5 15.6 all-to-all-start.10
  892.0 162.8 %reduce-scatter.9.cloned.1.call-start = ((), (), s32[]{:S(2)}) async-start(), calls=%async_computation.22 | async-start | bytes 7299072 | tf_op jit(solution)/shard_map/reduce_scatter | solution.py:353
  936.8 328.8 %reduce-scatter.17.cloned.1.call-start = ((), (), s32[]{:S(2)}) async-start(), calls=%async_computation.26 | async-start | bytes 14155776 | tf_op jit(solution)/shard_map/reduce_scatter | solution.py:239
  950.0 526.3 %reduce-scatter.13.cloned.1.call-start = ((), (), s32[]{:S(2)}) async-start(), calls=%async_computation.24 | async-start | bytes 14155776 | tf_op jit(solution)/shard_map/reduce_scatter | solution.py:237
  962.2 724.5 %reduce-scatter.15.cloned.1.call-start = ((), (), s32[]{:S(2)}) async-start(), calls=%async_computation.25 | async-start | bytes 14155776 | tf_op jit(solution)/shard_map/reduce_scatter | solution.py:238
  (126 other events, 1620.2 us)
Sparse Core Ops, SparseCore 0:
  10.9 61.3 all-gather.9
  75.2 54.1 all-gather.11
  131.6 99.6 all-gather.13
  233.3 97.5 all-gather.15
  333.0 97.2 all-gather.17
  698.3 96.2 reduce-scatter.10
  936.9 117.8 reduce-scatter.8
  1059.0 206.5 reduce-scatter.16
  1269.8 206.4 reduce-scatter.12
  1480.2 206.4 reduce-scatter.14
where the time goes:
time: 1710 us; the launch traced here: 1690 us
  waiting for transfers between devices  744 us (44%)
  matrix products  302 us (18%)
  blocking collectives  279 us (16%)
  other arithmetic  148 us (9%)
  local copies, waits for them, and re-layouts  134 us (8%)
  starting transfers between devices  56.3 us (3%)
  between operations  18.8 us (1%)
    reduce_scatter x1, waiting for transfers between devices, body(): lax.psum_scatter(grad_down, 'dp', scatter_dimension=1, tiled=True)  211 us
    reduce_scatter x1, waiting for transfers between devices, body(): lax.psum_scatter(grad_gate_w, 'dp', scatter_dimension=1, tiled=True)  211 us
    reduce_scatter x1, waiting for transfers between devices, body(): lax.psum_scatter(grad_up_w, 'dp', scatter_dimension=1, tiled=True)  210 us
    psum x2, blocking collectives, body(): lax.psum((jnp.sum(valid_f), jnp.sum(valid_f[:, None] * differ * differ)),...  89.5 us
    dot_general x8, matrix products, block_scores(): jnp.einsum('qhd,khd->hqk', query_block, key_three, preferred_element_type...  49.5 us
    unnamed x1, blocking collectives  41.5 us
    all_gather x1, blocking collectives, dense_weights(): lax.all_gather(router, ('dp', 'seq'), axis=0, tiled=True)  40.9 us
    all_gather x1, blocking collectives, dense_weights(): lax.all_gather(const_vectors, ('dp', 'seq'), axis=1, tiled=True)  36.6 us
  transfers between devices with their start and end apart: 20, of which 13 were waited for; matrix products, arithmetic and copies ran while one was open for 26% of the time, Pallas kernels for 0%

commit v1 on v0

v1 whole, which is shorter than its diff:
```python
import jax
import jax.numpy as jnp
import numpy as np
from jax import lax
from jax.sharding import Mesh, PartitionSpec as P

HEAD = 64
EXPERTS = 8
ROUTES = 12
CAP = 160

ALL = ("do", "di", "seq")
PLANE = ("di", "seq")

exact = lax.Precision.HIGHEST
epsilon = 1e-06
masked_out = -1e30
bf16 = jnp.bfloat16
f32 = jnp.float32


def rms_scale(values):
    return lax.rsqrt(jnp.mean(values * values, -1, keepdims=True) + epsilon)


def dot_rows(left, right, precision=None):
    return lax.dot_general(
        left,
        right,
        (((0,), (0,)), ((), ())),
        preferred_element_type=jnp.float32,
        precision=precision,
    )


def dot_last(left, right, precision=None):
    return lax.dot_general(
        left,
        right,
        (((1,), (1,)), ((), ())),
        preferred_element_type=jnp.float32,
        precision=precision,
    )


def exchange(blocks, axes):
    return lax.all_to_all(blocks, axes, split_axis=0, concat_axis=0, tiled=True)


def to_all(block, count):
    return exchange(jnp.broadcast_to(block[None], (count,) + block.shape), ALL)


def gather_seq(block, size):
    held = block[None]
    step = size // 2
    while step:
        pairs = [(i, i ^ step) for i in range(size)]
        held = jnp.concatenate([held, lax.ppermute(held, "seq", pairs)], 0)
        step //= 2
    order = [0]
    step = size // 2
    while step:
        order = order + [k ^ step for k in order]
        step //= 2
    return held, order


def body(
    block_input,
    teacher,
    prev_logits,
    valid_mask,
    segments,
    routes,
    input_proj,
    output_proj,
    attention_gain,
    mixture_gain,
    router,
    const_mix,
    const_vectors,
    expert_gate,
    expert_up,
    expert_down,
):
    n_out, n_in, n_seq = (lax.axis_size(a) for a in ALL)
    n_all = n_out * n_in * n_seq
    tokens_here, features = block_input.shape
    rows_here = input_proj.shape[0]
    wide = features // n_seq
    seq_id = lax.axis_index("seq")

    def expert_weight(shard):
        mine = exchange(shard, "di")
        whole = lax.all_gather(mine, "do", axis=0, tiled=False)
        return whole.reshape(-1, shard.shape[2])

    gate_full = expert_weight(expert_gate)
    up_full = expert_weight(expert_up)
    down_full = expert_weight(expert_down)

    own_cols = (
        input_proj.reshape(rows_here, 3, n_seq, wide)
        .transpose(2, 0, 1, 3)
        .reshape(n_seq, rows_here, 3 * wide)
    )
    count_here = jnp.sum(valid_mask)
    count_cols = jnp.stack([count_here // 32, count_here % 32]).astype(bf16)
    small = jnp.concatenate(
        [
            attention_gain[:, None],
            mixture_gain[:, None],
            router,
            const_mix,
            const_vectors.T,
            jnp.broadcast_to(count_cols[None], (rows_here, 2)),
        ],
        1,
    )
    pad = -(3 * wide + small.shape[1]) % 128
    packed = jnp.concatenate(
        [
            own_cols,
            jnp.broadcast_to(small[None], (n_seq,) + small.shape),
            jnp.zeros((n_seq, rows_here, pad), bf16),
        ],
        2,
    )
    packed = jnp.broadcast_to(packed[None], (n_out * n_in,) + packed.shape).reshape(
        n_all, rows_here, -1
    )
    got = exchange(packed, ALL)
    counts = got[:, 0, 3 * wide + 20 : 3 * wide + 22].astype(f32)
    valid_count = jnp.sum(counts[:, 0]) * 32.0 + jnp.sum(counts[:, 1])
    got = got.reshape(features, -1)
    own_in = got[:, : 3 * wide]
    small_all = got[:, 3 * wide : 3 * wide + 20].astype(f32)
    gain_first = small_all[:, 0]
    gain_mid = small_all[:, 1]
    router_f = small_all[:, 2:14]
    mix_f = small_all[:, 14:18]
    vectors_f = small_all[:, 18:20].T
    full_out = to_all(output_proj, n_all).reshape(features, features)

    seg_row = jnp.pad(segments.astype(bf16), (0, features * 2 - tokens_here)).reshape(2, features)
    with_seg = jnp.concatenate(
        [block_input, jnp.pad(seg_row, ((0, 14), (0, 0)))], 0
    )
    held, order = gather_seq(with_seg, n_seq)
    where = [order.index(j) for j in range(n_seq)]
    chosen = jnp.array(where, jnp.int32)[jnp.arange(n_seq) ^ seq_id]
    held = held[chosen]
    seq_inputs = held[:, :tokens_here].reshape(-1, features).astype(f32)
    seq_segments = (
        held[:, tokens_here : tokens_here + 2]
        .reshape(n_seq, 2 * features)[:, :tokens_here]
        .reshape(-1)
    )

    inputs_f = block_input.astype(f32)
    scale_seq = rms_scale(seq_inputs)
    unit_seq = seq_inputs * scale_seq
    normed_first = (unit_seq * gain_first).astype(bf16)
    projected = jnp.dot(normed_first, own_in, preferred_element_type=f32).astype(bf16)
    length = n_seq * tokens_here
    heads_here = wide // HEAD
    query_three, key_three, value_three = (
        projected[:, k * wide : (k + 1) * wide].reshape(length, heads_here, HEAD) for k in range(3)
    )
    block_rows = min(512, length)
    block_count = length // block_rows
    scaling = HEAD ** (-0.5)
    key_positions = jnp.arange(length)

    def block_scores(block_id):
        first_row = block_id * block_rows
        query_block = lax.dynamic_slice_in_dim(query_three, first_row, block_rows, 0)
        segment_block = lax.dynamic_slice_in_dim(seq_segments, first_row, block_rows, 0)
        scores = (
            jnp.einsum("qhd,khd->hqk", query_block, key_three, preferred_element_type=jnp.float32)
            * scaling
        )
        allowed = (seq_segments[None, :] == segment_block[:, None]) & (
            key_positions[None, :] <= first_row + jnp.arange(block_rows)[:, None]
        )
        return (query_block, jnp.where(allowed[None], scores, masked_out))

    def forward_block(block_id):
        query_block, scores = block_scores(block_id)
        row_max = jnp.max(scores, -1, keepdims=True)
        expo = jnp.exp(scores - row_max)
        row_total = jnp.sum(expo, -1, keepdims=True)
        weights = (expo / row_total).astype(jnp.bfloat16)
        attended = jnp.einsum(
            "hqk,khd->qhd", weights, value_three, preferred_element_type=jnp.float32
        )
        return (attended.astype(jnp.bfloat16), (row_max + jnp.log(row_total))[..., 0])

    attended_blocks, log_totals = lax.map(forward_block, jnp.arange(block_count))
    attended_heads = attended_blocks.reshape(n_seq, tokens_here, wide)
    attended_tok = exchange(attended_heads, "seq").transpose(1, 0, 2).reshape(tokens_here, features)

    residual_mid = inputs_f + jnp.dot(attended_tok, full_out, preferred_element_type=jnp.float32)
    scale_second = rms_scale(residual_mid)
    unit_second = residual_mid * scale_second
    normed = unit_second * gain_mid
    route_probs = jax.nn.softmax(jnp.dot(normed, router_f, precision=exact) + prev_logits, -1)
    onehot = (routes[:, :, None] == jnp.arange(ROUTES, dtype=jnp.int32)[None, None, :]).astype(
        jnp.float32
    )
    picked = jnp.sum(onehot * route_probs[:, None, :], -1)
    picked_sum = jnp.sum(picked, -1, keepdims=True)
    gate_weights = picked / picked_sum
    weights_all = jnp.sum(gate_weights[:, :, None] * onehot, 1)
    mix_weights = jax.nn.softmax(
        jnp.dot(normed, mix_f, precision=exact).reshape(tokens_here, 2, 2), -1
    )
    const_out = mix_weights[..., 0:1] * normed[:, None, :] + mix_weights[..., 1:2] * vectors_f[None]
    copy_weight = weights_all[:, EXPERTS + 1 : EXPERTS + 2]
    const_weight = weights_all[:, EXPERTS + 2 : EXPERTS + 4]
    local_terms = copy_weight * normed + jnp.sum(const_weight[:, :, None] * const_out, 1)

    flat_routes = routes.reshape(-1)
    onehot_e = (flat_routes[:, None] == jnp.arange(EXPERTS, dtype=jnp.int32)[None, :]).astype(
        jnp.int32
    )
    slot_rank = jnp.sum((jnp.cumsum(onehot_e, 0) - onehot_e) * onehot_e, -1)
    host = (flat_routes % n_in) * n_seq + flat_routes // n_in
    slot_dest = jnp.where(flat_routes < EXPERTS, host * CAP + slot_rank, EXPERTS * CAP)
    slots = jnp.arange(EXPERTS * CAP, dtype=jnp.int32)
    place = (slot_dest.reshape(tokens_here, 2)[:, :, None] == slots).astype(bf16)

    def dispatch(rows_zero, rows_one):
        return (
            dot_rows(place[:, 0], rows_zero) + dot_rows(place[:, 1], rows_one)
        ).astype(bf16).reshape(EXPERTS, CAP, features)

    def collect(rows, route):
        return jnp.dot(place[:, route], rows, preferred_element_type=f32)

    normed_low = normed.astype(bf16)
    recv_rows = exchange(dispatch(normed_low, normed_low), PLANE).reshape(-1, features)
    gate_part = jnp.dot(recv_rows, gate_full, preferred_element_type=f32)
    up_part = jnp.dot(recv_rows, up_full, preferred_element_type=f32)
    hidden = (jax.nn.silu(gate_part) * up_part).astype(bf16)
    result_rows = jnp.dot(hidden, down_full, preferred_element_type=f32).astype(bf16)
    back_rows = exchange(result_rows.reshape(EXPERTS, CAP, features), PLANE).reshape(-1, features)
    expert_terms = jnp.stack([collect(back_rows, 0), collect(back_rows, 1)], 1)
    full_output = residual_mid + local_terms + jnp.sum(gate_weights[:, :, None] * expert_terms, 1)
    valid_f = valid_mask.astype(jnp.float32)
    differ = full_output - teacher.astype(jnp.float32)
    squared = jnp.sum(valid_f[:, None] * differ * differ)
    grad_full = valid_f[:, None] * differ * (tokens_here * n_all / valid_count)
    gated = (gate_weights[:, :, None] * grad_full[:, None, :]).astype(bf16)
    grad_recv = exchange(dispatch(gated[:, 0], gated[:, 1]), PLANE).reshape(-1, features)

    def expert_grad(partial):
        low = partial.astype(bf16)
        part = lax.psum_scatter(low, "do", scatter_dimension=0, tiled=True)
        part = part.reshape(n_in, -1, partial.shape[1])
        return exchange(part, "di").astype(f32)

    grad_expert_down = expert_grad(dot_rows(hidden, grad_recv))
    sigmoid_gate = jax.nn.sigmoid(gate_part)
    silu_gate = gate_part * sigmoid_gate
    grad_hidden = dot_last(grad_recv, down_full)
    grad_gate_part = (
        grad_hidden * up_part * sigmoid_gate * (1.0 + gate_part * (1.0 - sigmoid_gate))
    ).astype(bf16)
    grad_up_part = (grad_hidden * silu_gate).astype(bf16)
    grad_rows = (dot_last(grad_gate_part, gate_full) + dot_last(grad_up_part, up_full)).astype(bf16)
    grad_back = exchange(grad_rows.reshape(EXPERTS, CAP, features), PLANE).reshape(-1, features)
    grad_expert_gate = expert_grad(dot_rows(recv_rows, grad_gate_part))
    grad_expert_up = expert_grad(dot_rows(recv_rows, grad_up_part))

    expert_dot = jnp.sum(grad_full[:, None, :] * expert_terms, -1)
    copy_dot = jnp.sum(grad_full * normed, -1)
    const_dot = jnp.sum(grad_full[:, None, :] * const_out, -1)
    grad_gates = (
        expert_dot
        + onehot[:, :, EXPERTS + 1] * copy_dot[:, None]
        + jnp.sum(onehot[:, :, EXPERTS + 2 : EXPERTS + 4] * const_dot[:, None, :], -1)
    )
    grad_picked = (grad_gates - jnp.sum(gate_weights * grad_gates, -1, keepdims=True)) / picked_sum
    grad_probs = jnp.sum(grad_picked[:, :, None] * onehot, 1)
    grad_logits = route_probs * (grad_probs - jnp.sum(route_probs * grad_probs, -1, keepdims=True))
    grad_router = dot_rows(normed, grad_logits, exact)
    grad_const = const_weight[:, :, None] * grad_full[:, None, :]
    grad_mix = jnp.stack(
        [jnp.sum(grad_const * normed[:, None, :], -1), jnp.sum(grad_const * vectors_f[None], -1)],
        -1,
    )
    grad_z = (
        mix_weights * (grad_mix - jnp.sum(mix_weights * grad_mix, -1, keepdims=True))
    ).reshape(tokens_here, 4)
    grad_const_mix = dot_rows(normed, grad_z, exact)
    grad_const_vectors = jnp.sum(mix_weights[..., 1:2] * grad_const, 0)
    grad_normed = copy_weight * grad_full + dot_last(grad_logits, router_f, exact)
    grad_normed = (
        grad_normed
        + jnp.sum(mix_weights[..., 0:1] * grad_const, 1)
        + dot_last(grad_z, mix_f, exact)
    )
    grad_normed = grad_normed + collect(grad_back, 0) + collect(grad_back, 1)
    grad_mixture_gain = jnp.sum(grad_normed * unit_second, 0)
    grad_hat = grad_normed * gain_mid
    grad_mid = grad_full + scale_second * (
        grad_hat - unit_second * jnp.mean(grad_hat * unit_second, -1, keepdims=True)
    )
    grad_branch = grad_mid.astype(bf16)
    grad_output_proj = dot_rows(attended_tok, grad_branch).astype(bf16)
    grad_output_proj = exchange(grad_output_proj.reshape(n_all, rows_here, features), ALL)
    grad_output_proj = jnp.sum(grad_output_proj.astype(f32), 0)
    grad_attended = dot_last(grad_branch, full_out).astype(bf16)
    grad_attended = grad_attended.reshape(tokens_here, n_seq, wide).transpose(1, 0, 2)
    grad_three = exchange(grad_attended, "seq").reshape(length, heads_here, HEAD)

    def backward_block(carry, block_id):
        grad_key, grad_value = carry
        first_row = block_id * block_rows
        query_block, scores = block_scores(block_id)
        probs_block = jnp.exp(scores - log_totals[block_id][..., None])
        grad_block = lax.dynamic_slice_in_dim(grad_three, first_row, block_rows, 0)
        grad_value = grad_value + jnp.einsum(
            "hqk,qhd->khd",
            probs_block.astype(jnp.bfloat16),
            grad_block,
            preferred_element_type=jnp.float32,
        )
        grad_prob = jnp.einsum(
            "qhd,khd->hqk", grad_block, value_three, preferred_element_type=jnp.float32
        )
        inner = jnp.sum(probs_block * grad_prob, -1, keepdims=True)
        grad_scores = (probs_block * (grad_prob - inner)).astype(jnp.bfloat16)
        grad_query = (
            jnp.einsum("hqk,khd->qhd", grad_scores, key_three, preferred_element_type=jnp.float32)
            * scaling
        )
        grad_key = (
            grad_key
            + jnp.einsum(
                "hqk,qhd->khd", grad_scores, query_block, preferred_element_type=jnp.float32
            )
            * scaling
        )
        return ((grad_key, grad_value), grad_query.astype(jnp.bfloat16))

    zeros_heads = jnp.zeros((length, heads_here, HEAD), jnp.float32)
    (grad_key, grad_value), grad_queries = lax.scan(
        backward_block, (zeros_heads, zeros_heads), jnp.arange(block_count)
    )
    grad_projected = jnp.concatenate(
        [
            grad_queries.reshape(length, wide),
            grad_key.astype(bf16).reshape(length, wide),
            grad_value.astype(bf16).reshape(length, wide),
        ],
        1,
    )
    grad_input_proj = dot_rows(normed_first, grad_projected).astype(bf16)
    grad_input_proj = exchange(grad_input_proj.reshape(n_all, rows_here, 3 * wide), ALL)
    grad_input_proj = (
        jnp.sum(
            grad_input_proj.reshape(n_out * n_in, n_seq, rows_here, 3, wide).astype(f32), 0
        )
        .transpose(1, 2, 0, 3)
        .reshape(rows_here, 3 * features)
    )
    partial_first = dot_last(grad_projected, own_in)
    grad_attention_gain = jnp.sum(partial_first * unit_seq, 0)

    held = partial_first.reshape(n_seq, tokens_here, features)[
        jnp.arange(n_seq) ^ seq_id
    ]
    step = 1
    index = list(range(n_seq))
    while step < n_seq:
        pairs = [(i, i ^ step) for i in range(n_seq)]
        keep = [k for k, t in enumerate(index) if not t & step]
        give = [index.index(index[k] ^ step) for k in keep]
        sent = held[np.array(give)].astype(bf16)
        held = held[np.array(keep)] + lax.ppermute(sent, "seq", pairs).astype(f32)
        index = [index[k] for k in keep]
        step *= 2
    grad_normed_first = held[0]

    scale_first = rms_scale(inputs_f)
    unit_first = inputs_f * scale_first
    grad_hat_first = grad_normed_first * gain_first
    grad_input = grad_mid + scale_first * (
        grad_hat_first - unit_first * jnp.mean(grad_hat_first * unit_first, -1, keepdims=True)
    )
    small_grads = jnp.concatenate(
        [
            grad_attention_gain[:, None],
            grad_mixture_gain[:, None],
            grad_router,
            grad_const_mix,
            grad_const_vectors.T,
            jnp.broadcast_to(squared, (features, 1)),
        ],
        1,
    )
    small_grads = jnp.sum(exchange(small_grads.reshape(n_all, rows_here, 21), ALL), 0)
    mean_loss = small_grads[0, 20] / (2.0 * features * valid_count)
    return (
        full_output.astype(bf16),
        mean_loss,
        grad_input,
        grad_input_proj,
        grad_output_proj,
        small_grads[:, 0],
        small_grads[:, 1],
        small_grads[:, 2:14],
        small_grads[:, 14:18],
        small_grads[:, 18:20].T,
        grad_expert_gate,
        grad_expert_up,
        grad_expert_down,
    )


def solution(mesh):
    n_seq = mesh.shape["seq"]
    n_in = EXPERTS // n_seq
    cut = Mesh(mesh.devices.reshape(-1, n_in, n_seq), ALL)
    rows = P(ALL, None)
    line = P(ALL)
    cols = P(None, ALL)
    expert = P("seq", ("do", "di"), None)
    return jax.shard_map(
        body,
        mesh=cut,
        in_specs=(rows, rows, rows, line, line, rows, rows, rows, line, line, rows, rows, cols)
        + (expert,) * 3,
        out_specs=(rows, P(), rows, rows, rows, line, line, rows, rows, cols) + (expert,) * 3,
        check_vma=False,
    )
```

time: 1710 us -> 825 us (0.48)
  waiting for transfers between devices: 744 us -> 147 us
  blocking collectives: 279 us -> 43.3 us
  local copies, waits for them, and re-layouts: 134 us -> 90.6 us
  other arithmetic: 148 us -> 113 us
  starting transfers between devices: 56.3 us -> 74.7 us
    reduce_scatter x5 -> x3, waiting for transfers between devices: 653 us -> 0.02 us  [expert_grad(): part = lax.psum_scatter(low, 'do', scatter_dimension=0, tiled=True)]
    all_gather x4 -> x0, blocking collectives: 120 us -> none  [the longest x1 40.9 us: dense_weights(): lax.all_gather(router, ('dp', 'seq'), axis=0, tiled=True)]
    psum x2 -> x0, blocking collectives: 89.5 us -> none  [body(): lax.psum((jnp.sum(valid_f), jnp.sum(valid_f[:, None] * differ * differ)),...]
    all_to_all x10 -> x15, waiting for transfers between devices: 70 us -> 147 us  [exchange(): return lax.all_to_all(blocks, axes, split_axis=0, concat_axis=0, tiled=True)]
    dot_general x10 -> x8, matrix products: 100 us -> 46.3 us  [the longest x4 12.4 us: collect(): return jnp.dot(place[:, route], rows, preferred_element_type=f32)]
    unnamed x1 -> x0, blocking collectives: 41.5 us -> none
    dot_general x4 -> x7, matrix products: 14.7 us -> 44.7 us  [dot_last(): lax.dot_general(left, right, (((1,), (1,)), ((), ())), preferred_element_...]
    dot_general x4 -> x11, matrix products: 12 us -> 38.3 us  [dot_rows(): lax.dot_general(left, right, (((0,), (0,)), ((), ())), preferred_element_...]
  transfers between devices with their start and end apart: 20 -> 25, of which waited for: 13 -> 12; matrix products, arithmetic and copies ran while one was open for 26% -> 56% of each run, Pallas kernels for 0% -> 0%
where the time goes in v1:
time: 825 us; the launch traced here: 815 us
  matrix products  311 us (38%)
  waiting for transfers between devices  147 us (18%)
  other arithmetic  113 us (14%)
  local copies, waits for them, and re-layouts  90.6 us (11%)
  starting transfers between devices  74.7 us (9%)
  blocking collectives  43.3 us (5%)
  between operations  21.4 us (3%)
  loops' own time  13.8 us (2%)
    all_to_all x15, waiting for transfers between devices, exchange(): return lax.all_to_all(blocks, axes, split_axis=0, concat_axis=0, tiled=True)  147 us
    all_to_all x15, starting transfers between devices, exchange(): return lax.all_to_all(blocks, axes, split_axis=0, concat_axis=0, tiled=True)  72.9 us
    dot_general x8, matrix products, block_scores(): jnp.einsum('qhd,khd->hqk', query_block, key_three, preferred_element_type...  56.5 us
    dot_general x7, matrix products, dot_last(): lax.dot_general(left, right, (((1,), (1,)), ((), ())), preferred_element_...  44.7 us
    all_to_all x2, blocking collectives, exchange(): return lax.all_to_all(blocks, axes, split_axis=0, concat_axis=0, tiled=True)  43.3 us
    dot_general x11, matrix products, dot_rows(): lax.dot_general(left, right, (((0,), (0,)), ((), ())), preferred_element_...  38.3 us
    dot_general x4, matrix products, backward_block(): jnp.einsum('qhd,khd->hqk', grad_block, value_three, preferred_element_typ...  31.7 us
    reduce_sum x4, other arithmetic, forward_block(): row_total = jnp.sum(expo, -1, keepdims=True)  27.2 us
  transfers between devices with their start and end apart: 25, of which 12 were waited for; matrix products, arithmetic and copies ran while one was open for 56% of the time, Pallas kernels for 0%

profile of v1, /device:TPU:2, one launch (start us, length us, event | category | flops | bytes accessed | tf_op | source)
XLA Modules:
  0.0 815.3 jit_solution(15084060951556868153)
XLA Ops:
  7.2 15.6 %all_to_all.85 = bf16[2,96,2048]{2,1,0:T(8,128)(2,1)} all-to-all(bf16[2,96,2048]{2,1,0:T(8,128)(2,1)} %param.42), channel_id=1, replica_groups=mesh['do'=4,'di'=2,'seq'=4] {'di'}, dimensions={0} | all-to-all | bytes 1572864 | tf_op jit(solution)/shard_map/all_to_all | solution.py:47
  50.6 43.0 %all-to-all-done = bf16[32,24,640]{2,1,0:T(8,128)(2,1)S(1)} async-done(((bf16[32,24,640]{2,1,0:T(8,128)(2,1)}), bf16[32,24,640]{2,1,0:T(8,128)(2,1)S(1)}, u32[]{:S(2)}, u32[]{:S(2)}) %all-to-all-start) | async-done | bytes 983072 | tf_op jit(solution)/shard_map/all_to_all | solution.py:47
  120.5 96.7 %while.30 = (s32[]{:T(128)}, bf16[4,512,3,64]{1,3,2,0:T(8,128)(2,1)S(1)}, f32[4,3,512]{2,1,0:T(4,128)}, bf16[4,512]{1,0:T(4,128)(2,1)}, s32[4]{0:T(128)S(1)}, /*...) while((s32[]{:T(128)}, ...), condition=%wide.region_5.6_spmd.clone, body=%wide.region_2.5_spmd.clone.sunk | while | flops 848395264 | bytes 43984584 | solution.py:200
  223.6 8.0 all-to-all-done.1
  250.1 18.4 %all-to-all-done.3 = bf16[8,160,768]{2,1,0:T(8,128)(2,1)} async-done(((bf16[8,160,768]{2,1,0:T(8,128)(2,1)}), bf16[8,160,768]{2,1,0:T(8,128)(2,1)}, u32[]{:S(2)}, u32[]{:S(2)}) %all-to-all-start.3) | async-done | bytes 1966112 | tf_op jit(solution)/shard_map/all_to_all | solution.py:47
  268.5 10.7 %fusion.110 = f32[1280,2048]{1,0:T(8,128)} fusion(bf16[1280,768]{1,0:T(8,128)(2,1)} %bitcast.26, bf16[768,2048]{1,0:T(8,128)(2,1)} %bitcast.345), kind=kOutput, calls=%fused_computation.248 | convolution fusion | flops 4026531840 | bytes 15597568 | tf_op jit(solution)/shard_map/dot_general | solution.py:244
  279.2 12.1 %multiply_convert_fusion.3 = (bf16[1280,2048]{1,0:T(8,128)(2,1)}, f32[1280,2048]{1,0:T(8,128)}) fusion(f32[1280,2048]{1,0:T(8,128)} %fusion.110, bf16[1280,768]{1,0:T(8,128)(2,1)} %bitcast.26, bf16[768,2048]{1,0:T(8,128)(2,1)} %bitcast.347), kind=kOutput, calls=%fused_computation.58 | convolution fusion | flops 4042260480 | bytes 31326208 | tf_op jit(solution)/shard_map/dot_general | solution.py:245
  291.3 9.0 %convolution_convert_fusion.3 = bf16[1280,768]{1,0:T(8,128)(2,1)} fusion(bf16[1280,2048]{1,0:T(8,128)(2,1)} %get-tuple-element.304, bf16[2048,768]{1,0:T(8,128)(2,1)} %bitcast.349), kind=kOutput, calls=%fused_computation.78 | convolution fusion | flops 4027514880 | bytes 10354688 | tf_op jit(solution)/shard_map/dot_general | solution.py:247
  310.6 19.2 %all-to-all-done.7 = bf16[8,160,768]{2,1,0:T(8,128)(2,1)} async-done(((bf16[8,160,768]{2,1,0:T(8,128)(2,1)}), bf16[8,160,768]{2,1,0:T(8,128)(2,1)}, u32[]{:S(2)}, u32[]{:S(2)}) %all-to-all-start.7) | async-done | bytes 1966112 | tf_op jit(solution)/shard_map/all_to_all | solution.py:47
  346.9 27.7 %all_to_all.86 = bf16[8,160,768]{2,1,0:T(8,128)(2,1)S(1)} all-to-all(bf16[8,160,768]{2,1,0:T(8,128)(2,1)S(1)} %bitcast.315), channel_id=1, replica_groups=mesh['do'=4,'di'=2,'seq'=4] {'di','seq'}, dimensions={0} | all-to-all | bytes 3932160 | tf_op jit(solution)/shard_map/all_to_all | solution.py:47
  382.5 16.1 %multiply_convert_fusion.1 = (bf16[1280,2048]{1,0:T(8,128)(2,1)}, bf16[1280,2048]{1,0:T(8,128)(2,1)S(1)}) fusion(f32[1280,2048]{1,0:T(8,128)} %fusion.110, f32[1280,2048]{1,0:T(8,128)} %get-tuple-element.305, bf16[1280,768]{1,0:T(8,128)(2,1)} %bitcast.313, bf16[2048,768]{1,0:T(8,128)(2,1)} %bitcast.350), kind=kOutput, calls=%fused_computation.56 | convolution fusion | flops 4060610560 | bytes 36569088 | tf_op jit(solution)/shard_map/dot_general | solution.py:37
  408.1 7.4 fusion.111
  415.5 8.2 %add_convert_fusion = bf16[1280,768]{1,0:T(8,128)(2,1)} fusion(f32[1280,768]{1,0:T(8,128)S(1)} %fusion.111, bf16[1280,2048]{1,0:T(8,128)(2,1)} %get-tuple-element.287, bf16[768,2048]{1,0:T(8,128)(2,1)S(1)} %bitcast.348), kind=kOutput, calls=%fused_computation.72 | convolution fusion | flops 4028497920 | bytes 14286848 | tf_op jit(solution)/shard_map/dot_general | solution.py:37
  437.6 16.1 %all-to-all-done.9 = bf16[8,160,768]{2,1,0:T(8,128)(2,1)} async-done(((bf16[8,160,768]{2,1,0:T(8,128)(2,1)}), bf16[8,160,768]{2,1,0:T(8,128)(2,1)}, u32[]{:S(2)}, u32[]{:S(2)}) %all-to-all-start.9) | async-done | bytes 1966112 | tf_op jit(solution)/shard_map/all_to_all | solution.py:47
  472.7 9.1 %convolution_convert_fusion.1 = bf16[768,2048]{1,0:T(8,128)(2,1)} fusion(bf16[1280,768]{1,0:T(8,128)(2,1)} %bitcast.26, bf16[1280,2048]{1,0:T(8,128)(2,1)} %get-tuple-element.287), kind=kOutput, calls=%fused_computation.76 | convolution fusion | flops 4028104704 | bytes 10354688 | tf_op jit(solution)/shard_map/dot_general | solution.py:27
  485.7 185.4 %while.31 = (s32[]{:T(128)}, f32[2048,3,64]{0,2,1:T(8,128)}, f32[2048,3,64]{0,2,1:T(8,128)}, bf16[4,512,3,64]{1,3,2,0:T(8,128)(2,1)}, s32[4]{0:T(128)S(1)}, /*in...) while((s32[]{:T(128)}, f32[2048,3,64]{0,2,1:T(8,128)}, ...), condition=%wide.region_35.36_spmd.clone, body=%wide.region_33.35_spmd.clone.sunk | while | flops 2067856384 | bytes 191100960 | solution.py:350
  491.0 7.3 fusion.184
  500.9 7.9 multiply_reduce_fusion.14
  546.9 8.0 multiply_reduce_fusion.14
  593.4 7.9 multiply_reduce_fusion.14
  639.6 7.9 multiply_reduce_fusion.14
  716.8 10.9 %all-to-all-done.13 = bf16[32,24,768]{2,1,0:T(8,128)(2,1)S(1)} async-done(((bf16[32,24,768]{2,1,0:T(8,128)(2,1)}), bf16[32,24,768]{2,1,0:T(8,128)(2,1)S(1)}, u32[]{:S(2)}, u32[]{:S(2)}) %all-to-all-start.13) | async-done | bytes 1179680 | tf_op jit(solution)/shard_map/all_to_all | solution.py:47
  746.4 9.7 %all-to-all-done.12 = bf16[32,24,576]{2,1,0:T(8,128)(2,1)} async-done(((bf16[32,24,576]{2,1,0:T(8,128)(2,1)}), bf16[32,24,576]{2,1,0:T(8,128)(2,1)}, u32[]{:S(2)}, u32[]{:S(2)}) %all-to-all-start.12) | async-done | bytes 884768 | tf_op jit(solution)/shard_map/all_to_all | solution.py:47
  761.6 10.1 %all-to-all-done.16 = bf16[2,256,768]{2,1,0:T(8,128)(2,1)} async-done(((bf16[2,256,768]{2,1,0:T(8,128)(2,1)}), bf16[2,256,768]{2,1,0:T(8,128)(2,1)}, u32[]{:S(2)}, u32[]{:S(2)}) %all-to-all-start.16) | async-done | bytes 786464 | tf_op jit(solution)/shard_map/all_to_all | solution.py:47
  (508 shorter events, 489.8 us)
Async XLA Ops:
  7.2 261.3 %all-gather.7.cloned.1.call-start = ((), (), s32[]{:S(2)}) async-start(), calls=%async_computation.23 | async-start | bytes 3932160 | tf_op jit(solution)/shard_map/all_gather | solution.py:96
  23.0 20.5 %collective-permute-start = (bf16[1,528,768]{2,1,0:T(8,128)(2,1)S(1)}, bf16[1,528,768]{2,1,0:T(8,128)(2,1)S(1)}, u32[]{:S(2)}, u32[]{:S(2)}) collective-permute-start(bf16[1,528,768]{2,1,0:T(8,128)(2,1)S(1)} %fusion.66), channel_id=1, source_target_pairs={{0,2},{1,3},{2,0},{3,1},{4,6},{5,7},{6,4},{7,5},{8,10},{9,11},{10,... | collective-permute-start | bytes 2433032 | tf_op jit(solution)/shard_map/ppermute | solution.py:59
  23.4 13.8 %all-to-all-start.5 = ((bf16[2,96,2048]{2,1,0:T(8,128)(2,1)}), bf16[2,96,2048]{2,1,0:T(8,128)(2,1)S(1)}, u32[]{:S(2)}, u32[]{:S(2)}) async-start(bf16[2,96,2048]{2,1,0:T(8,128)(2,1)} %param.43), calls=%async_computation.5 | async-start | bytes 1572864 | tf_op jit(solution)/shard_map/all_to_all | solution.py:47
  38.4 55.2 %all-to-all-start = ((bf16[32,24,640]{2,1,0:T(8,128)(2,1)}), bf16[32,24,640]{2,1,0:T(8,128)(2,1)S(1)}, u32[]{:S(2)}, u32[]{:S(2)}) async-start(bf16[32,24,640]{2,1,0:T(8,128)(2,1)} %bitcast.306), calls=%async_computation | async-start | bytes 1966080 | tf_op jit(solution)/shard_map/all_to_all | solution.py:47
  43.5 235.7 %all-gather.9.cloned.1.call-start = ((), (), s32[]{:S(2)}) async-start(), calls=%async_computation.24 | async-start | bytes 3932160 | tf_op jit(solution)/shard_map/all_gather | solution.py:96
  44.9 54.8 %collective-permute-start.1 = (bf16[2,528,768]{2,1,0:T(8,128)(2,1)}, bf16[2,528,768]{2,1,0:T(8,128)(2,1)}, u32[]{:S(2)}, u32[]{:S(2)}) collective-permute-start(bf16[2,528,768]{2,1,0:T(8,128)(2,1)} %pad_maximum_fusion.3), channel_id=1, source_target_pairs={{0,1},{1,0},{2,3},{3,2},{4,5},{5,4},{6,7},{7,6},{8,9},{9,8},{10,11... | collective-permute-start | bytes 4866056 | tf_op jit(solution)/shard_map/ppermute | solution.py:59
  93.6 18.4 %all-to-all-start.6 = ((bf16[2,256,768]{2,1,0:T(8,128)(2,1)}), bf16[2,256,768]{2,1,0:T(8,128)(2,1)}, u32[]{:S(2)}, u32[]{:S(2)}) async-start(bf16[2,256,768]{2,1,0:T(8,128)(2,1)} %param.44), calls=%async_computation.6 | async-start | bytes 1572864 | tf_op jit(solution)/shard_map/all_to_all | solution.py:47
  113.1 104.1 %all-to-all-start.2 = ((bf16[32,24,768]{2,1,0:T(8,128)(2,1)}), bf16[32,24,768]{2,1,0:T(8,128)(2,1)}, u32[]{:S(2)}, u32[]{:S(2)}) async-start(bf16[32,24,768]{2,1,0:T(8,128)(2,1)} %broadcast_in_dim.77), calls=%async_computation.2 | async-start | bytes 2359296 | tf_op jit(solution)/shard_map/all_to_all | solution.py:47
  218.0 13.6 %all-to-all-start.1 = ((bf16[4,512,192]{1,2,0:T(8,128)(2,1)}), bf16[4,512,192]{1,2,0:T(8,128)(2,1)S(1)}, u32[]{:S(2)}, u32[]{:S(2)}) async-start(bf16[4,512,192]{1,2,0:T(8,128)(2,1)} %bitcast.309), calls=%async_computation.1 | async-start | bytes 1572864 | tf_op jit(solution)/shard_map/all_to_all | solution.py:47
  221.6 69.6 %all-gather.11.cloned.1.call-start = ((), (), s32[]{:S(2)}) async-start(), calls=%async_computation.25 | async-start | bytes 3932160 | tf_op jit(solution)/shard_map/all_gather | solution.py:96
  238.5 30.0 %all-to-all-start.3 = ((bf16[8,160,768]{2,1,0:T(8,128)(2,1)}), bf16[8,160,768]{2,1,0:T(8,128)(2,1)}, u32[]{:S(2)}, u32[]{:S(2)}) async-start(bf16[8,160,768]{2,1,0:T(8,128)(2,1)} %bitcast.314), calls=%async_computation.3 | async-start | bytes 3932160 | tf_op jit(solution)/shard_map/all_to_all | solution.py:47
  300.3 29.6 %all-to-all-start.7 = ((bf16[8,160,768]{2,1,0:T(8,128)(2,1)}), bf16[8,160,768]{2,1,0:T(8,128)(2,1)}, u32[]{:S(2)}, u32[]{:S(2)}) async-start(bf16[8,160,768]{2,1,0:T(8,128)(2,1)} %bitcast.30), calls=%async_computation.7 | async-start | bytes 3932160 | tf_op jit(solution)/shard_map/all_to_all | solution.py:47
  306.0 450.2 %reduce-scatter.8.cloned.1.call-start = ((), (), s32[]{:S(2)}) async-start(), calls=%async_computation.22 | async-start | bytes 3932160 | tf_op jit(solution)/shard_map/reduce_scatter | solution.py:260
  381.8 379.9 %reduce-scatter.4.cloned.1.call-start = ((), (), s32[]{:S(2)}) async-start(), calls=%async_computation.20 | async-start | bytes 3932160 | tf_op jit(solution)/shard_map/reduce_scatter | solution.py:260
  423.7 29.9 %all-to-all-start.9 = ((bf16[8,160,768]{2,1,0:T(8,128)(2,1)}), bf16[8,160,768]{2,1,0:T(8,128)(2,1)}, u32[]{:S(2)}, u32[]{:S(2)}) async-start(bf16[8,160,768]{2,1,0:T(8,128)(2,1)} %bitcast.311), calls=%async_computation.9 | async-start | bytes 3932160 | tf_op jit(solution)/shard_map/all_to_all | solution.py:47
  467.7 15.0 %all-to-all-start.10 = ((bf16[4,512,192]{1,2,0:T(8,128)(2,1)}), bf16[4,512,192]{1,2,0:T(8,128)(2,1)S(1)}, u32[]{:S(2)}, u32[]{:S(2)}) async-start(bf16[4,512,192]{1,2,0:T(8,128)(2,1)} %bitcast.47), calls=%async_computation.10 | async-start | bytes 1572864 | tf_op jit(solution)/shard_map/all_to_all | solution.py:47
  472.7 317.2 %reduce-scatter.6.cloned.1.call-start = ((), (), s32[]{:S(2)}) async-start(), calls=%async_computation.21 | async-start | bytes 3932160 | tf_op jit(solution)/shard_map/reduce_scatter | solution.py:260
  694.9 32.7 %all-to-all-start.13 = ((bf16[32,24,768]{2,1,0:T(8,128)(2,1)}), bf16[32,24,768]{2,1,0:T(8,128)(2,1)S(1)}, u32[]{:S(2)}, u32[]{:S(2)}) async-start(bf16[32,24,768]{2,1,0:T(8,128)(2,1)} %bitcast.57), calls=%async_computation.13 | async-start | bytes 2359296 | tf_op jit(solution)/shard_map/all_to_all | solution.py:47
  709.0 28.1 %collective-permute-start.2 = (bf16[2,512,768]{2,1,0:T(8,128)(2,1)S(1)}, bf16[2,512,768]{2,1,0:T(8,128)(2,1)}, u32[]{:S(2)}, u32[]{:S(2)}) collective-permute-start(bf16[2,512,768]{2,1,0:T(8,128)(2,1)S(1)} %gather_fusion.4), channel_id=1, source_target_pairs={{0,1},{1,0},{2,3},{3,2},{4,5},{5,4},{6,7},{7,6},{8,9},{9,8},{10,11... | collective-permute-start | bytes 4718600 | tf_op jit(solution)/shard_map/ppermute | solution.py:383
  727.7 28.5 %all-to-all-start.12 = ((bf16[32,24,576]{2,1,0:T(8,128)(2,1)}), bf16[32,24,576]{2,1,0:T(8,128)(2,1)}, u32[]{:S(2)}, u32[]{:S(2)}) async-start(bf16[32,24,576]{2,1,0:T(8,128)(2,1)} %bitcast.54), calls=%async_computation.12 | async-start | bytes 1966080 | tf_op jit(solution)/shard_map/all_to_all | solution.py:47
  740.7 47.3 %collective-permute-start.3 = (bf16[1,512,768]{2,1,0:T(8,128)(2,1)}, bf16[1,512,768]{2,1,0:T(8,128)(2,1)}, u32[]{:S(2)}, u32[]{:S(2)}) collective-permute-start(bf16[1,512,768]{2,1,0:T(8,128)(2,1)} %slice.265), channel_id=1, source_target_pairs={{0,2},{1,3},{2,0},{3,1},{4,6},{5,7},{6,4},{7,5},{8,10},{9,11},{10,... | collective-permute-start | bytes 2359304 | tf_op jit(solution)/shard_map/ppermute | solution.py:383
  756.2 15.6 %all-to-all-start.16 = ((bf16[2,256,768]{2,1,0:T(8,128)(2,1)}), bf16[2,256,768]{2,1,0:T(8,128)(2,1)}, u32[]{:S(2)}, u32[]{:S(2)}) async-start(bf16[2,256,768]{2,1,0:T(8,128)(2,1)} %bitcast.318), calls=%async_computation.19 | async-start | bytes 1572864 | tf_op jit(solution)/shard_map/all_to_all | solution.py:47
  771.8 18.2 %all-to-all-start.14 = ((bf16[2,96,2048]{2,1,0:T(8,128)(2,1)}), bf16[2,96,2048]{2,1,0:T(8,128)(2,1)}, u32[]{:S(2)}, u32[]{:S(2)}) async-start(bf16[2,96,2048]{2,1,0:T(8,128)(2,1)} %bitcast.319), calls=%async_computation.15 | async-start | bytes 1572864 | tf_op jit(solution)/shard_map/all_to_all | solution.py:47
  790.0 14.7 %all-to-all-start.15 = ((bf16[2,96,2048]{2,1,0:T(8,128)(2,1)}), bf16[2,96,2048]{2,1,0:T(8,128)(2,1)}, u32[]{:S(2)}, u32[]{:S(2)}) async-start(bf16[2,96,2048]{2,1,0:T(8,128)(2,1)} %bitcast.320), calls=%async_computation.17 | async-start | bytes 1572864 | tf_op jit(solution)/shard_map/all_to_all | solution.py:47
  (102 other events, 867.8 us)
Sparse Core Ops, SparseCore 0:
  23.0 84.4 all-gather.6
  109.7 86.8 all-gather.8
  224.0 64.6 all-gather.10
  381.9 60.4 reduce-scatter.7
  444.6 60.2 reduce-scatter.3
  507.1 60.2 reduce-scatter.5

commit v2 on v1

--- a/solution.py
+++ b/solution.py
@@ -2,12 +2,15 @@
 import jax.numpy as jnp
 import numpy as np
 from jax import lax
+from jax.experimental import pallas as pl
+from jax.experimental.pallas import tpu as pltpu
 from jax.sharding import Mesh, PartitionSpec as P
 
 HEAD = 64
 EXPERTS = 8
 ROUTES = 12
 CAP = 160
+BLK = 256
 
 ALL = ("do", "di", "seq")
 PLANE = ("di", "seq")
@@ -41,6 +44,146 @@
         preferred_element_type=jnp.float32,
         precision=precision,
     )
+
+
+def nt(a,b): return lax.dot_general(a,b,(((1,),(1,)),((),())),preferred_element_type=f32)
+def nn(a,b): return jnp.dot(a,b,preferred_element_type=f32)
+def tn(a,b): return lax.dot_general(a,b,(((0,),(0,)),((),())),preferred_element_type=f32)
+
+def fwd_kernel(tbl, held, gain, win, winT, start, normed, att, oT, lse, qn, kn, vn, qT, kT, kbuf, vbuf):
+    i=pl.program_id(0)
+    wide=win.shape[1]//3
+    heads=wide//HEAD
+    per=held.shape[1]//BLK
+    t=tbl[i//per]
+    off=pl.multiple_of((i%per)*BLK,BLK)
+    x=held[t,pl.ds(off,BLK),:].astype(f32)
+    scale=lax.rsqrt(jnp.mean(x*x,-1,keepdims=True)+epsilon)
+    nb=(x*scale*gain[...]).astype(bf16)
+    normed[...]=nb
+    proj=nn(nb,win[...]).astype(bf16)
+    projT=nt(winT[...],nb).astype(bf16)
+    qs=projT[:wide]*bf16(HEAD ** -0.5)
+    qT[...]=qs
+    kT[...]=projT[wide:2*wide]
+    vbuf[i]=projT[2*wide:]
+    for h in range(heads):
+        qn[h]=proj[:,h*HEAD:(h+1)*HEAD]*bf16(HEAD ** -0.5)
+        kh=proj[:,wide+h*HEAD:wide+(h+1)*HEAD]
+        kn[h]=kh
+        kbuf[i,h]=kh
+        vn[h]=proj[:,2*wide+h*HEAD:2*wide+(h+1)*HEAD]
+    rows=lax.broadcasted_iota(jnp.int32,(BLK,BLK),0)
+    cols=lax.broadcasted_iota(jnp.int32,(BLK,BLK),1)
+    first=start[...]
+    def tile(j,h,mask):
+        s=nn(kbuf[j,h],qs[h*HEAD:(h+1)*HEAD])
+        return jnp.where(mask,s,masked_out)
+    mask=(rows+i*BLK>=first)&(rows<=cols)
+    state=[]
+    for h in range(heads):
+        s=tile(i,h,mask)
+        m=jnp.max(s,0,keepdims=True)
+        e=jnp.exp(s-m)
+        l=jnp.sum(e,0,keepdims=True)
+        o=nn(vbuf[i,h*HEAD:(h+1)*HEAD],e.astype(bf16))
+        state.append((m,l,o))
+    def step(j,state):
+        mask=rows+j*BLK>=first
+        new=[]
+        for h in range(heads):
+            m,l,o=state[h]
+            s=tile(j,h,mask)
+            n=jnp.maximum(m,jnp.max(s,0,keepdims=True))
+            a=jnp.exp(m-n)
+            e=jnp.exp(s-n)
+            l=l*a+jnp.sum(e,0,keepdims=True)
+            o=o*a+nn(vbuf[j,h*HEAD:(h+1)*HEAD],e.astype(bf16))
+            new.append((n,l,o))
+        return tuple(new)
+    state=lax.fori_loop(0,i,step,tuple(state))
+    for h in range(heads):
+        m,l,o=state[h]
+        o=o/l
+        oT[h*HEAD:(h+1)*HEAD]=o
+        lse[h:h+1]=m+jnp.log(l)
+    lse[heads:]=jnp.zeros((lse.shape[0]-heads,BLK),f32)
+    att[...]=oT[...].T.astype(bf16)
+
+def attend_forward(tbl, held, gain, win, winT, start):
+    feat=held.shape[2]
+    length=start.shape[1]; wide=win.shape[1]//3; heads=wide//HEAD; nb=length//BLK
+    full=lambda shape: pl.BlockSpec(shape,lambda i,*_:(0,)*len(shape))
+    tokb=pl.BlockSpec((wide,BLK),lambda i,*_:(0,i))
+    headb=pl.BlockSpec((heads,BLK,HEAD),lambda i,*_:(0,i,0))
+    S=jax.ShapeDtypeStruct
+    return pl.pallas_call(fwd_kernel,
+      grid_spec=pltpu.PrefetchScalarGridSpec(num_scalar_prefetch=1,grid=(nb,),
+        in_specs=[full(held.shape),full(gain.shape),full(win.shape),full(winT.shape),pl.BlockSpec((1,BLK),lambda i,*_:(0,i))],
+        out_specs=[pl.BlockSpec((BLK,feat),lambda i,*_:(i,0)),pl.BlockSpec((BLK,wide),lambda i,*_:(i,0)),tokb,pl.BlockSpec((8,BLK),lambda i,*_:(0,i)),headb,headb,headb,tokb,tokb],
+        scratch_shapes=[pltpu.VMEM((nb,heads,BLK,HEAD),bf16),pltpu.VMEM((nb,wide,BLK),bf16)]),
+      out_shape=[S((length,feat),bf16),S((length,wide),bf16),S((wide,length),f32),S((8,length),f32),S((heads,length,HEAD),bf16),S((heads,length,HEAD),bf16),S((heads,length,HEAD),bf16),S((wide,length),bf16),S((wide,length),bf16)],
+      compiler_params=pltpu.CompilerParams(vmem_limit_bytes=48<<20),
+      name="attend_forward")(tbl,held,gain,win,winT,start)
+
+def bwd_kernel(go, oT, lse, qn, kn, vn, qT, kT, start, gq, gk, gv, gT, dq, delta):
+    j=pl.program_id(0)
+    nb=pl.num_programs(0)
+    heads=kn.shape[0]
+    rows=lax.broadcasted_iota(jnp.int32,(BLK,BLK),0)
+    cols=lax.broadcasted_iota(jnp.int32,(BLK,BLK),1)
+    @pl.when(j==0)
+    def _():
+        dq[...]=jnp.zeros_like(dq)
+        for b in range(gT.shape[0]):
+            g=go[b*BLK:(b+1)*BLK,:].astype(f32).T
+            gT[b]=g.astype(bf16)
+            prod=g*oT[:,b*BLK:(b+1)*BLK]
+            for h in range(heads):
+                delta[b,h:h+1]=jnp.sum(prod[h*HEAD:(h+1)*HEAD],0,keepdims=True)
+    def tile(i,accs,mask):
+        new=[]
+        at=pl.multiple_of(i*BLK,BLK)
+        ds_=pl.ds(at,BLK)
+        if mask is None:
+            mask=rows+j*BLK>=start[:,ds_]
+        else:
+            mask=mask&(rows+j*BLK>=start[:,ds_])
+        gblk=go[ds_,:]
+        for h in range(heads):
+            dk,dv=accs[h]
+            hs=slice(h*HEAD,(h+1)*HEAD)
+            s=nn(kn[h],qT[hs,ds_])
+            p=jnp.exp(jnp.where(mask,s,masked_out)-lse[h:h+1,ds_])
+            g=gblk[:,hs]
+            dv=dv+nn(p.astype(bf16),g)
+            dp=nn(vn[h],gT[i,hs])
+            d=(p*(dp-delta[i,h:h+1])).astype(bf16)
+            dk=dk+nn(d,qn[h,ds_])
+            dq[i,hs]+=nn(kT[hs],d)
+            new.append((dk,dv))
+        return tuple(new)
+    zero=jnp.zeros((BLK,HEAD),f32)
+    accs=tile(j,tuple((zero,zero) for _ in range(heads)),rows<=cols)
+    accs=lax.fori_loop(j+1,nb,lambda i,a:tile(i,a,None),accs)
+    gk[...]=jnp.concatenate([a[0] for a in accs],1).astype(bf16)
+    gv[...]=jnp.concatenate([a[1] for a in accs],1).astype(bf16)
+    gq[...]=(dq[j]*HEAD ** -0.5).T.astype(bf16)
+
+def attend_backward(go,oT,lse,qn,kn,vn,qT,kT,start):
+    length,wide=go.shape; heads=wide//HEAD; nb=length//BLK
+    full=lambda a: pl.BlockSpec(a.shape,lambda i,*_:(0,)*a.ndim)
+    headb=pl.BlockSpec((heads,BLK,HEAD),lambda i,*_:(0,i,0))
+    tokb=pl.BlockSpec((wide,BLK),lambda i,*_:(0,i))
+    rowb=pl.BlockSpec((BLK,wide),lambda i,*_:(i,0))
+    S=jax.ShapeDtypeStruct
+    return pl.pallas_call(bwd_kernel,grid=(nb,),
+      in_specs=[full(go),full(oT),full(lse),full(qn),headb,headb,full(qT),tokb,full(start)],
+      out_specs=[rowb]*3,
+      out_shape=[S((length,wide),bf16)]*3,
+      scratch_shapes=[pltpu.VMEM((nb,wide,BLK),bf16),pltpu.VMEM((nb,wide,BLK),f32),pltpu.VMEM((nb,8,BLK),f32)],
+      compiler_params=pltpu.CompilerParams(vmem_limit_bytes=48<<20),
+      name="attend_backward")(go,oT,lse,qn,kn,vn,qT,kT,start)
 
 
 def exchange(blocks, axes):
@@ -150,55 +293,21 @@
     held, order = gather_seq(with_seg, n_seq)
     where = [order.index(j) for j in range(n_seq)]
     chosen = jnp.array(where, jnp.int32)[jnp.arange(n_seq) ^ seq_id]
-    held = held[chosen]
-    seq_inputs = held[:, :tokens_here].reshape(-1, features).astype(f32)
+    length = n_seq * tokens_here
     seq_segments = (
         held[:, tokens_here : tokens_here + 2]
-        .reshape(n_seq, 2 * features)[:, :tokens_here]
-        .reshape(-1)
-    )
+        .reshape(n_seq, 2 * features)[:, :tokens_here][chosen]
+        .reshape(1, -1)
+    )
+    positions = jnp.arange(length, dtype=jnp.int32)[None]
+    fresh = seq_segments != jnp.pad(seq_segments[:, :-1], ((0, 0), (1, 0)), constant_values=-1)
+    start = lax.cummax(jnp.where(fresh, positions, 0), axis=1)
 
     inputs_f = block_input.astype(f32)
-    scale_seq = rms_scale(seq_inputs)
-    unit_seq = seq_inputs * scale_seq
-    normed_first = (unit_seq * gain_first).astype(bf16)
-    projected = jnp.dot(normed_first, own_in, preferred_element_type=f32).astype(bf16)
-    length = n_seq * tokens_here
-    heads_here = wide // HEAD
-    query_three, key_three, value_three = (
-        projected[:, k * wide : (k + 1) * wide].reshape(length, heads_here, HEAD) for k in range(3)
-    )
-    block_rows = min(512, length)
-    block_count = length // block_rows
-    scaling = HEAD ** (-0.5)
-    key_positions = jnp.arange(length)
-
-    def block_scores(block_id):
-        first_row = block_id * block_rows
-        query_block = lax.dynamic_slice_in_dim(query_three, first_row, block_rows, 0)
-        segment_block = lax.dynamic_slice_in_dim(seq_segments, first_row, block_rows, 0)
-        scores = (
-            jnp.einsum("qhd,khd->hqk", query_block, key_three, preferred_element_type=jnp.float32)
-            * scaling
-        )
-        allowed = (seq_segments[None, :] == segment_block[:, None]) & (
-            key_positions[None, :] <= first_row + jnp.arange(block_rows)[:, None]
-        )
-        return (query_block, jnp.where(allowed[None], scores, masked_out))
-
-    def forward_block(block_id):
-        query_block, scores = block_scores(block_id)
-        row_max = jnp.max(scores, -1, keepdims=True)
-        expo = jnp.exp(scores - row_max)
-        row_total = jnp.sum(expo, -1, keepdims=True)
-        weights = (expo / row_total).astype(jnp.bfloat16)
-        attended = jnp.einsum(
-            "hqk,khd->qhd", weights, value_three, preferred_element_type=jnp.float32
-        )
-        return (attended.astype(jnp.bfloat16), (row_max + jnp.log(row_total))[..., 0])
-
-    attended_blocks, log_totals = lax.map(forward_block, jnp.arange(block_count))
-    attended_heads = attended_blocks.reshape(n_seq, tokens_here, wide)
+    normed_first, attended, attended_t, log_totals, *heads_saved = attend_forward(
+        chosen, held, gain_first[None], own_in, own_in.T, start
+    )
+    attended_heads = attended.reshape(n_seq, tokens_here, wide)
     attended_tok = exchange(attended_heads, "seq").transpose(1, 0, 2).reshape(tokens_here, features)
 
     residual_mid = inputs_f + jnp.dot(attended_tok, full_out, preferred_element_type=jnp.float32)
@@ -314,49 +423,10 @@
     grad_output_proj = jnp.sum(grad_output_proj.astype(f32), 0)
     grad_attended = dot_last(grad_branch, full_out).astype(bf16)
     grad_attended = grad_attended.reshape(tokens_here, n_seq, wide).transpose(1, 0, 2)
-    grad_three = exchange(grad_attended, "seq").reshape(length, heads_here, HEAD)
-
-    def backward_block(carry, block_id):
-        grad_key, grad_value = carry
-        first_row = block_id * block_rows
-        query_block, scores = block_scores(block_id)
-        probs_block = jnp.exp(scores - log_totals[block_id][..., None])
-        grad_block = lax.dynamic_slice_in_dim(grad_three, first_row, block_rows, 0)
-        grad_value = grad_value + jnp.einsum(
-            "hqk,qhd->khd",
-            probs_block.astype(jnp.bfloat16),
-            grad_block,
-            preferred_element_type=jnp.float32,
-        )
-        grad_prob = jnp.einsum(
-            "qhd,khd->hqk", grad_block, value_three, preferred_element_type=jnp.float32
-        )
-        inner = jnp.sum(probs_block * grad_prob, -1, keepdims=True)
-        grad_scores = (probs_block * (grad_prob - inner)).astype(jnp.bfloat16)
-        grad_query = (
-            jnp.einsum("hqk,khd->qhd", grad_scores, key_three, preferred_element_type=jnp.float32)
-            * scaling
-        )
-        grad_key = (
-            grad_key
-            + jnp.einsum(
-                "hqk,qhd->khd", grad_scores, query_block, preferred_element_type=jnp.float32
-            )
-            * scaling
-        )
-        return ((grad_key, grad_value), grad_query.astype(jnp.bfloat16))
-
-    zeros_heads = jnp.zeros((length, heads_here, HEAD), jnp.float32)
-    (grad_key, grad_value), grad_queries = lax.scan(
-        backward_block, (zeros_heads, zeros_heads), jnp.arange(block_count)
-    )
+    grad_heads = exchange(grad_attended, "seq").reshape(length, wide)
+
     grad_projected = jnp.concatenate(
-        [
-            grad_queries.reshape(length, wide),
-            grad_key.astype(bf16).reshape(length, wide),
-            grad_value.astype(bf16).reshape(length, wide),
-        ],
-        1,
+        attend_backward(grad_heads, attended_t, log_totals, *heads_saved, start), 1
     )
     grad_input_proj = dot_rows(normed_first, grad_projected).astype(bf16)
     grad_input_proj = exchange(grad_input_proj.reshape(n_all, rows_here, 3 * wide), ALL)
@@ -368,6 +438,8 @@
         .reshape(rows_here, 3 * features)
     )
     partial_first = dot_last(grad_projected, own_in)
+    seq_inputs = held[chosen, :tokens_here].reshape(-1, features).astype(f32)
+    unit_seq = seq_inputs * rms_scale(seq_inputs)
     grad_attention_gain = jnp.sum(partial_first * unit_seq, 0)
 
     held = partial_first.reshape(n_seq, tokens_here, features)[

time: 825 us -> 679 us (0.82)
  matrix products: 311 us -> 137 us
  Pallas kernels: 0 us -> 85 us
  other arithmetic: 113 us -> 47.4 us
  waiting for transfers between devices: 147 us -> 167 us
  local copies, waits for them, and re-layouts: 90.6 us -> 109 us
  blocking collectives: 43.3 us -> 29.2 us
  loops' own time: 13.8 us -> 0.22 us
    dot_general x29 -> x0, matrix products: 178 us -> none  [the longest x8 56.5 us: block_scores(): jnp.einsum('qhd,khd->hqk', query_block, key_three, preferred_element_type...]
    pallas_call x0 -> x2, Pallas kernels: none -> 85 us  [the longest x1 43.8 us: attend_forward(): pl.pallas_call(fwd_kernel, grid_spec=pltpu.PrefetchScalarGridSpec(num_sca...]
    gather x1 -> x38, local copies, waits for them, and re-layouts: 2.67 us -> 47.7 us  [body(): held = held[chosen]]
    reduce_sum x4 -> x0, other arithmetic: 27.2 us -> none  [forward_block(): row_total = jnp.sum(expo, -1, keepdims=True)]
    ppermute x2, waiting for transfers between devices: 0.01 us -> 26.6 us  [gather_seq(): held = jnp.concatenate([held, lax.ppermute(held, 'seq', pairs)], 0)]
    convert_element_type x7 -> x1, other arithmetic: 25.9 us -> 3.23 us  [body(): seq_inputs = held[chosen, :tokens_here].reshape(-1, features).astype(f32)]
    all_to_all x15, waiting for transfers between devices: 147 us -> 127 us  [exchange(): return lax.all_to_all(blocks, axes, split_axis=0, concat_axis=0, tiled=True)]
    while x73 -> x0, local copies, waits for them, and re-layouts: 15.7 us -> none
  transfers between devices with their start and end apart: 25 -> 25, of which waited for: 12 -> 15; matrix products, arithmetic and copies ran while one was open for 56% -> 36% of each run, Pallas kernels for 0% -> 13%
where the time goes in v2:
time: 679 us; the launch traced here: 668 us
  waiting for transfers between devices  167 us (25%)
  matrix products  137 us (20%)
  local copies, waits for them, and re-layouts  109 us (16%)
  Pallas kernels  85 us (13%)
  starting transfers between devices  71.8 us (11%)
  other arithmetic  47.4 us (7%)
  blocking collectives  29.2 us (4%)
  between operations  21.3 us (3%)
    all_to_all x15, waiting for transfers between devices, exchange(): return lax.all_to_all(blocks, axes, split_axis=0, concat_axis=0, tiled=True)  127 us
    all_to_all x15, starting transfers between devices, exchange(): return lax.all_to_all(blocks, axes, split_axis=0, concat_axis=0, tiled=True)  70.8 us
    dot_general x7, matrix products, dot_last(): lax.dot_general(left, right, (((1,), (1,)), ((), ())), preferred_element_...  45.1 us
    pallas_call x1, Pallas kernels, attend_forward(): pl.pallas_call(fwd_kernel, grid_spec=pltpu.PrefetchScalarGridSpec(num_sca...  43.8 us
    gather x36, local copies, waits for them, and re-layouts  43.4 us
    dot_general x11, matrix products, dot_rows(): lax.dot_general(left, right, (((0,), (0,)), ((), ())), preferred_element_...  43 us
    pallas_call x1, Pallas kernels, attend_backward(): pl.pallas_call(bwd_kernel, grid=(nb,), in_specs=[full(go), full(oT), full...  41.2 us
    all_to_all x2, blocking collectives, exchange(): return lax.all_to_all(blocks, axes, split_axis=0, concat_axis=0, tiled=True)  29.2 us
  transfers between devices with their start and end apart: 25, of which 15 were waited for; matrix products, arithmetic and copies ran while one was open for 36% of the time, Pallas kernels for 13%

profile of v2, /device:TPU:2, one launch (start us, length us, event | category | flops | bytes accessed | tf_op | source)
XLA Modules:
  0.0 667.9 jit_solution(7880490720282152926)
XLA Ops:
  7.2 15.6 %all_to_all.85 = bf16[2,96,2048]{2,1,0:T(8,128)(2,1)} all-to-all(bf16[2,96,2048]{2,1,0:T(8,128)(2,1)} %param.38), channel_id=1, replica_groups=mesh['do'=4,'di'=2,'seq'=4] {'di'}, dimensions={0} | all-to-all | bytes 1572864 | tf_op jit(solution)/shard_map/all_to_all | solution.py:190
  22.9 13.5 %all_to_all.86 = bf16[2,96,2048]{2,1,0:T(8,128)(2,1)} all-to-all(bf16[2,96,2048]{2,1,0:T(8,128)(2,1)S(1)} %copy-done.42), channel_id=1, replica_groups=mesh['do'=4,'di'=2,'seq'=4] {'di'}, dimensions={0} | all-to-all | bytes 1572864 | tf_op jit(solution)/shard_map/all_to_all | solution.py:190
  56.9 26.5 %collective-permute-done = bf16[1,528,768]{2,1,0:T(8,128)(2,1)S(1)} collective-permute-done((bf16[1,528,768]{2,1,0:T(8,128)(2,1)S(1)}, bf16[1,528,768]{2,1,0:T(8,128)(2,1)S(1)}, u32[]{:S(2)}, u32[]{:S(2)}) %collective-permute-start) | collective-permute-done | bytes 811040 | tf_op jit(solution)/shard_map/ppermute | solution.py:202
  88.7 15.1 %all-to-all-done = bf16[32,24,640]{2,1,0:T(8,128)(2,1)S(1)} async-done(((bf16[32,24,640]{2,1,0:T(8,128)(2,1)}), bf16[32,24,640]{2,1,0:T(8,128)(2,1)S(1)}, u32[]{:S(2)}, u32[]{:S(2)}) %all-to-all-start) | async-done | bytes 983072 | tf_op jit(solution)/shard_map/all_to_all | solution.py:190
  117.3 43.8 %attend_forward.1 = (bf16[2048,768]{1,0:T(8,128)(2,1)}, bf16[2048,192]{1,0:T(8,128)(2,1)S(1)}, f32[192,2048]{1,0:T(8,128)S(1)}, f32[8,2048]{1,0:T(8,128)S(1)}, b...) custom-call(s32[4]{0:T(128)S(1)} %gather_fusion, ...), custom_call_target="tpu_custom_call" | custom-call | tf_op jit(solution)/shard_map/attend_forward/pallas_call | solution.py:120
  171.1 8.1 %all-to-all-done.1 = bf16[4,512,192]{1,2,0:T(8,128)(2,1)S(1)} async-done(((bf16[4,512,192]{1,2,0:T(8,128)(2,1)}), bf16[4,512,192]{1,2,0:T(8,128)(2,1)S(1)}, u32[]{:S(2)}, u32[]{:S(2)}) %all-to-all-start.1) | async-done | bytes 786464 | tf_op jit(solution)/shard_map/all_to_all | solution.py:190
  197.0 20.1 %all-to-all-done.3 = bf16[8,160,768]{2,1,0:T(8,128)(2,1)} async-done(((bf16[8,160,768]{2,1,0:T(8,128)(2,1)}), bf16[8,160,768]{2,1,0:T(8,128)(2,1)}, u32[]{:S(2)}, u32[]{:S(2)}) %all-to-all-start.3) | async-done | bytes 1966112 | tf_op jit(solution)/shard_map/all_to_all | solution.py:190
  217.1 10.6 %fusion.70 = f32[1280,2048]{1,0:T(8,128)} fusion(bf16[1280,768]{1,0:T(8,128)(2,1)} %bitcast.27, bf16[768,2048]{1,0:T(8,128)(2,1)} %bitcast.281), kind=kOutput, calls=%fused_computation.207 | convolution fusion | flops 4026531840 | bytes 15597568 | tf_op jit(solution)/shard_map/dot_general | solution.py:353
  227.8 12.1 %multiply_convert_fusion.2 = (bf16[1280,2048]{1,0:T(8,128)(2,1)}, f32[1280,2048]{1,0:T(8,128)}) fusion(f32[1280,2048]{1,0:T(8,128)} %fusion.70, bf16[1280,768]{1,0:T(8,128)(2,1)} %bitcast.27, bf16[768,2048]{1,0:T(8,128)(2,1)} %bitcast.283), kind=kOutput, calls=%fused_computation.13 | convolution fusion | flops 4042260480 | bytes 31326208 | tf_op jit(solution)/shard_map/dot_general | solution.py:354
  239.8 12.8 %all-gather.11.cloned.1.call-done = bf16[8,256,768]{2,1,0:T(8,128)(2,1)} async-done(((bf16[2,256,768]{2,1,0:T(8,128)(2,1)}), bf16[8,256,768]{2,1,0:T(8,128)(2,1)}) %all-gather.11.cloned.1.call-update) | async-done | bytes 3145744 | tf_op jit(solution)/shard_map/all_gather | solution.py:239
  252.6 9.0 %convolution_convert_fusion.3 = bf16[1280,768]{1,0:T(8,128)(2,1)} fusion(bf16[1280,2048]{1,0:T(8,128)(2,1)} %get-tuple-element.148, bf16[2048,768]{1,0:T(8,128)(2,1)} %bitcast.285), kind=kOutput, calls=%fused_computation.33 | convolution fusion | flops 4027514880 | bytes 10354688 | tf_op jit(solution)/shard_map/dot_general | solution.py:356
  271.3 19.1 %all-to-all-done.7 = bf16[8,160,768]{2,1,0:T(8,128)(2,1)} async-done(((bf16[8,160,768]{2,1,0:T(8,128)(2,1)}), bf16[8,160,768]{2,1,0:T(8,128)(2,1)}, u32[]{:S(2)}, u32[]{:S(2)}) %all-to-all-start.7) | async-done | bytes 1966112 | tf_op jit(solution)/shard_map/all_to_all | solution.py:190
  319.9 14.5 %while.5 = (s32[]{:T(128)}, bf16[4,528,256]{2,1,0:T(8,128)(2,1)}, s32[4,2]{0,1:T(2,128)S(1)}, bf16[4,512,256]{2,1,0:T(8,128)(2,1)}, s32[]{:T(128)}) while((s32[]{:T(128)}, bf16[4,528,256]{2,1,0:T(8,128)(2,1)}, s32[4,2]{0,1:T(2,128)S(1)}, bf16[4,512,256]{2,1,0:T(8,128)(2,1)}, s32[]{:T(128)}) %tuple.93), condition=%wide.while_cond, body=%wide.while_body.sunk | while | flops 2 | bytes 525921 | solution.py:441
  338.9 9.1 %convolution_convert_fusion = bf16[2048,768]{1,0:T(8,128)(2,1)} fusion(bf16[1280,2048]{1,0:T(8,128)(2,1)} %get-tuple-element.148, bf16[1280,768]{1,0:T(8,128)(2,1)} %bitcast.44), kind=kOutput, calls=%fused_computation.30 | convolution fusion | flops 4028104704 | bytes 10354688 | tf_op jit(solution)/shard_map/dot_general | solution.py:30
  349.2 14.7 %while.6 = (s32[]{:T(128)}, bf16[4,528,256]{2,1,0:T(8,128)(2,1)}, s32[4,2]{0,1:T(2,128)S(1)}, bf16[4,512,256]{2,1,0:T(8,128)(2,1)}, s32[]{:T(128)}) while((s32[]{:T(128)}, bf16[4,528,256]{2,1,0:T(8,128)(2,1)}, s32[4,2]{0,1:T(2,128)S(1)}, bf16[4,512,256]{2,1,0:T(8,128)(2,1)}, s32[]{:T(128)}) %tuple.108), condition=%wide.while_cond.1, body=%wide.while_body.1.sunk | while | flops 2 | bytes 525921 | solution.py:441
  364.9 14.5 %while.7 = (s32[]{:T(128)}, bf16[4,528,256]{2,1,0:T(8,128)(2,1)}, s32[4,2]{0,1:T(2,128)S(1)}, bf16[4,512,256]{2,1,0:T(8,128)(2,1)}, s32[]{:T(128)}) while((s32[]{:T(128)}, bf16[4,528,256]{2,1,0:T(8,128)(2,1)}, s32[4,2]{0,1:T(2,128)S(1)}, bf16[4,512,256]{2,1,0:T(8,128)(2,1)}, s32[]{:T(128)}) %tuple.109), condition=%wide.while_cond.2, body=%wide.while_body.2.sunk | while | flops 2 | bytes 525921 | solution.py:441
  385.6 15.7 %multiply_convert_fusion = (bf16[1280,2048]{1,0:T(8,128)(2,1)}, bf16[1280,2048]{1,0:T(8,128)(2,1)S(1)}) fusion(f32[1280,2048]{1,0:T(8,128)} %fusion.70, f32[1280,2048]{1,0:T(8,128)} %get-tuple-element.149, bf16[1280,768]{1,0:T(8,128)(2,1)} %bitcast.44, bf16[2048,768]{1,0:T(8,128)(2,1)} %bitcast.286), kind=kOutput, calls=%fused_computation.11 | convolution fusion | flops 4060610560 | bytes 36569088 | tf_op jit(solution)/shard_map/dot_general | solution.py:40
  418.2 8.1 %add_convert_fusion = bf16[1280,768]{1,0:T(8,128)(2,1)} fusion(f32[1280,768]{1,0:T(8,128)S(1)} %fusion.71, bf16[1280,2048]{1,0:T(8,128)(2,1)} %get-tuple-element.131, bf16[768,2048]{1,0:T(8,128)(2,1)S(1)} %bitcast.284), kind=kOutput, calls=%fused_computation.27 | convolution fusion | flops 4028497920 | bytes 14286848 | tf_op jit(solution)/shard_map/dot_general | solution.py:40
  438.2 18.2 %all-to-all-done.9 = bf16[8,160,768]{2,1,0:T(8,128)(2,1)} async-done(((bf16[8,160,768]{2,1,0:T(8,128)(2,1)}), bf16[8,160,768]{2,1,0:T(8,128)(2,1)}, u32[]{:S(2)}, u32[]{:S(2)}) %all-to-all-start.9) | async-done | bytes 1966112 | tf_op jit(solution)/shard_map/all_to_all | solution.py:190
  475.5 9.1 %convolution_convert_fusion.1 = bf16[768,2048]{1,0:T(8,128)(2,1)} fusion(bf16[1280,768]{1,0:T(8,128)(2,1)} %bitcast.27, bf16[1280,2048]{1,0:T(8,128)(2,1)} %get-tuple-element.131), kind=kOutput, calls=%fused_computation.31 | convolution fusion | flops 4028104704 | bytes 10354688 | tf_op jit(solution)/shard_map/dot_general | solution.py:30
  488.0 41.2 %attend_backward.1 = (bf16[2048,192]{1,0:T(8,128)(2,1)S(1)}, bf16[2048,192]{1,0:T(8,128)(2,1)S(1)}, bf16[2048,192]{1,0:T(8,128)(2,1)S(1)}) custom-call(bf16[2048,192]{1,0:T(8,128)(2,1)S(1)} %bitcast.244, f32[192,2048]{1,0:T(8,128)} %copy-done, f32[8,2048]{1,0:T(8,128)S(1)} %get-tuple-element.27.lse, bf16[3,2048,64]{2,1,0:T(8,128)(2,1)} %get-tuple-element.28.qn, ...), custom_call_target="tpu_custom_call" | custom-call | tf_op jit(solution)/shard_map/attend_backward/pallas_call | solution.py:180
  573.9 9.5 %all-to-all-done.13 = bf16[32,24,768]{2,1,0:T(8,128)(2,1)} async-done(((bf16[32,24,768]{2,1,0:T(8,128)(2,1)}), bf16[32,24,768]{2,1,0:T(8,128)(2,1)}, u32[]{:S(2)}, u32[]{:S(2)}) %all-to-all-start.13) | async-done | bytes 1179680 | tf_op jit(solution)/shard_map/all_to_all | solution.py:190
  602.1 9.6 %all-to-all-done.12 = bf16[32,24,576]{2,1,0:T(8,128)(2,1)S(1)} async-done(((bf16[32,24,576]{2,1,0:T(8,128)(2,1)}), bf16[32,24,576]{2,1,0:T(8,128)(2,1)S(1)}, u32[]{:S(2)}, u32[]{:S(2)}) %all-to-all-start.12) | async-done | bytes 884768 | tf_op jit(solution)/shard_map/all_to_all | solution.py:190
  617.2 10.1 %all-to-all-done.16 = bf16[2,256,768]{2,1,0:T(8,128)(2,1)} async-done(((bf16[2,256,768]{2,1,0:T(8,128)(2,1)}), bf16[2,256,768]{2,1,0:T(8,128)(2,1)}, u32[]{:S(2)}, u32[]{:S(2)}) %all-to-all-start.16) | async-done | bytes 786464 | tf_op jit(solution)/shard_map/all_to_all | solution.py:190
  (377 shorter events, 309.3 us)
Async XLA Ops:
  7.2 210.0 %all-gather.7.cloned.1.call-start = ((), (), s32[]{:S(2)}) async-start(), calls=%async_computation.23 | async-start | bytes 3932160 | tf_op jit(solution)/shard_map/all_gather | solution.py:239
  36.5 12.8 %all-to-all-start.6 = ((bf16[2,256,768]{2,1,0:T(8,128)(2,1)}), bf16[2,256,768]{2,1,0:T(8,128)(2,1)S(1)}, u32[]{:S(2)}, u32[]{:S(2)}) async-start(bf16[2,256,768]{2,1,0:T(8,128)(2,1)} %param.40), calls=%async_computation.6 | async-start | bytes 1572864 | tf_op jit(solution)/shard_map/all_to_all | solution.py:190
  50.5 53.3 %all-to-all-start = ((bf16[32,24,640]{2,1,0:T(8,128)(2,1)}), bf16[32,24,640]{2,1,0:T(8,128)(2,1)S(1)}, u32[]{:S(2)}, u32[]{:S(2)}) async-start(bf16[32,24,640]{2,1,0:T(8,128)(2,1)} %bitcast.8), calls=%async_computation | async-start | bytes 1966080 | tf_op jit(solution)/shard_map/all_to_all | solution.py:190
  55.7 172.1 %all-gather.9.cloned.1.call-start = ((), (), s32[]{:S(2)}) async-start(), calls=%async_computation.24 | async-start | bytes 3932160 | tf_op jit(solution)/shard_map/all_gather | solution.py:239
  56.6 26.9 %collective-permute-start = (bf16[1,528,768]{2,1,0:T(8,128)(2,1)S(1)}, bf16[1,528,768]{2,1,0:T(8,128)(2,1)S(1)}, u32[]{:S(2)}, u32[]{:S(2)}) collective-permute-start(bf16[1,528,768]{2,1,0:T(8,128)(2,1)S(1)} %fusion.21), channel_id=1, source_target_pairs={{0,2},{1,3},{2,0},{3,1},{4,6},{5,7},{6,4},{7,5},{8,10},{9,11},{10,... | collective-permute-start | bytes 2433032 | tf_op jit(solution)/shard_map/ppermute | solution.py:202
  85.6 26.5 %collective-permute-start.1 = (bf16[2,528,768]{2,1,0:T(8,128)(2,1)}, bf16[2,528,768]{2,1,0:T(8,128)(2,1)}, u32[]{:S(2)}, u32[]{:S(2)}) collective-permute-start(bf16[2,528,768]{2,1,0:T(8,128)(2,1)} %pad_maximum_fusion.3), channel_id=1, source_target_pairs={{0,1},{1,0},{2,3},{3,2},{4,5},{5,4},{6,7},{7,6},{8,9},{9,8},{10,11... | collective-permute-start | bytes 4866056 | tf_op jit(solution)/shard_map/ppermute | solution.py:202
  104.9 60.4 %all-to-all-start.2 = ((bf16[32,24,768]{2,1,0:T(8,128)(2,1)}), bf16[32,24,768]{2,1,0:T(8,128)(2,1)}, u32[]{:S(2)}, u32[]{:S(2)}) async-start(bf16[32,24,768]{2,1,0:T(8,128)(2,1)} %broadcast_in_dim.42), calls=%async_computation.2 | async-start | bytes 2359296 | tf_op jit(solution)/shard_map/all_to_all | solution.py:190
  165.3 13.9 %all-to-all-start.1 = ((bf16[4,512,192]{1,2,0:T(8,128)(2,1)}), bf16[4,512,192]{1,2,0:T(8,128)(2,1)S(1)}, u32[]{:S(2)}, u32[]{:S(2)}) async-start(bf16[4,512,192]{1,2,0:T(8,128)(2,1)} %copy.154), calls=%async_computation.1 | async-start | bytes 1572864 | tf_op jit(solution)/shard_map/all_to_all | solution.py:190
  169.2 83.5 %all-gather.11.cloned.1.call-start = ((), (), s32[]{:S(2)}) async-start(), calls=%async_computation.25 | async-start | bytes 3932160 | tf_op jit(solution)/shard_map/all_gather | solution.py:239
  186.8 30.3 %all-to-all-start.3 = ((bf16[8,160,768]{2,1,0:T(8,128)(2,1)}), bf16[8,160,768]{2,1,0:T(8,128)(2,1)}, u32[]{:S(2)}, u32[]{:S(2)}) async-start(bf16[8,160,768]{2,1,0:T(8,128)(2,1)} %bitcast.253), calls=%async_computation.3 | async-start | bytes 3932160 | tf_op jit(solution)/shard_map/all_to_all | solution.py:190
  261.6 28.8 %all-to-all-start.7 = ((bf16[8,160,768]{2,1,0:T(8,128)(2,1)}), bf16[8,160,768]{2,1,0:T(8,128)(2,1)}, u32[]{:S(2)}, u32[]{:S(2)}) async-start(bf16[8,160,768]{2,1,0:T(8,128)(2,1)} %bitcast.254), calls=%async_computation.7 | async-start | bytes 3932160 | tf_op jit(solution)/shard_map/all_to_all | solution.py:190
  309.3 29.6 %all-to-all-start.8 = ((bf16[8,160,768]{2,1,0:T(8,128)(2,1)}), bf16[8,160,768]{2,1,0:T(8,128)(2,1)}, u32[]{:S(2)}, u32[]{:S(2)}) async-start(bf16[8,160,768]{2,1,0:T(8,128)(2,1)} %bitcast.251), calls=%async_computation.8 | async-start | bytes 3932160 | tf_op jit(solution)/shard_map/all_to_all | solution.py:190
  315.1 296.7 %reduce-scatter.8.cloned.1.call-start = ((), (), s32[]{:S(2)}) async-start(), calls=%async_computation.22 | async-start | bytes 3932160 | tf_op jit(solution)/shard_map/reduce_scatter | solution.py:369
  348.1 269.1 %reduce-scatter.4.cloned.1.call-start = ((), (), s32[]{:S(2)}) async-start(), calls=%async_computation.20 | async-start | bytes 3932160 | tf_op jit(solution)/shard_map/reduce_scatter | solution.py:369
  426.4 30.0 %all-to-all-start.9 = ((bf16[8,160,768]{2,1,0:T(8,128)(2,1)}), bf16[8,160,768]{2,1,0:T(8,128)(2,1)}, u32[]{:S(2)}, u32[]{:S(2)}) async-start(bf16[8,160,768]{2,1,0:T(8,128)(2,1)} %bitcast.252), calls=%async_computation.9 | async-start | bytes 3932160 | tf_op jit(solution)/shard_map/all_to_all | solution.py:190
  469.7 15.7 %all-to-all-start.10 = ((bf16[4,512,192]{1,2,0:T(8,128)(2,1)}), bf16[4,512,192]{1,2,0:T(8,128)(2,1)}, u32[]{:S(2)}, u32[]{:S(2)}) async-start(bf16[4,512,192]{1,2,0:T(8,128)(2,1)} %bitcast.48), calls=%async_computation.10 | async-start | bytes 1572864 | tf_op jit(solution)/shard_map/all_to_all | solution.py:190
  475.3 167.2 %reduce-scatter.6.cloned.1.call-start = ((), (), s32[]{:S(2)}) async-start(), calls=%async_computation.21 | async-start | bytes 3932160 | tf_op jit(solution)/shard_map/reduce_scatter | solution.py:369
  549.7 33.7 %all-to-all-start.13 = ((bf16[32,24,768]{2,1,0:T(8,128)(2,1)}), bf16[32,24,768]{2,1,0:T(8,128)(2,1)}, u32[]{:S(2)}, u32[]{:S(2)}) async-start(bf16[32,24,768]{2,1,0:T(8,128)(2,1)} %bitcast.248), calls=%async_computation.13 | async-start | bytes 2359296 | tf_op jit(solution)/shard_map/all_to_all | solution.py:190
  566.0 26.7 %collective-permute-start.2 = (bf16[2,512,768]{2,1,0:T(8,128)(2,1)}, bf16[2,512,768]{2,1,0:T(8,128)(2,1)}, u32[]{:S(2)}, u32[]{:S(2)}) collective-permute-start(bf16[2,512,768]{2,1,0:T(8,128)(2,1)} %gather_fusion.4), channel_id=1, source_target_pairs={{0,1},{1,0},{2,3},{3,2},{4,5},{5,4},{6,7},{7,6},{8,9},{9,8},{10,11... | collective-permute-start | bytes 4718600 | tf_op jit(solution)/shard_map/ppermute | solution.py:455
  583.4 28.4 %all-to-all-start.12 = ((bf16[32,24,576]{2,1,0:T(8,128)(2,1)}), bf16[32,24,576]{2,1,0:T(8,128)(2,1)S(1)}, u32[]{:S(2)}, u32[]{:S(2)}) async-start(bf16[32,24,576]{2,1,0:T(8,128)(2,1)} %bitcast.55), calls=%async_computation.12 | async-start | bytes 1966080 | tf_op jit(solution)/shard_map/all_to_all | solution.py:190
  598.0 42.5 %collective-permute-start.3 = (bf16[1,512,768]{2,1,0:T(8,128)(2,1)}, bf16[1,512,768]{2,1,0:T(8,128)(2,1)S(1)}, u32[]{:S(2)}, u32[]{:S(2)}) collective-permute-start(bf16[1,512,768]{2,1,0:T(8,128)(2,1)} %slice.291), channel_id=1, source_target_pairs={{0,2},{1,3},{2,0},{3,1},{4,6},{5,7},{6,4},{7,5},{8,10},{9,11},{10,... | collective-permute-start | bytes 2359304 | tf_op jit(solution)/shard_map/ppermute | solution.py:455
  611.8 15.6 %all-to-all-start.16 = ((bf16[2,256,768]{2,1,0:T(8,128)(2,1)}), bf16[2,256,768]{2,1,0:T(8,128)(2,1)}, u32[]{:S(2)}, u32[]{:S(2)}) async-start(bf16[2,256,768]{2,1,0:T(8,128)(2,1)} %bitcast.257), calls=%async_computation.19 | async-start | bytes 1572864 | tf_op jit(solution)/shard_map/all_to_all | solution.py:190
  627.3 15.2 %all-to-all-start.14 = ((bf16[2,96,2048]{2,1,0:T(8,128)(2,1)}), bf16[2,96,2048]{2,1,0:T(8,128)(2,1)}, u32[]{:S(2)}, u32[]{:S(2)}) async-start(bf16[2,96,2048]{2,1,0:T(8,128)(2,1)} %bitcast.258), calls=%async_computation.15 | async-start | bytes 1572864 | tf_op jit(solution)/shard_map/all_to_all | solution.py:190
  642.6 14.7 %all-to-all-start.15 = ((bf16[2,96,2048]{2,1,0:T(8,128)(2,1)}), bf16[2,96,2048]{2,1,0:T(8,128)(2,1)}, u32[]{:S(2)}, u32[]{:S(2)}) async-start(bf16[2,96,2048]{2,1,0:T(8,128)(2,1)} %bitcast.259), calls=%async_computation.17 | async-start | bytes 1572864 | tf_op jit(solution)/shard_map/all_to_all | solution.py:190
  (61 other events, 521.4 us)
Sparse Core Ops, SparseCore 0:
  23.1 84.5 all-gather.6
  109.2 79.1 all-gather.8
  189.9 62.6 all-gather.10
  348.2 58.0 reduce-scatter.7
  411.0 58.2 reduce-scatter.3
  484.7 58.0 reduce-scatter.5

commit v3 on v2

v3 whole, which is shorter than its diff:
```python
import jax
import jax.numpy as jnp
import numpy as np
from jax import lax
from jax.experimental import pallas as pl
from jax.experimental.pallas import tpu as pltpu
from jax.sharding import Mesh, PartitionSpec as P

HEAD = 64
EXPERTS = 8
ROUTES = 12
CAP = 160
BLK = 512

OUTER = ("a", "b")
SEQ = ("sx", "sc")
ALL = OUTER + ("d",) + SEQ
PLANE = ("d",) + SEQ
ROWS = ("b", "d", "sx")

exact = lax.Precision.HIGHEST
epsilon = 1e-06
masked_out = -1e30
bf16 = jnp.bfloat16
f32 = jnp.float32


def rms_scale(values):
    return lax.rsqrt(jnp.mean(values * values, -1, keepdims=True) + epsilon)


def dot_rows(left, right, precision=None):
    return lax.dot_general(
        left,
        right,
        (((0,), (0,)), ((), ())),
        preferred_element_type=jnp.float32,
        precision=precision,
    )


def dot_last(left, right, precision=None):
    return lax.dot_general(
        left,
        right,
        (((1,), (1,)), ((), ())),
        preferred_element_type=jnp.float32,
        precision=precision,
    )


def nt(a,b): return lax.dot_general(a,b,(((1,),(1,)),((),())),preferred_element_type=f32)
def nn(a,b): return jnp.dot(a,b,preferred_element_type=f32)
def tn(a,b): return lax.dot_general(a,b,(((0,),(0,)),((),())),preferred_element_type=f32)

def fwd_kernel(tbl, held, gain, win, winT, start, normed, att, oT, lse, qn, kn, vn, qT, kT, kbuf, vbuf):
    i=pl.program_id(0)
    wide=win.shape[1]//3
    heads=wide//HEAD
    per=held.shape[1]//BLK
    t=tbl[i//per]
    off=pl.multiple_of((i%per)*BLK,BLK)
    x=held[t,pl.ds(off,BLK),:].astype(f32)
    scale=lax.rsqrt(jnp.mean(x*x,-1,keepdims=True)+epsilon)
    nb=(x*scale*gain[...]).astype(bf16)
    normed[...]=nb
    proj=nn(nb,win[...]).astype(bf16)
    projT=nt(winT[...],nb).astype(bf16)
    qs=projT[:wide]*bf16(HEAD ** -0.5)
    qT[...]=qs
    kT[...]=projT[wide:2*wide]
    vbuf[i]=projT[2*wide:]
    for h in range(heads):
        qn[h]=proj[:,h*HEAD:(h+1)*HEAD]*bf16(HEAD ** -0.5)
        kh=proj[:,wide+h*HEAD:wide+(h+1)*HEAD]
        kn[h]=kh
        kbuf[i,h]=kh
        vn[h]=proj[:,2*wide+h*HEAD:2*wide+(h+1)*HEAD]
    rows=lax.broadcasted_iota(jnp.int32,(BLK,BLK),0)
    cols=lax.broadcasted_iota(jnp.int32,(BLK,BLK),1)
    first=start[...]
    def tile(j,h,mask):
        s=nn(kbuf[j,h],qs[h*HEAD:(h+1)*HEAD])
        return jnp.where(mask,s,masked_out)
    mask=(rows+i*BLK>=first)&(rows<=cols)
    state=[]
    for h in range(heads):
        s=tile(i,h,mask)
        m=jnp.max(s,0,keepdims=True)
        e=jnp.exp(s-m)
        l=jnp.sum(e,0,keepdims=True)
        o=nn(vbuf[i,h*HEAD:(h+1)*HEAD],e.astype(bf16))
        state.append((m,l,o))
    def step(j,state):
        mask=rows+j*BLK>=first
        new=[]
        for h in range(heads):
            m,l,o=state[h]
            s=tile(j,h,mask)
            n=jnp.maximum(m,jnp.max(s,0,keepdims=True))
            a=jnp.exp(m-n)
            e=jnp.exp(s-n)
            l=l*a+jnp.sum(e,0,keepdims=True)
            o=o*a+nn(vbuf[j,h*HEAD:(h+1)*HEAD],e.astype(bf16))
            new.append((n,l,o))
        return tuple(new)
    state=lax.fori_loop(0,i,step,tuple(state))
    for h in range(heads):
        m,l,o=state[h]
        o=o/l
        oT[h*HEAD:(h+1)*HEAD]=o
        att[0,h*HEAD:(h+1)*HEAD]=o.astype(bf16)
        lse[h:h+1]=m+jnp.log(l)
    lse[heads:]=jnp.zeros((lse.shape[0]-heads,BLK),f32)

def attend_forward(table, held, gain, win, win_t, start, tokens, after):
    feat = held.shape[2]
    length = start.shape[1]
    wide = win.shape[1] // 3
    heads = wide // HEAD
    nb = length // BLK
    per = tokens // BLK
    whole = (None, None)
    heads_out = (sds((heads, length, HEAD), bf16), (heads, BLK, HEAD), by_mid)
    cols_out = (sds((wide, length), bf16), (wide, BLK), by_col)
    return call(
        fwd_kernel,
        "attend_forward",
        26,
        (nb,),
        [
            (table,) + whole,
            (held,) + whole,
            (gain,) + whole,
            (win,) + whole,
            (win_t,) + whole,
            (start, (1, BLK), by_col),
        ],
        [
            (sds((length, feat), bf16), (BLK, feat), by_row),
            (sds((length // tokens, wide, tokens), bf16), (1, wide, BLK), lambda i, *_: (i // per, 0, i % per)),
            (sds((wide, length), f32), (wide, BLK), by_col),
            (sds((8, length), f32), (8, BLK), by_col),
            heads_out,
            heads_out,
            heads_out,
            cols_out,
            cols_out,
        ],
        [pltpu.VMEM((nb, heads, BLK, HEAD), bf16), pltpu.VMEM((nb, wide, BLK), bf16)],
        prefetch=1,
        after=after,
    )


def bwd_kernel(
    table, go, o_t, lse, qn, kn, vn, q_t, k_t, start, held, normed, win, small,
    keep, send, gin, g_nat, dq, delta, gin_acc, gain_acc,
):
    j = pl.program_id(0)
    nb = pl.num_programs(0)
    heads = kn.shape[0]
    wide = q_t.shape[0]
    per = go.shape[2] // BLK
    rows = lax.broadcasted_iota(jnp.int32, (BLK, BLK), 0)
    cols = lax.broadcasted_iota(jnp.int32, (BLK, BLK), 1)

    def chunk(ref, i, lanes):
        return ref[i // per, lanes, pl.ds(pl.multiple_of(i % per * BLK, BLK), BLK)]

    @pl.when(j == 0)
    def _():
        dq[...] = jnp.zeros_like(dq)
        gin_acc[...] = jnp.zeros_like(gin_acc)
        gain_acc[...] = jnp.zeros_like(gain_acc)
        for b in range(g_nat.shape[0]):
            g = chunk(go, b, slice(None)).astype(f32)
            g_nat[b] = g.T.astype(bf16)
            prod = g * o_t[:, b * BLK : (b + 1) * BLK]
            for h in range(heads):
                delta[b, h : h + 1] = jnp.sum(prod[h * HEAD : (h + 1) * HEAD], 0, keepdims=True)

    def tile(i, accs, mask):
        new = []
        here = pl.ds(pl.multiple_of(i * BLK, BLK), BLK)
        inside = rows + j * BLK >= start[:, here]
        mask = inside if mask is None else mask & inside
        g_all = g_nat[i]
        for h in range(heads):
            dk, dv = accs[h]
            hs = slice(h * HEAD, (h + 1) * HEAD)
            s = nn(kn[h], q_t[hs, here])
            p = jnp.exp(jnp.where(mask, s, masked_out) - lse[h : h + 1, here])
            dv = dv + nn(p.astype(bf16), g_all[:, hs])
            dp = nn(vn[h], chunk(go, i, hs))
            d = (p * (dp - delta[i, h : h + 1])).astype(bf16)
            dk = dk + nn(d, qn[h, here])
            dq[i, hs] += nn(k_t[hs], d)
            new.append((dk, dv))
        return tuple(new)

    zero = jnp.zeros((BLK, HEAD), f32)
    accs = tile(j, tuple((zero, zero) for _ in range(heads)), rows <= cols)
    accs = lax.fori_loop(j + 1, nb, lambda i, a: tile(i, a, None), accs)
    gp = jnp.concatenate(
        [(dq[j] * HEAD**-0.5).T] + [a[0] for a in accs] + [a[1] for a in accs], 1
    ).astype(bf16)
    back = nt(gp, win[...])
    x = held[0].astype(f32)
    scale = lax.rsqrt(jnp.mean(x * x, -1, keepdims=True) + epsilon)
    gain_acc[0:1] += jnp.sum(back * (x * scale), 0, keepdims=True)
    gin_acc[...] += tn(normed[...], gp)
    place = table[j // per]
    half = keep.shape[0]
    here = pl.ds(pl.multiple_of(j % per * BLK, BLK), BLK)

    @pl.when(place < half)
    def _():
        keep[place, here, :] = back

    @pl.when(place >= half)
    def _():
        send[place - half, here, :] = back.astype(bf16)

    @pl.when(j == nb - 1)
    def _():
        gain = gain_acc[...].T[:, 0:1]
        high = gain.astype(bf16).astype(f32)
        lane = lax.broadcasted_iota(jnp.int32, small.shape, 1)
        tail = jnp.where(lane == 0, high, small[...].astype(f32))
        tail = jnp.where(lane == 21, gain - high, tail)
        gin[...] = jnp.concatenate([gin_acc[...], tail], 1).astype(bf16)


def attend_backward(
    table, go, o_t, lse, qn, kn, vn, q_t, k_t, start, held, normed, win, small, after
):
    n_seq, wide, tokens = go.shape
    length = n_seq * tokens
    heads = wide // HEAD
    feat = win.shape[0]
    nb = length // BLK
    per = tokens // BLK
    half = n_seq // 2
    whole = (None, None)

    def by_table(i, tbl):
        return (tbl[i // per], i % per, 0)

    return call(
        bwd_kernel,
        "attend_backward",
        38,
        (nb,),
        [
            (table,) + whole,
            (go,) + whole,
            (o_t,) + whole,
            (lse,) + whole,
            (qn,) + whole,
            (kn, (heads, BLK, HEAD), by_mid),
            (vn, (heads, BLK, HEAD), by_mid),
            (q_t,) + whole,
            (k_t, (wide, BLK), by_col),
            (start,) + whole,
            (held, (1, BLK, feat), by_table),
            (normed, (BLK, feat), by_row),
            (win,) + whole,
            (small,) + whole,
        ],
        [
            (sds((half, tokens, feat), f32),) + whole,
            (sds((half, tokens, feat), bf16),) + whole,
            (sds((feat, 3 * wide + small.shape[1]), bf16),) + whole,
        ],
        [
            pltpu.VMEM((nb, BLK, wide), bf16),
            pltpu.VMEM((nb, wide, BLK), f32),
            pltpu.VMEM((nb, 8, BLK), f32),
            pltpu.VMEM((feat, 3 * wide), f32),
            pltpu.VMEM((8, feat), f32),
        ],
        prefetch=1,
        after=after,
    )


def call(kernel, name, cost, grid, ins, outs, scratch=(), prefetch=0, limit=60, after=()):
    def spec(shape, block, index):
        if block is None:
            return pl.BlockSpec(shape, lambda *_: (0,) * len(shape))
        return pl.BlockSpec(block, index)

    n_in, n_out = len(ins), len(outs)

    def ordered(*refs):
        rest = refs[n_in + len(after) :]
        rest[n_out][...] = jnp.zeros_like(rest[n_out])
        kernel(*refs[:n_in], *rest[:n_out], *rest[n_out + 1 :])

    outs = list(outs) + [(sds((1, 1), f32), None, None)]
    return pl.pallas_call(
        ordered,
        grid_spec=pltpu.PrefetchScalarGridSpec(
            num_scalar_prefetch=prefetch,
            grid=grid,
            in_specs=[spec(a.shape, b, i) for a, b, i in ins[prefetch:]]
            + [pl.BlockSpec(memory_space=pl.ANY)] * len(after),
            out_specs=[spec(s.shape, b, i) for s, b, i in outs],
            scratch_shapes=list(scratch),
        ),
        out_shape=[s for s, _, _ in outs],
        compiler_params=pltpu.CompilerParams(vmem_limit_bytes=limit << 20),
        cost_estimate=pl.CostEstimate(
            flops=cost * 1150000000,
            bytes_accessed=sum(v.size * v.dtype.itemsize for v, _, _ in ins[prefetch:] + outs),
            transcendentals=0,
        ),
        name=name,
    )(*[a for a, _, _ in ins], *after)


def sds(shape, dtype):
    return jax.ShapeDtypeStruct(shape, dtype)


def by_row(i, *_):
    return (i, 0)


def by_col(i, *_):
    return (0, i)


def by_first(i, *_):
    return (i, 0, 0)


def by_last(i, *_):
    return (0, 0, i)


def by_mid(i, *_):
    return (0, i, 0)


def exact_dot(a, b, dims=((1,), (0,))):
    return lax.dot_general(a, b, (dims, ((), ())), preferred_element_type=f32, precision=exact)


def dispatch_rows(dest, rows, send):
    hosts, cap, features = send.shape
    group = max(g for g in range(1, hosts + 1) if hosts % g == 0 and g * cap <= 640)

    def one(h, carry):
        slot = lax.broadcasted_iota(jnp.int32, (group * cap, dest.shape[1]), 0) + h * group * cap
        hits = [slot == dest[r : r + 1] for r in range(2)]
        if len(rows) == 1:
            hits = [hits[0] | hits[1]]
        total = None
        for hit, part in zip(hits, rows):
            term = nn(jnp.where(hit, 1.0, 0.0).astype(bf16), part[...])
            total = term if total is None else total + term
        send[pl.ds(h * group, group)] = total.astype(bf16).reshape(group, cap, features)
        return carry

    lax.fori_loop(0, hosts // group, one, 0)


def mid_kernel(att, x, wo, gain, wrm, prev, dest, res, normed, soft, send, low):
    i = pl.program_id(0)
    n_seq, wide, block = att.shape
    acc = x[...].astype(f32)
    for s in range(n_seq):
        acc = acc + tn(att[s], wo[s * wide : (s + 1) * wide])
    res[...] = acc
    scale = lax.rsqrt(jnp.mean(acc * acc, -1, keepdims=True) + epsilon)
    unit = acc * scale * gain[...]
    normed[...] = unit
    low[pl.ds(pl.multiple_of(i * block, block), block), :] = unit.astype(bf16)
    logits = exact_dot(unit, wrm[...]) + prev[...]
    lane = lax.broadcasted_iota(jnp.int32, logits.shape, 1)
    result = jnp.zeros_like(logits)
    for lo, hi in ((0, ROUTES), (ROUTES, ROUTES + 2), (ROUTES + 2, ROUTES + 4)):
        inside = (lane >= lo) & (lane < hi)
        part = jnp.where(inside, logits, masked_out)
        expo = jnp.where(inside, jnp.exp(part - jnp.max(part, -1, keepdims=True)), 0.0)
        result = result + expo / jnp.sum(expo, -1, keepdims=True)
    soft[...] = result

    @pl.when(i == pl.num_programs(0) - 1)
    def _():
        dispatch_rows(dest, (low,), send)


def prepare_kernel(got, win, win_t, gains, wrm, out):
    inner = win.shape[1]
    out[...] = got[:, got.shape[1] - out.shape[1] :]
    turned = got[:, : got.shape[1] - out.shape[1]].astype(f32).T
    win[...] = got[:, :inner]
    win_t[...] = turned[:inner].astype(bf16)
    gains[0:2] = turned[inner : inner + 2]
    gains[2:4] = turned[inner + 18 : inner + 20]
    gains[4:8] = jnp.zeros_like(gains[4:8])
    wrm[...] = got[:, inner + 2 : inner + 18].astype(f32)


def gate_parts(soft, routes):
    lane = lax.broadcasted_iota(jnp.int32, soft.shape, 1)
    hits = [(lane == routes[:, r : r + 1]).astype(f32) for r in range(2)]
    picked = [jnp.sum(h * soft, -1, keepdims=True) for h in hits]
    total = picked[0] + picked[1]
    gates = [p / total for p in picked]
    spread = gates[0] * hits[0] + gates[1] * hits[1]

    def lane_of(values, k):
        return values[:, k : k + 1]

    copy = lane_of(spread, EXPERTS + 1)
    const = [lane_of(spread, EXPERTS + 2 + c) for c in range(2)]
    mix = [[lane_of(soft, ROUTES + 2 * c + k) for k in range(2)] for c in range(2)]
    return lane, hits, total, gates, copy, const, mix


def loss_kernel(
    back, dest_col, dest, routes, soft, normed, res, teacher, valid, vectors, factor,
    out, grad, stats, send, squared, low0, low1,
):
    i = pl.program_id(0)
    block = res.shape[0]
    hosts, cap, features = back.shape
    rows = back[...].reshape(hosts * cap, features)
    slot = lax.broadcasted_iota(jnp.int32, (block, hosts * cap), 1)
    terms = [
        nn(jnp.where(slot == dest_col[:, r : r + 1], 1.0, 0.0).astype(bf16), rows)
        for r in range(2)
    ]
    lane, hits, total, gates, copy, const, mix = gate_parts(soft[...], routes[...])
    vec = [vectors[c : c + 1] for c in range(2)]
    unit = normed[...]
    full = res[...] + (copy + const[0] * mix[0][0] + const[1] * mix[1][0]) * unit
    full = full + (const[0] * mix[0][1]) * vec[0] + (const[1] * mix[1][1]) * vec[1]
    full = full + gates[0] * terms[0] + gates[1] * terms[1]
    out[...] = full.astype(bf16)
    ok = valid[...]
    differ = (full - teacher[...].astype(f32)) * ok
    gf = differ * factor[0, 0]
    grad[...] = gf
    here = pl.ds(pl.multiple_of(i * block, block), block)
    low0[here, :] = (gates[0] * gf).astype(bf16)
    low1[here, :] = (gates[1] * gf).astype(bf16)

    def over(values):
        return jnp.sum(gf * values, -1, keepdims=True)

    parts = [over(terms[0]), over(terms[1]), over(unit), over(vec[0]), over(vec[1])]
    tile = lax.broadcasted_iota(jnp.int32, stats.shape, 1)
    filled = jnp.zeros(stats.shape, f32)
    for k, part in enumerate(parts):
        filled = jnp.where(tile == k, part, filled)
    stats[...] = filled

    @pl.when(i == 0)
    def _():
        squared[...] = jnp.zeros_like(squared)

    squared[...] += jnp.sum(differ * differ, 0, keepdims=True)

    @pl.when(i == pl.num_programs(0) - 1)
    def _():
        dispatch_rows(dest, (low0, low1), send)


def route_kernel(soft, routes, stats, grad, normed, wrm, partial, small, small_vec):
    i = pl.program_id(0)
    probs = soft[...]
    lane, hits, total, gates, copy, const, mix = gate_parts(probs, routes[...])
    s = stats[...]
    dots = [s[:, k : k + 1] for k in range(5)]
    const_dot = [mix[c][0] * dots[2] + mix[c][1] * dots[3 + c] for c in range(2)]
    grad_gates = []
    for r in range(2):
        h = hits[r]
        grad_gates.append(
            dots[r]
            + h[:, EXPERTS + 1 : EXPERTS + 2] * dots[2]
            + h[:, EXPERTS + 2 : EXPERTS + 3] * const_dot[0]
            + h[:, EXPERTS + 3 : EXPERTS + 4] * const_dot[1]
        )
    mean = gates[0] * grad_gates[0] + gates[1] * grad_gates[1]
    grad_probs = sum(hits[r] * ((grad_gates[r] - mean) / total) for r in range(2))
    only = jnp.where(lane < ROUTES, probs, 0.0)
    both = only * (grad_probs - jnp.sum(only * grad_probs, -1, keepdims=True))
    for c in range(2):
        grad_mix = [const[c] * dots[2], const[c] * dots[3 + c]]
        inner = mix[c][0] * grad_mix[0] + mix[c][1] * grad_mix[1]
        for k in range(2):
            both = jnp.where(lane == ROUTES + 2 * c + k, mix[c][k] * (grad_mix[k] - inner), both)
    gf = grad[...]
    unit = normed[...]
    coef = copy + const[0] * mix[0][0] + const[1] * mix[1][0]
    partial[...] = coef * gf + exact_dot(both, wrm[...], ((1,), (1,)))
    spread = jnp.where(lane == 0, const[0] * mix[0][1], 0.0)
    spread = jnp.where(lane == 1, const[1] * mix[1][1], spread)

    @pl.when(i == 0)
    def _():
        small[...] = jnp.zeros_like(small)
        small_vec[...] = jnp.zeros_like(small_vec)

    small[...] += exact_dot(unit, both, ((0,), (0,)))
    small_vec[...] += exact_dot(gf, spread, ((0,), (0,)))


def join_kernel(
    back, dest_col, partial, res, grad, gain, wo, mid, branch, out, gain_grad
):
    i = pl.program_id(0)
    block = res.shape[0]
    hosts, cap, features = back.shape
    rows = back[...].reshape(hosts * cap, features)
    slot = lax.broadcasted_iota(jnp.int32, (block, hosts * cap), 1)
    hit = (slot == dest_col[:, 0:1]) | (slot == dest_col[:, 1:2])
    grad_normed = partial[...] + nn(jnp.where(hit, 1.0, 0.0).astype(bf16), rows)
    r = res[...]
    scale = lax.rsqrt(jnp.mean(r * r, -1, keepdims=True) + epsilon)
    unit = r * scale

    @pl.when(i == 0)
    def _():
        gain_grad[...] = jnp.zeros_like(gain_grad)

    gain_grad[...] += jnp.sum(grad_normed * unit, 0, keepdims=True)
    hat = grad_normed * gain[...]
    total = grad[...] + scale * (hat - unit * jnp.mean(hat * unit, -1, keepdims=True))
    mid[...] = total
    low = total.astype(bf16)
    branch[...] = low
    n_seq, wide, _ = out.shape
    for s in range(n_seq):
        out[s] = nt(wo[s * wide : (s + 1) * wide], low).astype(bf16)


def out_grad_kernel(att, branch, out):
    n_seq, wide, _ = att.shape
    for s in range(n_seq):
        out[s * wide : (s + 1) * wide] = nn(att[s], branch[...]).astype(bf16)


def whole_tile(me, own, other, tile):
    tile[:, pl.ds(me[0], 1)] = own[:, None]
    tile[:, pl.ds(1 - me[0], 1)] = other[:, None]
    return tile[...].reshape(-1, tile.shape[-1])


def split_tile(me, values, tile):
    tile[...] = values.reshape(tile.shape)
    return tile[:, pl.ds(me[0], 1)][:, 0], tile[:, pl.ds(1 - me[0], 1)][:, 0]


def expert_hidden_kernel(me, rows, own, other, gate_part, up_part, hidden, gate, up):
    x = rows[...]
    g = nn(x, whole_tile(me, own[:, 0], other[:, 0], gate))
    u = nn(x, whole_tile(me, own[:, 1], other[:, 1], up))
    gate_part[...] = g
    up_part[...] = u
    hidden[...] = (g / (1.0 + jnp.exp(-g)) * u).astype(bf16)


def expert_result_kernel(me, hidden, own, other, result, down):
    @pl.when(pl.program_id(0) == 0)
    def _():
        whole_tile(me, own[...], other[...], down)

    result[...] = nn(hidden[...], down[...].reshape(-1, down.shape[-1])).astype(bf16)


def down_grad_kernel(me, hidden, grad, own, other, parts):
    own[...], other[...] = split_tile(me, tn(hidden[...], grad[...]).astype(bf16), parts)


def expert_backward_kernel(
    me, rows, grad, gate_part, up_part, own, other, down_own, down_other,
    d_own, d_other, result, gate, up, down, parts, acc,
):
    f = pl.program_id(0)
    gh = nt(grad[...], whole_tile(me, down_own[...], down_other[...], down))
    g = gate_part[...]
    u = up_part[...]
    sig = 1.0 / (1.0 + jnp.exp(-g))
    dg = (gh * u * sig * (1.0 + g * (1.0 - sig))).astype(bf16)
    du = (gh * (g * sig)).astype(bf16)
    for k, d in enumerate((dg, du)):
        d_own[:, k], d_other[:, k] = split_tile(me, tn(rows[...], d).astype(bf16), parts)
    part = nt(dg, whole_tile(me, own[:, 0], other[:, 0], gate))
    part = part + nt(du, whole_tile(me, own[:, 1], other[:, 1], up))

    @pl.when(f == 0)
    def _():
        acc[...] = part

    @pl.when(f > 0)
    def _():
        acc[...] += part

    @pl.when(f == pl.num_programs(0) - 1)
    def _():
        result[...] = acc[...].astype(bf16)


def seq_add_kernel(keep, given, near, far):
    near[...] = keep[0] + given[0].astype(f32)
    far[...] = (keep[1] + given[1].astype(f32)).astype(bf16)


def finish_kernel(near, given, mid, x, gain, out):
    grad = near[...] + given[...].astype(f32)
    values = x[...].astype(f32)
    scale = lax.rsqrt(jnp.mean(values * values, -1, keepdims=True) + epsilon)
    unit = values * scale
    hat = grad * gain[...]
    out[...] = mid[...] + scale * (hat - unit * jnp.mean(hat * unit, -1, keepdims=True))


def exchange(blocks, axes):
    return lax.all_to_all(blocks, axes, split_axis=0, concat_axis=0, tiled=True)


def to_all(block, count):
    return exchange(jnp.broadcast_to(block[None], (count,) + block.shape), ALL)


def gather_seq(block, size):
    held = block[None]
    step = size // 2
    while step:
        pairs = [(i, i ^ step) for i in range(size)]
        held = jnp.concatenate([held, lax.ppermute(held, SEQ, pairs)], 0)
        step //= 2
    order = [0]
    step = size // 2
    while step:
        order = order + [k ^ step for k in order]
        step //= 2
    return held, order


def body(
    block_input,
    teacher,
    prev_logits,
    valid_mask,
    segments,
    routes,
    input_proj,
    output_proj,
    attention_gain,
    mixture_gain,
    router,
    const_mix,
    const_vectors,
    expert_gate,
    expert_up,
    expert_down,
):
    n_out, n_in, n_seq = (lax.axis_size(a) for a in (OUTER, "d", SEQ))
    n_all = n_out * n_in * n_seq
    n_far = lax.axis_size("a")
    tokens_here, features = block_input.shape
    rows_here = input_proj.shape[0]
    wide = features // n_seq
    seq_id = lax.axis_index(SEQ)

    a_id, b_id, d_id, c_id = (lax.axis_index(x) for x in ("a", "b", "d", "sc"))
    me = c_id.reshape(1)
    swap = [(0, 1), (1, 0)]
    cross = [(1, 2), (2, 1)]

    def item(values, index):
        return lax.dynamic_index_in_dim(values, index, 0, keepdims=False)

    def in_order(index, mine, given):
        return jnp.where(index == 0, jnp.stack([mine, given]), jnp.stack([given, mine]))

    place = [(b, d, c) for b in range(2) for d in range(2) for c in range(2)]
    alike = [(4 * b + 2 * d + c, 4 * b + 2 * c + d) for b, d, c in place if d != c]
    unlike = [(4 * b + 2 * d + c, 4 * (1 - b) + 2 * c + d) for b, d, c in place]

    def cross(same, other):
        same = jnp.where(c_id == d_id, same, lax.ppermute(same, ("b", "d", "sc"), alike))
        return in_order(b_id, same, lax.ppermute(other, ("b", "d", "sc"), unlike))

    def far_pair(pair):
        return lax.all_gather(pair, "a", axis=0, tiled=False)

    def both_cores(far, done):
        own = far.reshape((n_out,) + far.shape[2:]) + done[0, 0].astype(bf16)
        return own, lax.ppermute(own, "sc", swap)

    def core_sum(own, other):
        total = own.astype(f32) + lax.ppermute(other, "sc", swap).astype(f32)
        return total.astype(bf16).reshape((n_far, 2) + own.shape[1:])

    def far_sum(part):
        return lax.psum_scatter(part, "a", scatter_dimension=0, tiled=False)

    def to_owner(part):
        return cross(item(part, b_id), item(part, 1 - b_id)).astype(f32)

    slice_rows = expert_gate.shape[1]
    odd_rows = slice_rows % 16 != 0

    def to_order(own, other):
        pair = in_order(c_id, own, other)
        return pair.transpose(2, 1, 0, 3, 4).reshape(2, features, -1)

    def from_order(both, count):
        pair = both.reshape(2, count, 2, -1, both.shape[2]).transpose(2, 1, 0, 3, 4)
        return item(pair, c_id), item(pair, 1 - c_id)

    def gate_and_up(index):
        return jnp.stack([item(expert_gate, index), item(expert_up, index)])

    in_pair = cross(gate_and_up(b_id), gate_and_up(1 - b_id))
    down_pair = cross(item(expert_down, b_id), item(expert_down, 1 - b_id))
    own_cols = input_proj.reshape(rows_here, 3, n_seq, wide)
    own_cols = own_cols.transpose(0, 2, 1, 3).reshape(rows_here, -1)
    count_here = jnp.sum(valid_mask)
    count_cols = jnp.stack([count_here // 32, count_here % 32]).astype(bf16)
    small = jnp.concatenate(
        [
            attention_gain[:, None],
            mixture_gain[:, None],
            router,
            const_mix,
            const_vectors.T,
            jnp.broadcast_to(count_cols[None], (rows_here, 2)),
        ],
        1,
    )
    n_small = small.shape[1]
    small = jnp.pad(small, ((0, 0), (0, -(3 * wide + n_small) % 128)))
    packed = jnp.concatenate(
        [
            own_cols.reshape(rows_here, n_seq, 3 * wide).transpose(1, 0, 2),
            jnp.broadcast_to(small[None], (n_seq,) + small.shape),
        ],
        2,
    )
    n_plane = n_in * n_seq
    piece = features // n_plane
    out_piece = output_proj.reshape(rows_here, n_in, n_seq, piece).transpose(1, 2, 0, 3)
    inner = packed.shape[2]
    packed = jnp.concatenate(
        [jnp.broadcast_to(packed[None], (n_in,) + packed.shape), out_piece], 3
    )
    packed = jnp.pad(packed, ((0, 0),) * 3 + ((0, -packed.shape[3] % 128),))
    packed = jnp.broadcast_to(packed[None], (n_out,) + packed.shape)
    got = exchange(packed.reshape((n_all,) + packed.shape[3:]), ALL)
    counts = got[:, 0, 3 * wide + 20 : 3 * wide + 22].astype(f32)
    valid_count = jnp.sum(counts[:, 0]) * 32.0 + jnp.sum(counts[:, 1])
    got = got.reshape(features, -1)
    own_in, own_in_t, gains, wrm, out_cols, prepared = call(
        prepare_kernel,
        "prepare",
        3,
        (1,),
        [(got, None, None)],
        [
            (sds((features, 3 * wide), bf16), None, None),
            (sds((3 * wide, features), bf16), None, None),
            (sds((8, features), f32), None, None),
            (sds((features, ROUTES + 4), f32), None, None),
            (sds((features, got.shape[1] - inner), bf16), None, None),
        ],
    )
    in_far = far_pair(in_pair)
    down_far = far_pair(down_pair + prepared[0, 0].astype(bf16))
    gain_first, gain_mid, vectors_f = gains[0:1], gains[1:2], gains[2:4]
    out_part = jnp.broadcast_to(out_cols[None], (n_plane,) + out_cols.shape)
    full_out = exchange(out_part, PLANE)[:, :, :piece].transpose(1, 0, 2)
    full_out = full_out.reshape(features, features)

    seg_row = jnp.pad(segments.astype(bf16), (0, features * 2 - tokens_here)).reshape(2, features)
    with_seg = jnp.concatenate(
        [block_input, jnp.pad(seg_row, ((0, 14), (0, 0)))], 0
    )
    held, order = gather_seq(with_seg, n_seq)
    where = [order.index(j) for j in range(n_seq)]
    chosen = jnp.array(where, jnp.int32)[jnp.arange(n_seq) ^ seq_id]
    length = n_seq * tokens_here
    seq_segments = (
        held[:, tokens_here : tokens_here + 2]
        .reshape(n_seq, 2 * features)[:, :tokens_here][chosen]
        .reshape(1, -1)
    )
    positions = jnp.arange(length, dtype=jnp.int32)[None]
    fresh = seq_segments != jnp.pad(seq_segments[:, :-1], ((0, 0), (1, 0)), constant_values=-1)
    start = lax.cummax(jnp.where(fresh, positions, 0), axis=1)

    normed_first, attended, attended_t, log_totals, *heads_saved, forward_done = attend_forward(
        chosen, held, gain_first, own_in, own_in_t, start, tokens_here,
        [],
    )
    attended_tok = exchange(attended, SEQ)

    flat_routes = routes.reshape(-1)
    onehot_e = (flat_routes[:, None] == jnp.arange(EXPERTS, dtype=jnp.int32)[None, :]).astype(
        jnp.int32
    )
    slot_rank = jnp.sum((jnp.cumsum(onehot_e, 0) - onehot_e) * onehot_e, -1)
    host = (flat_routes % 2) * 4 + flat_routes // 2 % 2 * 2 + flat_routes // 4
    slot_dest = jnp.where(flat_routes < EXPERTS, host * CAP + slot_rank, EXPERTS * CAP)
    slot_dest = slot_dest.reshape(tokens_here, 2)
    slot_row = jnp.pad(slot_dest.T, ((0, 6), (0, 0)))

    whole = (None, None)
    rows_block = 128
    steps = (tokens_here // rows_block,)
    wide_block = ((rows_block, features), by_row)
    soft_block = ((rows_block, ROUTES + 4), by_row)
    pair_block = ((rows_block, 2), by_row)
    slots_shape = (EXPERTS, CAP, features)
    tok = sds((tokens_here, features), f32)
    residual_mid, normed, soft, send_rows, mid_done = call(
        mid_kernel,
        "mid",
        10,
        steps,
        [
            (attended_tok, (n_seq, wide, rows_block), by_last),
            (block_input,) + wide_block,
            (full_out,) + whole,
            (gain_mid,) + whole,
            (wrm,) + whole,
            (jnp.pad(prev_logits, ((0, 0), (0, 4))),) + soft_block,
            (slot_row,) + whole,
        ],
        [
            (tok,) + wide_block,
            (tok,) + wide_block,
            (sds((tokens_here, ROUTES + 4), f32),) + soft_block,
            (sds(slots_shape, bf16),) + whole,
        ],
        [pltpu.VMEM((tokens_here, features), bf16)],
    )
    in_parts_w = both_cores(in_far, mid_done)
    if odd_rows:
        in_parts_w = from_order(to_order(*in_parts_w), 4)
    recv_rows = exchange(send_rows, ROWS).reshape(-1, features)
    n_rows = recv_rows.shape[0]
    hid = expert_gate.shape[2]
    tile = 512 if hid % 512 == 0 else hid
    tiles = (hid // tile,)
    pieces, _, piece_rows, _ = in_parts_w[0].shape
    w_part = ((pieces, 2, piece_rows, tile), lambda i, *_: (0, 0, 0, i))
    w_tile = pltpu.VMEM((pieces, 2, piece_rows, tile), bf16)
    h_col = ((n_rows, tile), by_col)
    in_parts = [(w,) + w_part for w in in_parts_w]
    gate_part, up_part, hidden, hidden_done = call(
        expert_hidden_kernel,
        "expert_hidden",
        14,
        tiles,
        [(me,) + whole, (recv_rows,) + whole] + in_parts,
        [
            (sds((n_rows, hid), f32),) + h_col,
            (sds((n_rows, hid), f32),) + h_col,
            (sds((n_rows, hid), bf16),) + h_col,
        ],
        [w_tile] * 2,
        prefetch=1,
    )
    down_parts_w = both_cores(down_far, hidden_done)
    far_pieces, far_rows, _ = down_parts_w[0].shape
    per_tile = tile // (2 * far_rows)
    down_block = ((per_tile, far_rows, features), by_first)
    down_tile = pltpu.VMEM((per_tile, 2, far_rows, features), bf16)
    row_tile = n_rows // 4
    result_rows, _ = call(
        expert_result_kernel,
        "expert_result",
        8,
        (4,),
        [
            (me,) + whole,
            (hidden, (row_tile, hid), by_row),
            (down_parts_w[0],) + whole,
            (down_parts_w[1],) + whole,
        ],
        [(sds((n_rows, features), bf16), (row_tile, features), by_row)],
        [pltpu.VMEM((far_pieces, 2, far_rows, features), bf16)],
        prefetch=1,
    )
    back_rows = exchange(result_rows.reshape(slots_shape), ROWS)
    valid_f = valid_mask.astype(f32)[:, None]
    factor = (tokens_here * n_all / valid_count).reshape(1, 1)
    full_output, grad_full, stats, grad_send, squared, _ = call(
        loss_kernel,
        "loss",
        11,
        steps,
        [
            (back_rows,) + whole,
            (slot_dest,) + pair_block,
            (slot_row,) + whole,
            (routes,) + pair_block,
            (soft,) + soft_block,
            (normed,) + wide_block,
            (residual_mid,) + wide_block,
            (teacher,) + wide_block,
            (valid_f, (rows_block, 1), by_row),
            (vectors_f,) + whole,
            (factor,) + whole,
        ],
        [
            (sds((tokens_here, features), bf16),) + wide_block,
            (tok,) + wide_block,
            (sds((tokens_here, 8), f32), (rows_block, 8), by_row),
            (sds(slots_shape, bf16),) + whole,
            (sds((1, features), f32),) + whole,
        ],
        [pltpu.VMEM((tokens_here, features), bf16)] * 2,
    )
    grad_recv = exchange(grad_send, ROWS).reshape(-1, features)
    *down_grads, _ = call(
        down_grad_kernel,
        "down_grad",
        8,
        tiles,
        [(me,) + whole, (hidden,) + h_col, (grad_recv,) + whole],
        [(sds(down_parts_w[0].shape, bf16),) + down_block] * 2,
        [down_tile],
        prefetch=1,
    )
    down_sum = core_sum(*down_grads)
    part_out = (sds(in_parts_w[0].shape, bf16),) + w_part
    *in_grads, grad_rows, backward_done = call(
        expert_backward_kernel,
        "expert_backward",
        32,
        tiles,
        [
            (me,) + whole,
            (recv_rows,) + whole,
            (grad_recv,) + whole,
            (gate_part,) + h_col,
            (up_part,) + h_col,
        ]
        + in_parts
        + [
            (down_parts_w[0],) + down_block,
            (down_parts_w[1],) + down_block,
        ],
        [part_out] * 2 + [(sds((n_rows, features), bf16),) + whole],
        [w_tile] * 2 + [down_tile, w_tile, pltpu.VMEM((n_rows, features), f32)],
        prefetch=1,
        after=[down_sum],
    )
    grad_back = exchange(grad_rows.reshape(slots_shape), ROWS)
    if odd_rows:
        in_grads = from_order(to_order(*in_grads), n_out)
    partial_normed, small_cols, vector_cols, route_done = call(
        route_kernel,
        "route",
        14,
        steps,
        [
            (soft,) + soft_block,
            (routes,) + pair_block,
            (stats, (rows_block, 8), by_row),
            (grad_full,) + wide_block,
            (normed,) + wide_block,
            (wrm,) + whole,
        ],
        [
            (tok,) + wide_block,
            (sds((features, ROUTES + 4), f32),) + whole,
            (sds((features, ROUTES + 4), f32),) + whole,
        ],
    )
    in_sum = core_sum(*in_grads)

    grad_mid, grad_branch, grad_attended, grad_mixture_gain, _ = call(
        join_kernel,
        "join",
        8,
        steps,
        [
            (grad_back,) + whole,
            (slot_dest,) + pair_block,
            (partial_normed,) + wide_block,
            (residual_mid,) + wide_block,
            (grad_full,) + wide_block,
            (gain_mid,) + whole,
            (full_out,) + whole,
        ],
        [
            (tok,) + wide_block,
            (sds((tokens_here, features), bf16),) + wide_block,
            (sds((n_seq, wide, tokens_here), bf16), (n_seq, wide, rows_block), by_last),
            (sds((1, features), f32),) + whole,
        ],
        after=[in_sum],
    )
    grad_output_proj, _ = call(
        out_grad_kernel,
        "out_grad",
        3,
        (1,),
        [(attended_tok,) + whole, (grad_branch,) + whole],
        [(sds((features, features), bf16),) + whole],
    )
    down_part = far_sum(down_sum)
    grad_heads = exchange(grad_attended, SEQ)

    def to_plane(part):
        part = part.reshape(n_out, n_in * n_seq, rows_here, -1).transpose(1, 0, 2, 3)
        return exchange(part, PLANE)

    out_grad = jnp.sum(to_plane(grad_output_proj).astype(f32), 0).astype(bf16)

    small_grads = jnp.concatenate(
        [
            jnp.zeros((features, 1), f32),
            grad_mixture_gain.T,
            small_cols,
            vector_cols[:, :2],
            jnp.broadcast_to(jnp.sum(squared), (features, 1)),
        ],
        1,
    )
    n_small = small_grads.shape[1]

    def two_parts(values, axis):
        high = values.astype(bf16)
        rest = (values - high.astype(f32)).astype(bf16)
        both = jnp.concatenate([high, rest], axis)
        return both

    small_low = two_parts(small_grads, 1)
    small_low = jnp.pad(small_low, ((0, 0), (0, -(3 * wide + 2 * n_small) % 128)))
    keep, sent, last, attention_done = attend_backward(
        chosen, grad_heads, attended_t, log_totals, *heads_saved, start, held, normed_first,
        own_in, small_low, [grad_output_proj],
    )

    sent = lax.ppermute(sent, SEQ, [(i, i ^ 1) for i in range(n_seq)])
    near, sent, added = call(
        seq_add_kernel,
        "seq_add",
        3,
        (2,),
        [
            (keep, (2, tokens_here // 2, features), by_mid),
            (sent, (2, tokens_here // 2, features), by_mid),
        ],
        [
            (tok, (tokens_here // 2, features), by_row),
            (sds((tokens_here, features), bf16), (tokens_here // 2, features), by_row),
        ],
    )
    sent = lax.ppermute(sent, SEQ, [(i, i ^ 2) for i in range(n_seq)])
    grad_input, finished = call(
        finish_kernel,
        "finish",
        3,
        steps,
        [
            (near,) + wide_block,
            (sent,) + wide_block,
            (grad_mid,) + wide_block,
            (block_input,) + wide_block,
            (gain_first,) + whole,
        ],
        [(tok,) + wide_block],
    )
    grad_expert_down = to_owner(down_part + attention_done[0, 0].astype(bf16))
    in_grads = to_owner(far_sum(in_sum) + finished[0, 0].astype(bf16))
    grad_expert_gate, grad_expert_up = in_grads[:, 0], in_grads[:, 1]

    last = last + added[0, 0].astype(bf16)
    last = to_plane(last)
    cols = last[:, :, :, : 3 * wide].reshape(n_in, n_seq, n_out, rows_here, 3 * wide)
    cols = (jnp.sum(cols.astype(f32), 0) + finished[0, 0]).astype(bf16).transpose(1, 2, 0, 3)
    rest = jnp.sum(last[:, :, :, 3 * wide : 3 * wide + 2 * n_small].astype(f32), 0)
    rest = rest[:, :, :n_small] + rest[:, :, n_small:]
    last = jnp.concatenate(
        [cols.reshape(n_out, rows_here, -1), out_grad, two_parts(rest, 2)], 2
    )
    last = jnp.pad(last, ((0, 0), (0, 0), (0, -last.shape[2] % 128)))
    last = jnp.sum(exchange(last, OUTER).astype(f32), 0)
    grad_input_proj = (
        last[:, : 3 * features]
        .reshape(rows_here, n_seq, 3, wide)
        .transpose(0, 2, 1, 3)
        .reshape(rows_here, 3 * features)
    )
    grad_output_proj = last[:, 3 * features : 4 * features]
    last = last[:, 4 * features : 4 * features + 2 * n_small]
    small_grads = last[:, :n_small] + last[:, n_small:]
    mean_loss = small_grads[0, 20] / (2.0 * features * valid_count)
    return (
        full_output,
        mean_loss,
        grad_input,
        grad_input_proj,
        grad_output_proj,
        small_grads[:, 0],
        small_grads[:, 1],
        small_grads[:, 2:14],
        small_grads[:, 14:18],
        small_grads[:, 18:20].T,
        grad_expert_gate,
        grad_expert_up,
        grad_expert_down,
    )


def solution(mesh):
    cut = Mesh(mesh.devices.reshape(-1, 2, 2, 2, mesh.shape["seq"] // 2), ALL)
    rows = P(ALL, None)
    line = P(ALL)
    cols = P(None, ALL)
    expert = P(SEQ, OUTER + ("d",), None)
    return jax.shard_map(
        body,
        mesh=cut,
        in_specs=(rows, rows, rows, line, line, rows, rows, rows, line, line, rows, rows, cols)
        + (expert,) * 3,
        out_specs=(rows, P(), rows, rows, rows, line, line, rows, rows, cols) + (expert,) * 3,
        check_vma=False,
    )
```

time: 679 us -> 572 us (0.84)
  matrix products: 137 us -> 0 us
  Pallas kernels: 85 us -> 185 us
  local copies, waits for them, and re-layouts: 109 us -> 41.4 us
  waiting for transfers between devices: 167 us -> 193 us
  starting transfers between devices: 71.8 us -> 53.8 us
  other arithmetic: 47.4 us -> 36 us
    dot_general x28 -> x0, matrix products: 137 us -> none  [the longest x7 45.1 us: dot_last(): lax.dot_general(left, right, (((1,), (1,)), ((), ())), preferred_element_...]
    pallas_call x2 -> x14, Pallas kernels: 85 us -> 185 us  [call(): pl.pallas_call(ordered, grid_spec=pltpu.PrefetchScalarGridSpec(num_scalar...]
    gather x41 -> x0, local copies, waits for them, and re-layouts: 64.7 us -> none
    ppermute x4 -> x16, waiting for transfers between devices: 26.6 us -> 89.8 us  [the longest x4 66.9 us: cross(): return in_order(b_id, same, lax.ppermute(other, ('b', 'd', 'sc'), unlike))]
    all_to_all x15 -> x10, waiting for transfers between devices: 127 us -> 67.2 us  [exchange(): return lax.all_to_all(blocks, axes, split_axis=0, concat_axis=0, tiled=True)]
    all_gather x3 -> x2, waiting for transfers between devices: 12.8 us -> 35.7 us  [far_pair(): return lax.all_gather(pair, 'a', axis=0, tiled=False)]
    all_to_all x15 -> x10, starting transfers between devices: 70.8 us -> 48.2 us  [exchange(): return lax.all_to_all(blocks, axes, split_axis=0, concat_axis=0, tiled=True)]
    reduce_sum x21 -> x5, other arithmetic: 19.7 us -> 1.14 us  [the longest x1 0.61 us: body(): jnp.sum(squared)]
  transfers between devices with their start and end apart: 25 -> 30, of which waited for: 15 -> 16; matrix products, arithmetic and copies ran while one was open for 36% -> 11% of each run, Pallas kernels for 13% -> 22%
where the time goes in v3:
time: 572 us; the launch traced here: 561 us
  waiting for transfers between devices  193 us (34%)
  Pallas kernels  185 us (32%)
  starting transfers between devices  53.8 us (9%)
  local copies, waits for them, and re-layouts  41.4 us (7%)
  other arithmetic  36 us (6%)
  blocking collectives  27.5 us (5%)
  between operations  24.5 us (4%)
    pallas_call x14, Pallas kernels, call(): pl.pallas_call(ordered, grid_spec=pltpu.PrefetchScalarGridSpec(num_scalar...  185 us
    all_to_all x10, waiting for transfers between devices, exchange(): return lax.all_to_all(blocks, axes, split_axis=0, concat_axis=0, tiled=True)  67.2 us
    ppermute x4, waiting for transfers between devices, cross(): return in_order(b_id, same, lax.ppermute(other, ('b', 'd', 'sc'), unlike))  66.9 us
    all_to_all x10, starting transfers between devices, exchange(): return lax.all_to_all(blocks, axes, split_axis=0, concat_axis=0, tiled=True)  48.2 us
    all_gather x2, waiting for transfers between devices, far_pair(): return lax.all_gather(pair, 'a', axis=0, tiled=False)  35.7 us
    all_to_all x1, blocking collectives, exchange(): return lax.all_to_all(blocks, axes, split_axis=0, concat_axis=0, tiled=True)  27.5 us
  transfers between devices with their start and end apart: 30, of which 16 were waited for; matrix products, arithmetic and copies ran while one was open for 11% of the time, Pallas kernels for 22%

profile of v3, /device:TPU:2, one launch (start us, length us, event | category | flops | bytes accessed | tf_op | source)
XLA Modules:
  0.0 561.2 jit_solution(8638144787693353364)
XLA Ops:
  15.0 6.7 %all-to-all-start = ((bf16[32,24,768]{2,1,0:T(8,128)(2,1)}), bf16[32,24,768]{2,1,0:T(8,128)(2,1)}, u32[]{:S(2)}, u32[]{:S(2)}) async-start(bf16[32,24,768]{2,1,0:T(8,128)(2,1)} %bitcast.11), calls=%async_computation | async-start | bytes 2359296 | tf_op jit(solution)/shard_map/all_to_all | solution.py:626
  30.4 5.9 %collective-permute-done = bf16[1,528,768]{2,1,0:T(8,128)(2,1)S(1)} collective-permute-done((bf16[1,528,768]{2,1,0:T(8,128)(2,1)S(1)}, bf16[1,528,768]{2,1,0:T(8,128)(2,1)S(1)}, u32[]{:S(2)}, u32[]{:S(2)}) %collective-permute-start) | collective-permute-done | bytes 811040 | tf_op jit(solution)/shard_map/ppermute | solution.py:638
  37.8 22.3 %collective-permute-done.3 = bf16[2,96,2048]{2,1,0:T(8,128)(2,1)} collective-permute-done((bf16[2,96,2048]{2,1,0:T(8,128)(2,1)}, bf16[2,96,2048]{2,1,0:T(8,128)(2,1)}, u32[]{:S(2)}, u32[]{:S(2)}) %collective-permute-start.3) | collective-permute-done | bytes 786464 | tf_op jit(solution)/shard_map/ppermute | solution.py:691
  79.4 26.0 %attend_forward.1 = (bf16[2048,768]{1,0:T(8,128)(2,1)}, bf16[4,192,512]{2,1,0:T(8,128)(2,1)}, f32[192,2048]{1,0:T(8,128)}, f32[8,2048]{1,0:T(8,128)}, bf16[3,204...) custom-call(s32[4]{0:T(128)} %copy-done.26, ...), custom_call_target="tpu_custom_call" | custom-call | flops 29899999232 | bytes 14527492 | tf_op jit(solution)/shard_map/attend_forward/pallas_call | solution.py:302
  120.2 9.9 %mid.1 = (f32[512,768]{1,0:T(8,128)}, f32[512,768]{1,0:T(8,128)}, f32[512,16]{1,0:T(8,128)}, bf16[8,160,768]{2,1,0:T(8,128)(2,1)}, f32[1,1]{1,0:T(1,128)}) custom-call(bf16[4,192,512]{2,1,0:T(8,128)(2,1)} %copy-done.10, bf16[512,768]{1,0:T(8,128)(2,1)} %refs_3_.2, bf16[768,768]{1,0:T(8,128)(2,1)} %copy.244.refs_2_.refs_6_, ...), custom_call_target="tpu_custom_call" | custom-call | flops 11500000256 | bytes 7998468 | tf_op jit(solution)/shard_map/mid/pallas_call | solution.py:302
  130.8 5.8 %all-to-all-start.3 = ((bf16[8,160,768]{2,1,0:T(8,128)(2,1)}), bf16[8,160,768]{2,1,0:T(8,128)(2,1)}, u32[]{:S(2)}, u32[]{:S(2)}) async-start(bf16[8,160,768]{2,1,0:T(8,128)(2,1)} %get-tuple-element.71), calls=%async_computation.3 | async-start | bytes 3932160 | tf_op jit(solution)/shard_map/all_to_all | solution.py:626
  146.2 27.6 %collective-permute-done.6 = bf16[256,768]{1,0:T(8,128)(2,1)S(1)} collective-permute-done((bf16[256,768]{1,0:T(8,128)(2,1)S(1)}, bf16[256,768]{1,0:T(8,128)(2,1)S(1)}, u32[]{:S(2)}, u32[]{:S(2)}) %collective-permute-start.6) | collective-permute-done | bytes 393248 | tf_op jit(solution)/shard_map/ppermute | solution.py:691
  174.9 14.0 %expert_hidden.1 = (f32[1280,2048]{1,0:T(8,128)}, f32[1280,2048]{1,0:T(8,128)}, bf16[1280,2048]{1,0:T(8,128)(2,1)}, f32[1,1]{1,0:T(1,128)}) custom-call(s32[1]{0:T(128)} %bitcast.refs_0_, bf16[1280,768]{1,0:T(8,128)(2,1)} %bitcast.23.refs_1_, bf16[4,2,96,2048]{3,2,1,0:T(8,128)(2,1)} %bitcast.135, bf16[4,2,96,2048]{3,2,1,0:T(8,128)(2,1)} %collective-permute-done.4.refs_3_.refs_6_), custom_call_target="tpu_custom_call" | custom-call | flops 16099999744 | bytes 34471940 | tf_op jit(solution)/shard_map/expert_hidden/pallas_call | solution.py:302
  189.5 29.9 %all-gather.5.cloned.1.call-done = bf16[2,2,256,768]{3,2,1,0:T(8,128)(2,1)} async-done(((bf16[1,2,256,768]{3,2,1,0:T(8,128)(2,1)}), bf16[2,2,256,768]{3,2,1,0:T(8,128)(2,1)}) %all-gather.5.cloned.1.call-update) | async-done | bytes 1572880 | tf_op jit(solution)/shard_map/all_gather | solution.py:694
  225.5 8.4 %expert_result.1 = (bf16[1280,768]{1,0:T(8,128)(2,1)}, f32[1,1]{1,0:T(1,128)}) custom-call(s32[1]{0:T(128)} %bitcast.refs_0_, bf16[1280,2048]{1,0:T(8,128)(2,1)} %get-tuple-element.73.refs_1_, bf16[4,256,768]{2,1,0:T(8,128)(2,1)} %bitcast.143, bf16[4,256,768]{2,1,0:T(8,128)(2,1)} %copy-done.27), custom_call_target="tpu_custom_call" | custom-call | flops 9200000000 | bytes 10354692 | tf_op jit(solution)/shard_map/expert_result/pallas_call | solution.py:302
  243.4 21.2 %all-to-all-done.4.refs_0_ = bf16[8,160,768]{2,1,0:T(8,128)(2,1)S(1)} async-done(((bf16[8,160,768]{2,1,0:T(8,128)(2,1)}), bf16[8,160,768]{2,1,0:T(8,128)(2,1)S(1)}, u32[]{:S(2)}, u32[]{:S(2)}) %all-to-all-start.4) | async-done | bytes 1966112 | tf_op jit(solution)/shard_map/all_to_all | solution.py:626
  265.9 11.0 %loss.1 = (bf16[512,768]{1,0:T(8,128)(2,1)}, f32[512,768]{1,0:T(8,128)}, f32[512,8]{1,0:T(8,128)}, bf16[8,160,768]{2,1,0:T(8,128)(2,1)}, f32[1,768]{1,0:T(1,128)}, /*index=5*/f32[1,1]{1,0:T(1,128)}) custom-call(bf16[8,160,768]{2,1,0:T(8,128)(2,1)} %copy-done.5, s32[512,2]{1,0:T(8,128)} %copy-done.8, s32[8,512]{1,0:T(8,128)} %pad.42.clone.refs_6_.refs_2_, ...), custom_call_target="tpu_custom_call" | custom-call | flops 12650000384 | bytes 10308616 | tf_op jit(solution)/shard_map/loss/pallas_call | solution.py:302
  276.9 27.5 %all_to_all.55 = bf16[8,160,768]{2,1,0:T(8,128)(2,1)} all-to-all(bf16[8,160,768]{2,1,0:T(8,128)(2,1)} %get-tuple-element.81), channel_id=1, replica_groups=mesh['a'=2,'b'=2,'d'=2,'sx'=2,'sc'=2] {'b','d','sx'}, dimensions={0} | all-to-all | bytes 3932160 | tf_op jit(solution)/shard_map/all_to_all | solution.py:626
  304.4 8.3 %down_grad.1 = (bf16[4,256,768]{2,1,0:T(8,128)(2,1)}, bf16[4,256,768]{2,1,0:T(8,128)(2,1)}, f32[1,1]{1,0:T(1,128)}) custom-call(s32[1]{0:T(128)} %bitcast.refs_0_, bf16[1280,2048]{1,0:T(8,128)(2,1)} %get-tuple-element.73.refs_1_, bf16[1280,768]{1,0:T(8,128)(2,1)} %bitcast.138), custom_call_target="tpu_custom_call" | custom-call | flops 9200000000 | bytes 10354692 | tf_op jit(solution)/shard_map/down_grad/pallas_call | solution.py:302
  319.4 32.3 %expert_backward.1 = (bf16[4,2,96,2048]{3,2,1,0:T(8,128)(2,1)}, bf16[4,2,96,2048]{3,2,1,0:T(8,128)(2,1)}, bf16[1280,768]{1,0:T(8,128)(2,1)}, f32[1,1]{1,0:T(1,128)}) custom-call(s32[1]{0:T(128)} %bitcast.refs_0_, bf16[1280,768]{1,0:T(8,128)(2,1)} %bitcast.23.refs_1_, bf16[1280,768]{1,0:T(8,128)(2,1)} %bitcast.139, f32[1280,2048]{1,0:T(8,128)} %get-tuple-element.82.refs_3_, ...), custom_call_target="tpu_custom_call" | custom-call | flops 36800000000 | bytes 42598404 | tf_op jit(solution)/shard_map/expert_backward/pallas_call | solution.py:302
  351.9 5.9 %all-to-all-start.6 = ((bf16[8,160,768]{2,1,0:T(8,128)(2,1)}), bf16[8,160,768]{2,1,0:T(8,128)(2,1)}, u32[]{:S(2)}, u32[]{:S(2)}) async-start(bf16[8,160,768]{2,1,0:T(8,128)(2,1)} %bitcast.137), calls=%async_computation.6 | async-start | bytes 3932160 | tf_op jit(solution)/shard_map/all_to_all | solution.py:626
  359.1 13.5 %route.1 = (f32[512,768]{1,0:T(8,128)}, f32[768,16]{1,0:T(8,128)}, f32[768,16]{1,0:T(8,128)}, f32[1,1]{1,0:T(1,128)}) custom-call(f32[512,16]{1,0:T(8,128)} %get-tuple-element.77.refs_4_.refs_0_, s32[512,2]{1,0:T(8,128)} %copy-done.1, f32[512,8]{1,0:T(8,128)} %get-tuple-element.87.refs_2_, f32[512,768]{1,0:T(8,128)} %get-tuple-element.88.refs_3_.refs_4_, ...), custom_call_target="tpu_custom_call" | custom-call | flops 16099999744 | bytes 4919300 | tf_op jit(solution)/shard_map/route/pallas_call | solution.py:302
  379.9 17.1 %all-to-all-done.6.refs_0_ = bf16[8,160,768]{2,1,0:T(8,128)(2,1)} async-done(((bf16[8,160,768]{2,1,0:T(8,128)(2,1)}), bf16[8,160,768]{2,1,0:T(8,128)(2,1)}, u32[]{:S(2)}, u32[]{:S(2)}) %all-to-all-start.6) | async-done | bytes 1966112 | tf_op jit(solution)/shard_map/all_to_all | solution.py:626
  397.0 8.3 %join.1 = (f32[512,768]{1,0:T(8,128)}, bf16[512,768]{1,0:T(8,128)(2,1)}, bf16[4,192,512]{2,1,0:T(8,128)(2,1)}, f32[1,768]{1,0:T(1,128)}, f32[1,1]{1,0:T(1,128)}) custom-call(bf16[8,160,768]{2,1,0:T(8,128)(2,1)} %all-to-all-done.6.refs_0_, s32[512,2]{1,0:T(8,128)} %copy-done.8, f32[512,768]{1,0:T(8,128)} %get-tuple-element.89.refs_2_, ...), custom_call_target="tpu_custom_call" | custom-call | flops 9200000000 | bytes 11020292 | tf_op jit(solution)/shard_map/join/pallas_call | solution.py:302
  419.6 38.1 %attend_backward.1 = (f32[2,512,768]{2,1,0:T(8,128)}, bf16[2,512,768]{2,1,0:T(8,128)(2,1)}, bf16[768,640]{1,0:T(8,128)(2,1)}, f32[1,1]{1,0:T(1,128)}) custom-call(s32[4]{0:T(128)} %copy-done.26, bf16[4,192,512]{2,1,0:T(8,128)(2,1)} %copy-done.11, f32[192,2048]{1,0:T(8,128)} %get-tuple-element.93.refs_2_, f32[8,2048]{1,0:T(8,128)} %get-tuple-element.94.refs_3_, ...), custom_call_target="tpu_custom_call" | custom-call | flops 43699998720 | bytes 19439620 | tf_op jit(solution)/shard_map/attend_backward/pallas_call | solution.py:302
  473.0 6.4 %all-to-all-done.9 = bf16[8,4,24,768]{3,2,1,0:T(8,128)(2,1)S(1)} async-done(((bf16[8,4,24,768]{3,2,1,0:T(8,128)(2,1)}), bf16[8,4,24,768]{3,2,1,0:T(8,128)(2,1)S(1)}, u32[]{:S(2)}, u32[]{:S(2)}) %all-to-all-start.9) | async-done | bytes 1179680 | tf_op jit(solution)/shard_map/all_to_all | solution.py:626
  485.6 9.9 %collective-permute-done.11.refs_1_ = bf16[512,768]{1,0:T(8,128)(2,1)} collective-permute-done((bf16[512,768]{1,0:T(8,128)(2,1)}, bf16[512,768]{1,0:T(8,128)(2,1)}, u32[]{:S(2)}, u32[]{:S(2)}) %collective-permute-start.11) | collective-permute-done | bytes 786464 | tf_op jit(solution)/shard_map/ppermute | solution.py:1063
  518.6 9.3 %all-to-all-done.10 = bf16[4,24,3200]{2,1,0:T(8,128)(2,1)S(1)} async-done(((bf16[4,24,3200]{2,1,0:T(8,128)(2,1)}), bf16[4,24,3200]{2,1,0:T(8,128)(2,1)S(1)}, u32[]{:S(2)}, u32[]{:S(2)}) %all-to-all-start.10) | async-done | bytes 614432 | tf_op jit(solution)/shard_map/all_to_all | solution.py:626
  534.1 17.0 %collective-permute-done.13 = bf16[2,96,2048]{2,1,0:T(8,128)(2,1)S(1)} collective-permute-done((bf16[2,96,2048]{2,1,0:T(8,128)(2,1)}, bf16[2,96,2048]{2,1,0:T(8,128)(2,1)S(1)}, u32[]{:S(2)}, u32[]{:S(2)}) %collective-permute-start.13) | collective-permute-done | bytes 786464 | tf_op jit(solution)/shard_map/ppermute | solution.py:691
  (237 shorter events, 154.2 us)
Async XLA Ops:
  9.2 27.1 %collective-permute-start = (bf16[1,528,768]{2,1,0:T(8,128)(2,1)S(1)}, bf16[1,528,768]{2,1,0:T(8,128)(2,1)S(1)}, u32[]{:S(2)}, u32[]{:S(2)}) collective-permute-start(bf16[1,528,768]{2,1,0:T(8,128)(2,1)S(1)} %fusion.4), channel_id=1, source_target_pairs={{0,2},{1,3},{2,0},{3,1},{4,6},{5,7},{6,4},{7,5},{8,10},{9,11},{10,... | collective-permute-start | bytes 2433032 | tf_op jit(solution)/shard_map/ppermute | solution.py:638
  15.0 48.0 %all-to-all-start = ((bf16[32,24,768]{2,1,0:T(8,128)(2,1)}), bf16[32,24,768]{2,1,0:T(8,128)(2,1)}, u32[]{:S(2)}, u32[]{:S(2)}) async-start(bf16[32,24,768]{2,1,0:T(8,128)(2,1)} %bitcast.11), calls=%async_computation | async-start | bytes 2359296 | tf_op jit(solution)/shard_map/all_to_all | solution.py:626
  21.7 120.6 %all-gather.3.cloned.1.call-start = ((), (), s32[]{:S(2)}) async-start(), calls=%async_computation.13 | async-start | bytes 4718592 | tf_op jit(solution)/shard_map/all_gather | solution.py:694
  25.7 34.4 %collective-permute-start.3 = (bf16[2,96,2048]{2,1,0:T(8,128)(2,1)}, bf16[2,96,2048]{2,1,0:T(8,128)(2,1)}, u32[]{:S(2)}, u32[]{:S(2)}) collective-permute-start(bf16[2,96,2048]{2,1,0:T(8,128)(2,1)} %pad_maximum_fusion.3), channel_id=1, source_target_pairs={{0,8},{1,12},{4,9},{5,13},{8,0},{9,4},{12,1},{13,5},{2,10},{3,14},... | collective-permute-start | bytes 2359304 | tf_op jit(solution)/shard_map/ppermute | solution.py:691
  37.7 36.2 %collective-permute-start.1 = (bf16[2,528,768]{2,1,0:T(8,128)(2,1)}, bf16[2,528,768]{2,1,0:T(8,128)(2,1)}, u32[]{:S(2)}, u32[]{:S(2)}) collective-permute-start(bf16[2,528,768]{2,1,0:T(8,128)(2,1)} %pad_maximum_fusion.1), channel_id=1, source_target_pairs={{0,1},{1,0},{2,3},{3,2},{4,5},{5,4},{6,7},{7,6},{8,9},{9,8},{10,11... | collective-permute-start | bytes 4866056 | tf_op jit(solution)/shard_map/ppermute | solution.py:638
  68.3 37.1 %all-to-all-start.2 = ((bf16[8,768,128]{1,2,0:T(8,128)(2,1)}), bf16[8,768,128]{1,2,0:T(8,128)(2,1)S(1)}, u32[]{:S(2)}, u32[]{:S(2)}) async-start(bf16[8,768,128]{1,2,0:T(8,128)(2,1)} %broadcast_in_dim.68), calls=%async_computation.2 | async-start | bytes 3145728 | tf_op jit(solution)/shard_map/all_to_all | solution.py:626
  105.5 13.9 %all-to-all-start.1 = ((bf16[4,192,512]{2,1,0:T(8,128)(2,1)}), bf16[4,192,512]{2,1,0:T(8,128)(2,1)S(1)}, u32[]{:S(2)}, u32[]{:S(2)}) async-start(bf16[4,192,512]{2,1,0:T(8,128)(2,1)} %get-tuple-element.68), calls=%async_computation.1 | async-start | bytes 1572864 | tf_op jit(solution)/shard_map/all_to_all | solution.py:626
  130.8 44.1 %all-to-all-start.3 = ((bf16[8,160,768]{2,1,0:T(8,128)(2,1)}), bf16[8,160,768]{2,1,0:T(8,128)(2,1)}, u32[]{:S(2)}, u32[]{:S(2)}) async-start(bf16[8,160,768]{2,1,0:T(8,128)(2,1)} %get-tuple-element.71), calls=%async_computation.3 | async-start | bytes 3932160 | tf_op jit(solution)/shard_map/all_to_all | solution.py:626
  136.6 82.8 %all-gather.5.cloned.1.call-start = ((), (), s32[]{:S(2)}) async-start(), calls=%async_computation.14 | async-start | bytes 2359296 | tf_op jit(solution)/shard_map/all_gather | solution.py:694
  144.5 30.3 %collective-permute-start.4 = (bf16[4,2,96,2048]{3,2,1,0:T(8,128)(2,1)S(1)}, bf16[4,2,96,2048]{3,2,1,0:T(8,128)(2,1)}, u32[]{:S(2)}, u32[]{:S(2)}) collective-permute-start(bf16[4,2,96,2048]{3,2,1,0:T(8,128)(2,1)S(1)} %bitcast.134), channel_id=1, source_target_pairs={{0,1},{1,0},{2,3},{3,2},{4,5},{5,4},{6,7},{7,6},{8,9},{9,8},{10,11... | collective-permute-start | bytes 9437192 | tf_op jit(solution)/shard_map/ppermute | solution.py:698
  145.4 28.5 %collective-permute-start.6 = (bf16[256,768]{1,0:T(8,128)(2,1)S(1)}, bf16[256,768]{1,0:T(8,128)(2,1)S(1)}, u32[]{:S(2)}, u32[]{:S(2)}) collective-permute-start(bf16[256,768]{1,0:T(8,128)(2,1)S(1)} %get-tuple-element.223), channel_id=1, source_target_pairs={{0,8},{1,12},{4,9},{5,13},{8,0},{9,4},{12,1},{13,5},{2,10},{3,14},... | collective-permute-start | bytes 1179656 | tf_op jit(solution)/shard_map/ppermute | solution.py:691
  234.0 30.6 %all-to-all-start.4 = ((bf16[8,160,768]{2,1,0:T(8,128)(2,1)}), bf16[8,160,768]{2,1,0:T(8,128)(2,1)S(1)}, u32[]{:S(2)}, u32[]{:S(2)}) async-start(bf16[8,160,768]{2,1,0:T(8,128)(2,1)} %bitcast.140), calls=%async_computation.4 | async-start | bytes 3932160 | tf_op jit(solution)/shard_map/all_to_all | solution.py:626
  351.7 23.3 %collective-permute-start.9 = (bf16[4,2,96,2048]{3,2,1,0:T(8,128)(2,1)}, bf16[4,2,96,2048]{3,2,1,0:T(8,128)(2,1)}, u32[]{:S(2)}, u32[]{:S(2)}) collective-permute-start(bf16[4,2,96,2048]{3,2,1,0:T(8,128)(2,1)} %get-tuple-element.91), channel_id=1, source_target_pairs={{0,1},{1,0},{2,3},{3,2},{4,5},{5,4},{6,7},{7,6},{8,9},{9,8},{10,11... | collective-permute-start | bytes 9437192 | tf_op jit(solution)/shard_map/ppermute | solution.py:701
  351.9 45.1 %all-to-all-start.6 = ((bf16[8,160,768]{2,1,0:T(8,128)(2,1)}), bf16[8,160,768]{2,1,0:T(8,128)(2,1)}, u32[]{:S(2)}, u32[]{:S(2)}) async-start(bf16[8,160,768]{2,1,0:T(8,128)(2,1)} %bitcast.137), calls=%async_computation.6 | async-start | bytes 3932160 | tf_op jit(solution)/shard_map/all_to_all | solution.py:626
  357.8 107.0 %reduce-scatter.5.cloned.1.call-start = ((), (), s32[]{:S(2)}) async-start(), calls=%async_computation.16 | async-start | bytes 2359296 | tf_op jit(solution)/shard_map/reduce_scatter | solution.py:705
  358.5 154.3 %reduce-scatter.3.cloned.1.call-start = ((), (), s32[]{:S(2)}) async-start(), calls=%async_computation.15 | async-start | bytes 4718592 | tf_op jit(solution)/shard_map/reduce_scatter | solution.py:705
  458.9 20.5 %all-to-all-start.9 = ((bf16[8,4,24,768]{3,2,1,0:T(8,128)(2,1)}), bf16[8,4,24,768]{3,2,1,0:T(8,128)(2,1)S(1)}, u32[]{:S(2)}, u32[]{:S(2)}) async-start(bf16[8,4,24,768]{3,2,1,0:T(8,128)(2,1)} %bitcast.119), calls=%async_computation.9 | async-start | bytes 2359296 | tf_op jit(solution)/shard_map/all_to_all | solution.py:626
  466.8 18.6 %collective-permute-start.14 = (bf16[256,768]{1,0:T(8,128)(2,1)S(1)}, bf16[256,768]{1,0:T(8,128)(2,1)S(1)}, u32[]{:S(2)}, u32[]{:S(2)}) collective-permute-start(bf16[256,768]{1,0:T(8,128)(2,1)S(1)} %get-tuple-element.220), channel_id=1, source_target_pairs={{1,4},{4,1},{9,12},{12,9},{3,6},{6,3},{11,14},{14,11},{17,20},{20,... | collective-permute-start | bytes 1179656 | tf_op jit(solution)/shard_map/ppermute | solution.py:690
  471.7 23.9 %collective-permute-start.11 = (bf16[512,768]{1,0:T(8,128)(2,1)}, bf16[512,768]{1,0:T(8,128)(2,1)}, u32[]{:S(2)}, u32[]{:S(2)}) collective-permute-start(bf16[512,768]{1,0:T(8,128)(2,1)} %get-tuple-element.112), channel_id=1, source_target_pairs={{0,2},{1,3},{2,0},{3,1},{4,6},{5,7},{6,4},{7,5},{8,10},{9,11},{10,... | collective-permute-start | bytes 2359304 | tf_op jit(solution)/shard_map/ppermute | solution.py:1063
  479.4 27.0 %all-to-all-start.8 = ((bf16[8,4,24,640]{3,2,1,0:T(8,128)(2,1)}), bf16[8,4,24,640]{3,2,1,0:T(8,128)(2,1)S(1)}, u32[]{:S(2)}, u32[]{:S(2)}) async-start(bf16[8,4,24,640]{3,2,1,0:T(8,128)(2,1)} %bitcast.120), calls=%async_computation.8 | async-start | bytes 1966080 | tf_op jit(solution)/shard_map/all_to_all | solution.py:626
  484.9 31.1 %collective-permute-start.15 = (bf16[256,768]{1,0:T(8,128)(2,1)}, bf16[256,768]{1,0:T(8,128)(2,1)}, u32[]{:S(2)}, u32[]{:S(2)}) collective-permute-start(bf16[256,768]{1,0:T(8,128)(2,1)} %get-tuple-element.221), channel_id=1, source_target_pairs={{0,8},{1,12},{4,9},{5,13},{8,0},{9,4},{12,1},{13,5},{2,10},{3,14},... | collective-permute-start | bytes 1179656 | tf_op jit(solution)/shard_map/ppermute | solution.py:691
  509.2 18.6 %all-to-all-start.10 = ((bf16[4,24,3200]{2,1,0:T(8,128)(2,1)}), bf16[4,24,3200]{2,1,0:T(8,128)(2,1)S(1)}, u32[]{:S(2)}, u32[]{:S(2)}) async-start(bf16[4,24,3200]{2,1,0:T(8,128)(2,1)} %pad.44), calls=%async_computation.10 | async-start | bytes 1228800 | tf_op jit(solution)/shard_map/all_to_all | solution.py:626
  515.3 18.7 %collective-permute-start.12 = (bf16[2,96,2048]{2,1,0:T(8,128)(2,1)S(1)}, bf16[2,96,2048]{2,1,0:T(8,128)(2,1)S(1)}, u32[]{:S(2)}, u32[]{:S(2)}) collective-permute-start(bf16[2,96,2048]{2,1,0:T(8,128)(2,1)S(1)} %get-tuple-element.218), channel_id=1, source_target_pairs={{1,4},{4,1},{9,12},{12,9},{3,6},{6,3},{11,14},{14,11},{17,20},{20,... | collective-permute-start | bytes 2359304 | tf_op jit(solution)/shard_map/ppermute | solution.py:690
  530.7 20.4 %collective-permute-start.13 = (bf16[2,96,2048]{2,1,0:T(8,128)(2,1)}, bf16[2,96,2048]{2,1,0:T(8,128)(2,1)S(1)}, u32[]{:S(2)}, u32[]{:S(2)}) collective-permute-start(bf16[2,96,2048]{2,1,0:T(8,128)(2,1)} %get-tuple-element.219), channel_id=1, source_target_pairs={{0,8},{1,12},{4,9},{5,13},{8,0},{9,4},{12,1},{13,5},{2,10},{3,14},... | collective-permute-start | bytes 2359304 | tf_op jit(solution)/shard_map/ppermute | solution.py:691
  (34 other events, 310.1 us)
Sparse Core Ops, SparseCore 0:
  63.1 79.1 all-gather.2
  175.0 44.3 all-gather.4
  360.8 43.3 reduce-scatter.4
  406.4 76.9 reduce-scatter.2

commit v4 on v3

--- a/solution.py
+++ b/solution.py
@@ -1,3 +1,5 @@
+import functools
+
 import jax
 import jax.numpy as jnp
 import numpy as np
@@ -53,14 +55,24 @@
 def nn(a,b): return jnp.dot(a,b,preferred_element_type=f32)
 def tn(a,b): return lax.dot_general(a,b,(((0,),(0,)),((),())),preferred_element_type=f32)
 
-def fwd_kernel(tbl, held, gain, win, winT, start, normed, att, oT, lse, qn, kn, vn, qT, kT, kbuf, vbuf):
+def fwd_kernel(tbl, held, held_far, gain, win, winT, start, inputs, normed, att, oT, lse, qn, kn, vn, qT, kT, kbuf, vbuf):
     i=pl.program_id(0)
     wide=win.shape[1]//3
     heads=wide//HEAD
     per=held.shape[1]//BLK
     t=tbl[i//per]
     off=pl.multiple_of((i%per)*BLK,BLK)
-    x=held[t,pl.ds(off,BLK),:].astype(f32)
+    half = held.shape[0]
+
+    @pl.when(t < half)
+    def _():
+        inputs[...] = held[t, pl.ds(off, BLK), :]
+
+    @pl.when(t >= half)
+    def _():
+        inputs[...] = held_far[t - half, pl.ds(off, BLK), :]
+
+    x = inputs[...].astype(f32)
     scale=lax.rsqrt(jnp.mean(x*x,-1,keepdims=True)+epsilon)
     nb=(x*scale*gain[...]).astype(bf16)
     normed[...]=nb
@@ -114,7 +126,7 @@
     lse[heads:]=jnp.zeros((lse.shape[0]-heads,BLK),f32)
 
 def attend_forward(table, held, gain, win, win_t, start, tokens, after):
-    feat = held.shape[2]
+    feat = held[0].shape[2]
     length = start.shape[1]
     wide = win.shape[1] // 3
     heads = wide // HEAD
@@ -130,13 +142,15 @@
         (nb,),
         [
             (table,) + whole,
-            (held,) + whole,
+            (held[0],) + whole,
+            (held[1],) + whole,
             (gain,) + whole,
             (win,) + whole,
             (win_t,) + whole,
             (start, (1, BLK), by_col),
         ],
         [
+            (sds((length, feat), bf16), (BLK, feat), by_row),
             (sds((length, feat), bf16), (BLK, feat), by_row),
             (sds((length // tokens, wide, tokens), bf16), (1, wide, BLK), lambda i, *_: (i // per, 0, i % per)),
             (sds((wide, length), f32), (wide, BLK), by_col),
@@ -206,7 +220,7 @@
         [(dq[j] * HEAD**-0.5).T] + [a[0] for a in accs] + [a[1] for a in accs], 1
     ).astype(bf16)
     back = nt(gp, win[...])
-    x = held[0].astype(f32)
+    x = held[...].astype(f32)
     scale = lax.rsqrt(jnp.mean(x * x, -1, keepdims=True) + epsilon)
     gain_acc[0:1] += jnp.sum(back * (x * scale), 0, keepdims=True)
     gin_acc[...] += tn(normed[...], gp)
@@ -244,13 +258,10 @@
     half = n_seq // 2
     whole = (None, None)
 
-    def by_table(i, tbl):
-        return (tbl[i // per], i % per, 0)
-
     return call(
         bwd_kernel,
         "attend_backward",
-        38,
+        7600,
         (nb,),
         [
             (table,) + whole,
@@ -263,7 +274,7 @@
             (q_t,) + whole,
             (k_t, (wide, BLK), by_col),
             (start,) + whole,
-            (held, (1, BLK, feat), by_table),
+            (held, (BLK, feat), by_row),
             (normed, (BLK, feat), by_row),
             (win,) + whole,
             (small,) + whole,
@@ -312,7 +323,7 @@
         out_shape=[s for s, _, _ in outs],
         compiler_params=pltpu.CompilerParams(vmem_limit_bytes=limit << 20),
         cost_estimate=pl.CostEstimate(
-            flops=cost * 1150000000,
+            flops=int(cost * 5750000),
             bytes_accessed=sum(v.size * v.dtype.itemsize for v, _, _ in ins[prefetch:] + outs),
             transcendentals=0,
         ),
@@ -547,30 +558,82 @@
         out[s * wide : (s + 1) * wide] = nn(att[s], branch[...]).astype(bf16)
 
 
-def whole_tile(me, own, other, tile):
-    tile[:, pl.ds(me[0], 1)] = own[:, None]
-    tile[:, pl.ds(1 - me[0], 1)] = other[:, None]
+def whole_tile(me, parts, tile):
+    far, core = me[0], me[1]
+    for part, f, c in zip(parts, (far, 1 - far, far, 1 - far), (core, core, 1 - core, 1 - core)):
+        tile[pl.ds(f, 1), :, pl.ds(c, 1)] = part[None, :, None]
     return tile[...].reshape(-1, tile.shape[-1])
+
+
+def pick_kernel(index, *refs):
+    shards, same, other = refs[:-2], refs[-2], refs[-1]
+    for k, shard in enumerate(shards):
+        same[k] = shard[index[0]]
+        other[k] = shard[1 - index[0]]
+
+
+def total_kernel(n_small, parts, gin, gout, router, mix, small, vectors):
+    total = jnp.sum(parts[...].astype(f32), 0)
+    features = gout.shape[1]
+    wide = HEAD * (features // HEAD // 4)
+    for s in range(features // wide):
+        for k in range(3):
+            at = (3 * s + k) * wide
+            gin[:, k * features + s * wide : k * features + (s + 1) * wide] = total[:, at : at + wide]
+    gout[...] = total[:, 3 * features : 4 * features]
+    tail = total[:, 4 * features :]
+    both = tail[:, :n_small] + tail[:, n_small : 2 * n_small]
+    n_pad = small.shape[0]
+    unit = lax.broadcasted_iota(jnp.int32, (n_pad, tail.shape[1]), 0)
+    unit = (unit == lax.broadcasted_iota(jnp.int32, unit.shape, 1)).astype(f32)
+    wide_both = tail + jnp.concatenate([tail[:, n_small:], tail[:, :n_small]], 1)
+    small[...] = exact_dot(unit, wide_both, ((1,), (1,)))
+    vectors[...] = small[18:20]
+    router[...] = both[:, 2 : 2 + ROUTES]
+    mix[...] = both[:, 2 + ROUTES : 6 + ROUTES]
+
+
+def owner_kernel(which, part, alike, unlike, gate, up):
+    mine = part[which[0]]
+    first = jnp.where(which[1] == 1, mine, alike[...])
+    for k, out in enumerate((gate, up)):
+        out[which[0]] = first[k].astype(f32)
+        out[1 - which[0]] = unlike[k].astype(f32)
+
+
+def cross_kernel(which, same, alike, unlike, out):
+    @pl.when(which[1] == 1)
+    def _():
+        out[pl.ds(which[0], 1)] = same[...][None]
+
+    @pl.when(which[1] != 1)
+    def _():
+        out[pl.ds(which[0], 1)] = alike[...][None]
+
+    out[pl.ds(1 - which[0], 1)] = unlike[...][None]
 
 
 def split_tile(me, values, tile):
     tile[...] = values.reshape(tile.shape)
-    return tile[:, pl.ds(me[0], 1)][:, 0], tile[:, pl.ds(1 - me[0], 1)][:, 0]
-
-
-def expert_hidden_kernel(me, rows, own, other, gate_part, up_part, hidden, gate, up):
+    return tile[:, pl.ds(me[1], 1)][:, 0], tile[:, pl.ds(1 - me[1], 1)][:, 0]
+
+
+def expert_hidden_kernel(
+    me, rows, near, far, near_other, far_other, gate_part, up_part, hidden, gate, up
+):
     x = rows[...]
-    g = nn(x, whole_tile(me, own[:, 0], other[:, 0], gate))
-    u = nn(x, whole_tile(me, own[:, 1], other[:, 1], up))
+    parts = (near, far, near_other, far_other)
+    g = nn(x, whole_tile(me, [p[:, 0] for p in parts], gate))
+    u = nn(x, whole_tile(me, [p[:, 1] for p in parts], up))
     gate_part[...] = g
     up_part[...] = u
     hidden[...] = (g / (1.0 + jnp.exp(-g)) * u).astype(bf16)
 
 
-def expert_result_kernel(me, hidden, own, other, result, down):
+def expert_result_kernel(me, hidden, near, far, near_other, far_other, result, down):
     @pl.when(pl.program_id(0) == 0)
     def _():
-        whole_tile(me, own[...], other[...], down)
+        whole_tile(me, [p[...] for p in (near, far, near_other, far_other)], down)
 
     result[...] = nn(hidden[...], down[...].reshape(-1, down.shape[-1])).astype(bf16)
 
@@ -580,11 +643,18 @@
 
 
 def expert_backward_kernel(
-    me, rows, grad, gate_part, up_part, own, other, down_own, down_other,
+    me, rows, grad, gate_part, up_part, near, far, near_other, far_other,
+    down_near, down_far, down_near_other, down_far_other,
     d_own, d_other, result, gate, up, down, parts, acc,
 ):
     f = pl.program_id(0)
-    gh = nt(grad[...], whole_tile(me, down_own[...], down_other[...], down))
+
+    @pl.when(f == 0)
+    def _():
+        pieces = (down_near, down_far, down_near_other, down_far_other)
+        whole_tile(me, [p[...] for p in pieces], down)
+
+    gh = nt(grad[...], down[f // 2, f % 2].reshape(-1, down.shape[-1]))
     g = gate_part[...]
     u = up_part[...]
     sig = 1.0 / (1.0 + jnp.exp(-g))
@@ -592,8 +662,9 @@
     du = (gh * (g * sig)).astype(bf16)
     for k, d in enumerate((dg, du)):
         d_own[:, k], d_other[:, k] = split_tile(me, tn(rows[...], d).astype(bf16), parts)
-    part = nt(dg, whole_tile(me, own[:, 0], other[:, 0], gate))
-    part = part + nt(du, whole_tile(me, own[:, 1], other[:, 1], up))
+    weights = (near, far, near_other, far_other)
+    part = nt(dg, whole_tile(me, [p[:, 0] for p in weights], gate))
+    part = part + nt(du, whole_tile(me, [p[:, 1] for p in weights], up))
 
     @pl.when(f == 0)
     def _():
@@ -633,10 +704,11 @@
 def gather_seq(block, size):
     held = block[None]
     step = size // 2
-    while step:
+    while step > 1:
         pairs = [(i, i ^ step) for i in range(size)]
         held = jnp.concatenate([held, lax.ppermute(held, SEQ, pairs)], 0)
         step //= 2
+    held = (held, lax.ppermute(held, SEQ, [(i, i ^ 1) for i in range(size)]))
     order = [0]
     step = size // 2
     while step:
@@ -672,7 +744,7 @@
     seq_id = lax.axis_index(SEQ)
 
     a_id, b_id, d_id, c_id = (lax.axis_index(x) for x in ("a", "b", "d", "sc"))
-    me = c_id.reshape(1)
+    me = jnp.stack([a_id * (n_far == 2), c_id])
     swap = [(0, 1), (1, 0)]
     cross = [(1, 2), (2, 1)]
 
@@ -681,49 +753,123 @@
 
     def in_order(index, mine, given):
         return jnp.where(index == 0, jnp.stack([mine, given]), jnp.stack([given, mine]))
+
+    which = jnp.stack([b_id, (c_id == d_id).astype(jnp.int32)])
 
     place = [(b, d, c) for b in range(2) for d in range(2) for c in range(2)]
     alike = [(4 * b + 2 * d + c, 4 * b + 2 * c + d) for b, d, c in place if d != c]
     unlike = [(4 * b + 2 * d + c, 4 * (1 - b) + 2 * c + d) for b, d, c in place]
 
-    def cross(same, other):
+    def crossed(same, other):
         same = jnp.where(c_id == d_id, same, lax.ppermute(same, ("b", "d", "sc"), alike))
         return in_order(b_id, same, lax.ppermute(other, ("b", "d", "sc"), unlike))
 
+    def cross(same, other, after):
+        given = [lax.ppermute(same, ("b", "d", "sc"), alike)]
+        given.append(lax.ppermute(other, ("b", "d", "sc"), unlike))
+        count, height, width = same.shape
+        quarter = width // (4 if width % 512 == 0 else 2)
+        block = ((count, height, quarter), by_last)
+        pair, _ = call(
+            cross_kernel,
+            "cross",
+            2,
+            (width // quarter,),
+            [(which, None, None)] + [(x,) + block for x in [same] + given],
+            [(sds((2,) + same.shape, bf16), (2,) + block[0], lambda i, *_: (0, 0, 0, i))],
+            prefetch=1,
+            after=after,
+        )
+        return pair
+
     def far_pair(pair):
         return lax.all_gather(pair, "a", axis=0, tiled=False)
 
-    def both_cores(far, done):
-        own = far.reshape((n_out,) + far.shape[2:]) + done[0, 0].astype(bf16)
-        return own, lax.ppermute(own, "sc", swap)
-
-    def core_sum(own, other):
+    def far_parts(far, done):
+        if n_far == 2:
+            far = item(far, 1 - a_id)
+        far = far + done[0, 0].astype(bf16)
+        return far, lax.ppermute(far, "sc", swap)
+
+    def core_sum(own, other, done=None):
         total = own.astype(f32) + lax.ppermute(other, "sc", swap).astype(f32)
+        if done is not None:
+            total = total + done[0, 0]
         return total.astype(bf16).reshape((n_far, 2) + own.shape[1:])
 
     def far_sum(part):
         return lax.psum_scatter(part, "a", scatter_dimension=0, tiled=False)
 
     def to_owner(part):
-        return cross(item(part, b_id), item(part, 1 - b_id)).astype(f32)
-
-    slice_rows = expert_gate.shape[1]
-    odd_rows = slice_rows % 16 != 0
-
-    def to_order(own, other):
-        pair = in_order(c_id, own, other)
-        return pair.transpose(2, 1, 0, 3, 4).reshape(2, features, -1)
-
-    def from_order(both, count):
-        pair = both.reshape(2, count, 2, -1, both.shape[2]).transpose(2, 1, 0, 3, 4)
+        return crossed(item(part, b_id), item(part, 1 - b_id)).astype(f32)
+
+    def regroup(near, far, near_other, far_other):
+        if n_far == 2:
+            return near, far, near_other, far_other
+        pair = in_order(c_id, far, far_other).transpose(3, 1, 2, 0, 4, 5)
+        pair = pair.reshape(pair.shape[:1] + (2, 2, 2, -1) + pair.shape[5:])
+        pair = pair.transpose(1, 3, 2, 0, 4, 5)
+        return tuple(item(pair[f], c) for c in (c_id, 1 - c_id) for f in range(2))
+
+    def owner_slices(own, other):
+        if n_far == 2:
+            return own, other
+        pair = in_order(c_id, own, other).transpose(2, 1, 0, 3, 4)
+        pair = pair.reshape(pair.shape[:1] + (n_out, 2, -1) + pair.shape[4:])
+        pair = pair.transpose(2, 1, 0, 3, 4)
         return item(pair, c_id), item(pair, 1 - c_id)
 
-    def gate_and_up(index):
-        return jnp.stack([item(expert_gate, index), item(expert_up, index)])
-
-    in_pair = cross(gate_and_up(b_id), gate_and_up(1 - b_id))
-    down_pair = cross(item(expert_down, b_id), item(expert_down, 1 - b_id))
-    own_cols = input_proj.reshape(rows_here, 3, n_seq, wide)
+    def pick(shards, after=()):
+        _, height, width = shards[0].shape
+        quarter = width // (4 if width % 512 == 0 else 2)
+        block = ((2, height, quarter), by_last)
+        out_block = ((len(shards), height, quarter), by_last)
+        return call(
+            pick_kernel,
+            "pick",
+            3,
+            (width // quarter,),
+            [(b_id.reshape(1), None, None)] + [(x,) + block for x in shards],
+            [(sds((len(shards), height, width), bf16),) + out_block] * 2,
+            prefetch=1,
+            after=after,
+        )
+
+    same_in, other_in, picked = pick([expert_gate, expert_up])
+    seg_row = jnp.pad(segments.astype(bf16), (0, features * 2 - tokens_here)).reshape(2, features)
+    with_seg = jnp.concatenate(
+        [block_input, jnp.pad(seg_row, ((0, 14), (0, 0)))], 0
+    )
+    held, order = gather_seq(with_seg, n_seq)
+    where = [order.index(j) for j in range(n_seq)]
+    chosen = jnp.array(where, jnp.int32)[jnp.arange(n_seq) ^ seq_id]
+    length = n_seq * tokens_here
+    seg_rows = [h[:, tokens_here : tokens_here + 2] for h in held]
+    seq_segments = (
+        jnp.concatenate(seg_rows, 0)
+        .reshape(n_seq, 2 * features)[:, :tokens_here][chosen]
+        .reshape(1, -1)
+    )
+    positions = jnp.arange(length, dtype=jnp.int32)[None]
+    fresh = seq_segments != jnp.pad(seq_segments[:, :-1], ((0, 0), (1, 0)), constant_values=-1)
+    start = lax.cummax(jnp.where(fresh, positions, 0), axis=1)
+
+    flat_routes = routes.reshape(-1)
+    onehot_e = (flat_routes[:, None] == jnp.arange(EXPERTS, dtype=jnp.int32)[None, :]).astype(
+        jnp.int32
+    )
+    slot_rank = jnp.sum((jnp.cumsum(onehot_e, 0) - onehot_e) * onehot_e, -1)
+    host = (flat_routes % 2) * 4 + flat_routes // 2 % 2 * 2 + flat_routes // 4
+    slot_dest = jnp.where(flat_routes < EXPERTS, host * CAP + slot_rank, EXPERTS * CAP)
+    slot_dest = slot_dest.reshape(tokens_here, 2)
+    slot_row = jnp.pad(slot_dest.T, ((0, 6), (0, 0)))
+
+    in_pair = cross(same_in, other_in, [held[1], start, slot_row])
+    in_far = far_pair(in_pair)
+    in_other = lax.ppermute(in_pair, "sc", swap)
+    same_down, other_down, _ = pick([expert_down], [in_pair])
+
+    own_cols = (input_proj + picked[0, 0].astype(bf16)).reshape(rows_here, 3, n_seq, wide)
     own_cols = own_cols.transpose(0, 2, 1, 3).reshape(rows_here, -1)
     count_here = jnp.sum(valid_mask)
     count_cols = jnp.stack([count_here // 32, count_here % 32]).astype(bf16)
@@ -774,45 +920,20 @@
             (sds((features, got.shape[1] - inner), bf16), None, None),
         ],
     )
-    in_far = far_pair(in_pair)
-    down_far = far_pair(down_pair + prepared[0, 0].astype(bf16))
     gain_first, gain_mid, vectors_f = gains[0:1], gains[1:2], gains[2:4]
     out_part = jnp.broadcast_to(out_cols[None], (n_plane,) + out_cols.shape)
     full_out = exchange(out_part, PLANE)[:, :, :piece].transpose(1, 0, 2)
     full_out = full_out.reshape(features, features)
 
-    seg_row = jnp.pad(segments.astype(bf16), (0, features * 2 - tokens_here)).reshape(2, features)
-    with_seg = jnp.concatenate(
-        [block_input, jnp.pad(seg_row, ((0, 14), (0, 0)))], 0
-    )
-    held, order = gather_seq(with_seg, n_seq)
-    where = [order.index(j) for j in range(n_seq)]
-    chosen = jnp.array(where, jnp.int32)[jnp.arange(n_seq) ^ seq_id]
-    length = n_seq * tokens_here
-    seq_segments = (
-        held[:, tokens_here : tokens_here + 2]
-        .reshape(n_seq, 2 * features)[:, :tokens_here][chosen]
-        .reshape(1, -1)
-    )
-    positions = jnp.arange(length, dtype=jnp.int32)[None]
-    fresh = seq_segments != jnp.pad(seq_segments[:, :-1], ((0, 0), (1, 0)), constant_values=-1)
-    start = lax.cummax(jnp.where(fresh, positions, 0), axis=1)
-
-    normed_first, attended, attended_t, log_totals, *heads_saved, forward_done = attend_forward(
+    seq_inputs, normed_first, attended, attended_t, log_totals, *heads_saved, forward_done = attend_forward(
         chosen, held, gain_first, own_in, own_in_t, start, tokens_here,
-        [],
+        [in_other],
     )
     attended_tok = exchange(attended, SEQ)
 
-    flat_routes = routes.reshape(-1)
-    onehot_e = (flat_routes[:, None] == jnp.arange(EXPERTS, dtype=jnp.int32)[None, :]).astype(
-        jnp.int32
-    )
-    slot_rank = jnp.sum((jnp.cumsum(onehot_e, 0) - onehot_e) * onehot_e, -1)
-    host = (flat_routes % 2) * 4 + flat_routes // 2 % 2 * 2 + flat_routes // 4
-    slot_dest = jnp.where(flat_routes < EXPERTS, host * CAP + slot_rank, EXPERTS * CAP)
-    slot_dest = slot_dest.reshape(tokens_here, 2)
-    slot_row = jnp.pad(slot_dest.T, ((0, 6), (0, 0)))
+    down_pair = cross(same_down, other_down, [normed_first])
+    down_far = far_pair(down_pair)
+    down_other = lax.ppermute(down_pair, "sc", swap)
 
     whole = (None, None)
     rows_block = 128
@@ -843,18 +964,18 @@
             (sds(slots_shape, bf16),) + whole,
         ],
         [pltpu.VMEM((tokens_here, features), bf16)],
-    )
-    in_parts_w = both_cores(in_far, mid_done)
-    if odd_rows:
-        in_parts_w = from_order(to_order(*in_parts_w), 4)
+        after=[down_other, in_far],
+    )
+    in_far, in_far_other = far_parts(in_far, mid_done)
+    in_parts_w = regroup(in_pair, in_far, in_other, in_far_other)
     recv_rows = exchange(send_rows, ROWS).reshape(-1, features)
     n_rows = recv_rows.shape[0]
     hid = expert_gate.shape[2]
     tile = 512 if hid % 512 == 0 else hid
     tiles = (hid // tile,)
-    pieces, _, piece_rows, _ = in_parts_w[0].shape
-    w_part = ((pieces, 2, piece_rows, tile), lambda i, *_: (0, 0, 0, i))
-    w_tile = pltpu.VMEM((pieces, 2, piece_rows, tile), bf16)
+    _, _, piece_rows, _ = in_parts_w[0].shape
+    w_part = ((2, 2, piece_rows, tile), lambda i, *_: (0, 0, 0, i))
+    w_tile = pltpu.VMEM((2, 2, 2, piece_rows, tile), bf16)
     h_col = ((n_rows, tile), by_col)
     in_parts = [(w,) + w_part for w in in_parts_w]
     gate_part, up_part, hidden, hidden_done = call(
@@ -871,11 +992,10 @@
         [w_tile] * 2,
         prefetch=1,
     )
-    down_parts_w = both_cores(down_far, hidden_done)
-    far_pieces, far_rows, _ = down_parts_w[0].shape
-    per_tile = tile // (2 * far_rows)
-    down_block = ((per_tile, far_rows, features), by_first)
-    down_tile = pltpu.VMEM((per_tile, 2, far_rows, features), bf16)
+    down_far, down_far_other = far_parts(down_far, hidden_done)
+    down_parts_w = [p[:, 0] for p in regroup(down_pair, down_far, down_other, down_far_other)]
+    far_rows = down_parts_w[0].shape[1]
+    down_tile = pltpu.VMEM((2, 2, 2, far_rows, features), bf16)
     row_tile = n_rows // 4
     result_rows, _ = call(
         expert_result_kernel,
@@ -885,11 +1005,10 @@
         [
             (me,) + whole,
             (hidden, (row_tile, hid), by_row),
-            (down_parts_w[0],) + whole,
-            (down_parts_w[1],) + whole,
-        ],
+        ]
+        + [(p,) + whole for p in down_parts_w],
         [(sds((n_rows, features), bf16), (row_tile, features), by_row)],
-        [pltpu.VMEM((far_pieces, 2, far_rows, features), bf16)],
+        [down_tile],
         prefetch=1,
     )
     back_rows = exchange(result_rows.reshape(slots_shape), ROWS)
@@ -929,12 +1048,12 @@
         8,
         tiles,
         [(me,) + whole, (hidden,) + h_col, (grad_recv,) + whole],
-        [(sds(down_parts_w[0].shape, bf16),) + down_block] * 2,
-        [down_tile],
+        [(sds((4, far_rows, features), bf16), (1, far_rows, features), by_first)] * 2,
+        [pltpu.VMEM((1, 2, far_rows, features), bf16)],
         prefetch=1,
     )
-    down_sum = core_sum(*down_grads)
-    part_out = (sds(in_parts_w[0].shape, bf16),) + w_part
+    down_sum = core_sum(*owner_slices(*(p[:, None] for p in down_grads)))
+    part_out = (sds((4, 2, piece_rows, hid), bf16), (4, 2, piece_rows, tile), w_part[1])
     *in_grads, grad_rows, backward_done = call(
         expert_backward_kernel,
         "expert_backward",
@@ -948,18 +1067,19 @@
             (up_part,) + h_col,
         ]
         + in_parts
+        + [(p,) + whole for p in down_parts_w],
+        [part_out] * 2 + [(sds((n_rows, features), bf16),) + whole],
+        [w_tile] * 2
         + [
-            (down_parts_w[0],) + down_block,
-            (down_parts_w[1],) + down_block,
-        ],
-        [part_out] * 2 + [(sds((n_rows, features), bf16),) + whole],
-        [w_tile] * 2 + [down_tile, w_tile, pltpu.VMEM((n_rows, features), f32)],
+            down_tile,
+            pltpu.VMEM((4, 2, piece_rows, tile), bf16),
+            pltpu.VMEM((n_rows, features), f32),
+        ],
         prefetch=1,
         after=[down_sum],
     )
     grad_back = exchange(grad_rows.reshape(slots_shape), ROWS)
-    if odd_rows:
-        in_grads = from_order(to_order(*in_grads), n_out)
+    down_part = far_sum(down_sum)
     partial_normed, small_cols, vector_cols, route_done = call(
         route_kernel,
         "route",
@@ -979,9 +1099,10 @@
             (sds((features, ROUTES + 4), f32),) + whole,
         ],
     )
-    in_sum = core_sum(*in_grads)
-
-    grad_mid, grad_branch, grad_attended, grad_mixture_gain, _ = call(
+
+    in_sum = core_sum(*owner_slices(*in_grads), route_done)
+
+    grad_mid, grad_branch, grad_attended, grad_mixture_gain, join_done = call(
         join_kernel,
         "join",
         8,
@@ -1011,14 +1132,13 @@
         [(attended_tok,) + whole, (grad_branch,) + whole],
         [(sds((features, features), bf16),) + whole],
     )
-    down_part = far_sum(down_sum)
     grad_heads = exchange(grad_attended, SEQ)
 
-    def to_plane(part):
-        part = part.reshape(n_out, n_in * n_seq, rows_here, -1).transpose(1, 0, 2, 3)
-        return exchange(part, PLANE)
-
-    out_grad = jnp.sum(to_plane(grad_output_proj).astype(f32), 0).astype(bf16)
+    def plane_blocks(part):
+        return part.reshape(n_out, n_plane, rows_here, -1).transpose(1, 0, 2, 3)
+
+    out_blocks = plane_blocks(grad_output_proj)
+    out_grad = jnp.sum(exchange(out_blocks, PLANE).astype(f32), 0).astype(bf16)
 
     small_grads = jnp.concatenate(
         [
@@ -1041,9 +1161,15 @@
     small_low = two_parts(small_grads, 1)
     small_low = jnp.pad(small_low, ((0, 0), (0, -(3 * wide + 2 * n_small) % 128)))
     keep, sent, last, attention_done = attend_backward(
-        chosen, grad_heads, attended_t, log_totals, *heads_saved, start, held, normed_first,
-        own_in, small_low, [grad_output_proj],
-    )
+        chosen, grad_heads, attended_t, log_totals, *heads_saved, start, seq_inputs, normed_first,
+        own_in, small_low, [out_blocks],
+    )
+
+    in_part = far_sum(in_sum) + attention_done[0, 0].astype(bf16)
+    given = [
+        lax.ppermute(item(part, i), ("b", "d", "sc"), pairs)
+        for part, i, pairs in ((in_part, b_id, alike), (in_part, 1 - b_id, unlike))
+    ]
 
     sent = lax.ppermute(sent, SEQ, [(i, i ^ 1) for i in range(n_seq)])
     near, sent, added = call(
@@ -1059,7 +1185,9 @@
             (tok, (tokens_here // 2, features), by_row),
             (sds((tokens_here, features), bf16), (tokens_here // 2, features), by_row),
         ],
-    )
+        after=[in_part],
+    )
+    last = exchange(plane_blocks(last + added[0, 0].astype(bf16)), PLANE)
     sent = lax.ppermute(sent, SEQ, [(i, i ^ 2) for i in range(n_seq)])
     grad_input, finished = call(
         finish_kernel,
@@ -1074,13 +1202,23 @@
             (gain_first,) + whole,
         ],
         [(tok,) + wide_block],
-    )
-    grad_expert_down = to_owner(down_part + attention_done[0, 0].astype(bf16))
-    in_grads = to_owner(far_sum(in_sum) + finished[0, 0].astype(bf16))
-    grad_expert_gate, grad_expert_up = in_grads[:, 0], in_grads[:, 1]
-
-    last = last + added[0, 0].astype(bf16)
-    last = to_plane(last)
+        after=[last],
+    )
+
+    in_shape = (2,) + in_part.shape[2:]
+    in_block = (in_shape[0], in_shape[1], hid // 4)
+    cols_part = ((2,) + in_block, lambda i, *_: (0, 0, 0, i))
+    cols_item = (in_block, by_last)
+    grad_expert_gate, grad_expert_up, _ = call(
+        owner_kernel,
+        "owner",
+        4,
+        (4,),
+        [(which, None, None), (in_part,) + cols_part] + [(x,) + cols_item for x in given],
+        [(sds(in_shape, f32),) + cols_item] * 2,
+        prefetch=1,
+        after=[grad_input],
+    )
     cols = last[:, :, :, : 3 * wide].reshape(n_in, n_seq, n_out, rows_here, 3 * wide)
     cols = (jnp.sum(cols.astype(f32), 0) + finished[0, 0]).astype(bf16).transpose(1, 2, 0, 3)
     rest = jnp.sum(last[:, :, :, 3 * wide : 3 * wide + 2 * n_small].astype(f32), 0)
@@ -1089,28 +1227,35 @@
         [cols.reshape(n_out, rows_here, -1), out_grad, two_parts(rest, 2)], 2
     )
     last = jnp.pad(last, ((0, 0), (0, 0), (0, -last.shape[2] % 128)))
-    last = jnp.sum(exchange(last, OUTER).astype(f32), 0)
-    grad_input_proj = (
-        last[:, : 3 * features]
-        .reshape(rows_here, n_seq, 3, wide)
-        .transpose(0, 2, 1, 3)
-        .reshape(rows_here, 3 * features)
-    )
-    grad_output_proj = last[:, 3 * features : 4 * features]
-    last = last[:, 4 * features : 4 * features + 2 * n_small]
-    small_grads = last[:, :n_small] + last[:, n_small:]
-    mean_loss = small_grads[0, 20] / (2.0 * features * valid_count)
+    *last, small_grads, grad_const_vectors, _ = call(
+        functools.partial(total_kernel, n_small),
+        "total",
+        2,
+        (1,),
+        [(exchange(last, OUTER),) + whole],
+        [
+            (sds((rows_here, 3 * features), f32),) + whole,
+            (sds((rows_here, features), f32),) + whole,
+            (sds((rows_here, ROUTES), f32),) + whole,
+            (sds((rows_here, 4), f32),) + whole,
+            (sds((24, rows_here), f32),) + whole,
+            (sds((2, rows_here), f32),) + whole,
+        ],
+    )
+    grad_expert_down = to_owner(down_part + finished[0, 0].astype(bf16))[:, 0]
+    grad_input_proj, grad_output_proj, grad_router, grad_const_mix = last
+    mean_loss = small_grads[20, 0] / (2.0 * features * valid_count)
     return (
         full_output,
         mean_loss,
         grad_input,
         grad_input_proj,
         grad_output_proj,
-        small_grads[:, 0],
-        small_grads[:, 1],
-        small_grads[:, 2:14],
-        small_grads[:, 14:18],
-        small_grads[:, 18:20].T,
+        small_grads[0],
+        small_grads[1],
+        grad_router,
+        grad_const_mix,
+        grad_const_vectors,
         grad_expert_gate,
         grad_expert_up,
         grad_expert_down,

time: 572 us -> 549 us (0.960)
  the two profiles are of different devices: /device:TPU:2 before, /device:TPU:1 now
where the time goes in v4:
time: 549 us; the launch traced here: 539 us
  Pallas kernels  208 us (38%)
  waiting for transfers between devices  113 us (21%)
  starting transfers between devices  77.3 us (14%)
  local copies, waits for them, and re-layouts  46.7 us (9%)
  other arithmetic  39.2 us (7%)
  blocking collectives  29.5 us (5%)
  between operations  24.7 us (4%)
    pallas_call x20, Pallas kernels, call(): pl.pallas_call(ordered, grid_spec=pltpu.PrefetchScalarGridSpec(num_scalar...  208 us
    all_to_all x10, waiting for transfers between devices, exchange(): return lax.all_to_all(blocks, axes, split_axis=0, concat_axis=0, tiled=True)  63.8 us
    all_to_all x10, starting transfers between devices, exchange(): return lax.all_to_all(blocks, axes, split_axis=0, concat_axis=0, tiled=True)  48.2 us
    all_to_all x1, blocking collectives, exchange(): return lax.all_to_all(blocks, axes, split_axis=0, concat_axis=0, tiled=True)  29.5 us
    ppermute x1, waiting for transfers between devices, body(): sent = lax.ppermute(sent, SEQ, [(i, i ^ 2) for i in range(n_seq)])  21.6 us
    unnamed x87, local copies, waits for them, and re-layouts  18.5 us
  transfers between devices with their start and end apart: 32, of which 14 were waited for; matrix products, arithmetic and copies ran while one was open for 11% of the time, Pallas kernels for 25%

profile of v4, /device:TPU:1, one launch (start us, length us, event | category | flops | bytes accessed | tf_op | source)
XLA Modules:
  0.0 539.1 jit_solution(11289256304186370200)
XLA Ops:
  52.3 6.6 %all-to-all-done = bf16[32,24,768]{2,1,0:T(8,128)(2,1)} async-done(((bf16[32,24,768]{2,1,0:T(8,128)(2,1)}), bf16[32,24,768]{2,1,0:T(8,128)(2,1)}, u32[]{:S(2)}, u32[]{:S(2)}) %all-to-all-start) | async-done | bytes 1179680 | tf_op jit(solution)/shard_map/all_to_all | solution.py:697
  64.3 5.3 all-to-all-start.2
  77.6 26.6 %attend_forward.1 = (bf16[2048,768]{1,0:T(8,128)(2,1)}, bf16[2048,768]{1,0:T(8,128)(2,1)}, bf16[4,192,512]{2,1,0:T(8,128)(2,1)}, f32[192,2048]{1,0:T(8,128)}, f3...) custom-call(s32[4]{0:T(128)} %copy-done.34, ...), custom_call_target="tpu_custom_call" | custom-call | flops 149500000 | bytes 17673220 | tf_op jit(solution)/shard_map/attend_forward/pallas_call | solution.py:313
  115.8 7.2 %all-to-all-done.1.refs_0_ = bf16[4,192,512]{2,1,0:T(8,128)(2,1)S(1)} async-done(((bf16[4,192,512]{2,1,0:T(8,128)(2,1)}), bf16[4,192,512]{2,1,0:T(8,128)(2,1)S(1)}, u32[]{:S(2)}, u32[]{:S(2)}) %all-to-all-start.1) | async-done | bytes 786464 | tf_op jit(solution)/shard_map/all_to_all | solution.py:697
  123.0 5.3 all-gather.5.cloned.1.call-done
  128.3 9.9 %mid.1 = (f32[512,768]{1,0:T(8,128)}, f32[512,768]{1,0:T(8,128)}, f32[512,16]{1,0:T(8,128)}, bf16[8,160,768]{2,1,0:T(8,128)(2,1)}, f32[1,1]{1,0:T(1,128)}) custom-call(bf16[4,192,512]{2,1,0:T(8,128)(2,1)} %copy-done.9, bf16[512,768]{1,0:T(8,128)(2,1)} %refs_3_.2, bf16[768,768]{1,0:T(8,128)(2,1)} %copy.181.refs_2_.refs_6_, ...), custom_call_target="tpu_custom_call" | custom-call | flops 57500000 | bytes 7998468 | tf_op jit(solution)/shard_map/mid/pallas_call | solution.py:313
  148.0 25.9 %all-to-all-done.3 = bf16[8,160,768]{2,1,0:T(8,128)(2,1)S(1)} async-done(((bf16[8,160,768]{2,1,0:T(8,128)(2,1)}), bf16[8,160,768]{2,1,0:T(8,128)(2,1)S(1)}, u32[]{:S(2)}, u32[]{:S(2)}) %all-to-all-start.3) | async-done | bytes 1966112 | tf_op jit(solution)/shard_map/all_to_all | solution.py:697
  175.1 14.7 %expert_hidden.1 = (f32[1280,2048]{1,0:T(8,128)}, f32[1280,2048]{1,0:T(8,128)}, bf16[1280,2048]{1,0:T(8,128)(2,1)}, f32[1,1]{1,0:T(1,128)}) custom-call(s32[2]{0:T(128)} %pad_add_fusion.refs_0_, bf16[1280,768]{1,0:T(8,128)(2,1)} %bitcast.133, bf16[2,2,96,2048]{3,2,1,0:T(8,128)(2,1)} %get-tuple-element.87.refs_2_.refs_5_, bf16[2,2,96,2048]{3,2,1,0:T(8,128)(2,1)} %copy-done.3, ...), custom_call_target="tpu_custom_call" | custom-call | flops 80500000 | bytes 34471940 | tf_op jit(solution)/shard_map/expert_hidden/pallas_call | solution.py:313
  197.6 9.1 %expert_result.1 = (bf16[1280,768]{1,0:T(8,128)(2,1)}, f32[1,1]{1,0:T(1,128)}) custom-call(s32[2]{0:T(128)} %pad_add_fusion.refs_0_, bf16[1280,2048]{1,0:T(8,128)(2,1)} %get-tuple-element.97.refs_1_, bf16[2,256,768]{2,1,0:T(8,128)(2,1)} %bitcast.141, bf16[2,256,768]{2,1,0:T(8,128)(2,1)} %get-tuple-element.223.refs_3_.refs_10_, ...), custom_call_target="tpu_custom_call" | custom-call | flops 46000000 | bytes 10354692 | tf_op jit(solution)/shard_map/expert_result/pallas_call | solution.py:313
  206.7 8.9 %all-to-all-start.4 = ((bf16[8,160,768]{2,1,0:T(8,128)(2,1)}), bf16[8,160,768]{2,1,0:T(8,128)(2,1)S(1)}, u32[]{:S(2)}, u32[]{:S(2)}) async-start(bf16[8,160,768]{2,1,0:T(8,128)(2,1)} %bitcast.152), calls=%async_computation.4 | async-start | bytes 3932160 | tf_op jit(solution)/shard_map/all_to_all | solution.py:697
  220.8 18.2 %all-to-all-done.4.refs_0_ = bf16[8,160,768]{2,1,0:T(8,128)(2,1)S(1)} async-done(((bf16[8,160,768]{2,1,0:T(8,128)(2,1)}), bf16[8,160,768]{2,1,0:T(8,128)(2,1)S(1)}, u32[]{:S(2)}, u32[]{:S(2)}) %all-to-all-start.4) | async-done | bytes 1966112 | tf_op jit(solution)/shard_map/all_to_all | solution.py:697
  240.3 11.1 %loss.1 = (bf16[512,768]{1,0:T(8,128)(2,1)}, f32[512,768]{1,0:T(8,128)}, f32[512,8]{1,0:T(8,128)}, bf16[8,160,768]{2,1,0:T(8,128)(2,1)}, f32[1,768]{1,0:T(1,128)}, /*index=5*/f32[1,1]{1,0:T(1,128)}) custom-call(bf16[8,160,768]{2,1,0:T(8,128)(2,1)} %copy-done.8, s32[512,2]{1,0:T(8,128)} %copy-done.14, s32[8,512]{1,0:T(8,128)} %pad.41.clone.refs_6_.refs_2_, ...), custom_call_target="tpu_custom_call" | custom-call | flops 63250000 | bytes 10308616 | tf_op jit(solution)/shard_map/loss/pallas_call | solution.py:313
  251.5 29.5 %all_to_all.55 = bf16[8,160,768]{2,1,0:T(8,128)(2,1)} all-to-all(bf16[8,160,768]{2,1,0:T(8,128)(2,1)} %get-tuple-element.104), channel_id=1, replica_groups=mesh['a'=2,'b'=2,'d'=2,'sx'=2,'sc'=2] {'b','d','sx'}, dimensions={0} | all-to-all | bytes 3932160 | tf_op jit(solution)/shard_map/all_to_all | solution.py:697
  280.9 9.0 %down_grad.1 = (bf16[4,256,768]{2,1,0:T(8,128)(2,1)}, bf16[4,256,768]{2,1,0:T(8,128)(2,1)}, f32[1,1]{1,0:T(1,128)}) custom-call(s32[2]{0:T(128)} %pad_add_fusion.refs_0_, bf16[1280,2048]{1,0:T(8,128)(2,1)} %get-tuple-element.97.refs_1_, bf16[1280,768]{1,0:T(8,128)(2,1)} %bitcast.131), custom_call_target="tpu_custom_call" | custom-call | flops 46000000 | bytes 10354692 | tf_op jit(solution)/shard_map/down_grad/pallas_call | solution.py:313
  298.9 33.6 %expert_backward.1 = (bf16[4,2,96,2048]{3,2,1,0:T(8,128)(2,1)}, bf16[4,2,96,2048]{3,2,1,0:T(8,128)(2,1)}, bf16[1280,768]{1,0:T(8,128)(2,1)}, f32[1,1]{1,0:T(1,128)}) custom-call(s32[2]{0:T(128)} %pad_add_fusion.refs_0_, bf16[1280,768]{1,0:T(8,128)(2,1)} %bitcast.134, bf16[1280,768]{1,0:T(8,128)(2,1)} %bitcast.132, f32[1280,2048]{1,0:T(8,128)} %get-tuple-element.105.refs_3_, ...), custom_call_target="tpu_custom_call" | custom-call | flops 184000000 | bytes 42598404 | tf_op jit(solution)/shard_map/expert_backward/pallas_call | solution.py:313
  336.6 13.4 %route.1 = (f32[512,768]{1,0:T(8,128)}, f32[768,16]{1,0:T(8,128)}, f32[768,16]{1,0:T(8,128)}, f32[1,1]{1,0:T(1,128)}) custom-call(f32[512,16]{1,0:T(8,128)} %get-tuple-element.100.refs_4_.refs_0_, s32[512,2]{1,0:T(8,128)} %copy-done.6, f32[512,8]{1,0:T(8,128)} %get-tuple-element.110.refs_2_, f32[512,768]{1,0:T(8,128)} %get-tuple-element.111.refs_3_.refs_4_, ...), custom_call_target="tpu_custom_call" | custom-call | flops 80500000 | bytes 4919300 | tf_op jit(solution)/shard_map/route/pallas_call | solution.py:313
  350.1 6.9 %add_convert_fusion = bf16[4,2,96,2048]{3,2,1,0:T(8,128)(2,1)} fusion(bf16[4,2,96,2048]{3,2,1,0:T(8,128)(2,1)} %collective-permute-done.11, bf16[4,2,96,2048]{3,2,1,0:T(8,128)(2,1)} %get-tuple-element.113, f32[]{:T(128)} %bitcast.50), kind=kLoop, calls=%fused_computation.2 | loop fusion | flops 7864320 | bytes 9437188 | tf_op jit(solution)/shard_map/convert_element_type | solution.py:798
  362.1 9.3 %join.1 = (f32[512,768]{1,0:T(8,128)}, bf16[512,768]{1,0:T(8,128)(2,1)}, bf16[4,192,512]{2,1,0:T(8,128)(2,1)}, f32[1,768]{1,0:T(1,128)}, f32[1,1]{1,0:T(1,128)}) custom-call(bf16[8,160,768]{2,1,0:T(8,128)(2,1)} %copy-done.7, s32[512,2]{1,0:T(8,128)} %copy-done.14, f32[512,768]{1,0:T(8,128)} %get-tuple-element.112.refs_2_, ...), custom_call_target="tpu_custom_call" | custom-call | flops 46000000 | bytes 11020292 | tf_op jit(solution)/shard_map/join/pallas_call | solution.py:313
  371.4 5.3 all-to-all-start.7
  388.4 37.9 %attend_backward.1 = (f32[2,512,768]{2,1,0:T(8,128)}, bf16[2,512,768]{2,1,0:T(8,128)(2,1)}, bf16[768,640]{1,0:T(8,128)(2,1)}, f32[1,1]{1,0:T(1,128)}) custom-call(s32[4]{0:T(128)} %copy-done.34, bf16[4,192,512]{2,1,0:T(8,128)(2,1)} %copy-done.21, f32[192,2048]{1,0:T(8,128)} %get-tuple-element.117.refs_2_, f32[8,2048]{1,0:T(8,128)} %get-tuple-element.118.refs_3_, ...), custom_call_target="tpu_custom_call" | custom-call | flops 43699998720 | bytes 19341316 | tf_op jit(solution)/shard_map/attend_backward/pallas_call | solution.py:313
  446.3 6.0 %all-to-all-start.8 = ((bf16[8,4,24,640]{3,2,1,0:T(8,128)(2,1)}), bf16[8,4,24,640]{3,2,1,0:T(8,128)(2,1)S(1)}, u32[]{:S(2)}, u32[]{:S(2)}) async-start(bf16[8,4,24,640]{3,2,1,0:T(8,128)(2,1)} %bitcast.122), calls=%async_computation.9 | async-start | bytes 1966080 | tf_op jit(solution)/shard_map/all_to_all | solution.py:697
  460.7 21.6 %collective-permute-done.13.refs_1_ = bf16[512,768]{1,0:T(8,128)(2,1)} collective-permute-done((bf16[512,768]{1,0:T(8,128)(2,1)}, bf16[512,768]{1,0:T(8,128)(2,1)}, u32[]{:S(2)}, u32[]{:S(2)}) %collective-permute-start.13) | collective-permute-done | bytes 786464 | tf_op jit(solution)/shard_map/ppermute | solution.py:1191
  506.5 4.8 owner.1
  512.4 7.5 %collective-permute-done.17 = bf16[1,256,768]{2,1,0:T(8,128)(2,1)} collective-permute-done((bf16[1,256,768]{2,1,0:T(8,128)(2,1)}, bf16[1,256,768]{2,1,0:T(8,128)(2,1)}, u32[]{:S(2)}, u32[]{:S(2)}) %collective-permute-start.17) | collective-permute-done | bytes 393248 | tf_op jit(solution)/shard_map/ppermute | solution.py:765
  (252 shorter events, 180.8 us)
Async XLA Ops:
  9.2 22.4 %collective-permute-start = (bf16[1,528,768]{2,1,0:T(8,128)(2,1)S(1)}, bf16[1,528,768]{2,1,0:T(8,128)(2,1)S(1)}, u32[]{:S(2)}, u32[]{:S(2)}) collective-permute-start(bf16[1,528,768]{2,1,0:T(8,128)(2,1)S(1)} %fusion.3), channel_id=1, source_target_pairs={{0,2},{1,3},{2,0},{3,1},{4,6},{5,7},{6,4},{7,5},{8,10},{9,11},{10,... | collective-permute-start | bytes 2433032 | tf_op jit(solution)/shard_map/ppermute | solution.py:709
  15.0 27.6 %collective-permute-start.3 = (bf16[2,96,2048]{2,1,0:T(8,128)(2,1)}, bf16[2,96,2048]{2,1,0:T(8,128)(2,1)}, u32[]{:S(2)}, u32[]{:S(2)}) collective-permute-start(bf16[2,96,2048]{2,1,0:T(8,128)(2,1)} %get-tuple-element.86), channel_id=1, source_target_pairs={{0,8},{1,12},{4,9},{5,13},{8,0},{9,4},{12,1},{13,5},{2,10},{3,14},... | collective-permute-start | bytes 2359304 | tf_op jit(solution)/shard_map/ppermute | solution.py:769
  18.0 28.3 %collective-permute-start.2 = (bf16[2,96,2048]{2,1,0:T(8,128)(2,1)}, bf16[2,96,2048]{2,1,0:T(8,128)(2,1)}, u32[]{:S(2)}, u32[]{:S(2)}) collective-permute-start(bf16[2,96,2048]{2,1,0:T(8,128)(2,1)} %get-tuple-element.85.refs_1_), channel_id=1, source_target_pairs={{1,4},{4,1},{9,12},{12,9},{3,6},{6,3},{11,14},{14,11},{17,20},{20,... | collective-permute-start | bytes 2359304 | tf_op jit(solution)/shard_map/ppermute | solution.py:768
  26.3 32.6 %all-to-all-start = ((bf16[32,24,768]{2,1,0:T(8,128)(2,1)}), bf16[32,24,768]{2,1,0:T(8,128)(2,1)}, u32[]{:S(2)}, u32[]{:S(2)}) async-start(bf16[32,24,768]{2,1,0:T(8,128)(2,1)} %bitcast.14), calls=%async_computation | async-start | bytes 2359296 | tf_op jit(solution)/shard_map/all_to_all | solution.py:697
  30.6 97.7 %all-gather.5.cloned.1.call-start = ((), (), s32[]{:S(2)}) async-start(), calls=%async_computation.15 | async-start | bytes 4718592 | tf_op jit(solution)/shard_map/all_gather | solution.py:786
  52.3 24.2 %collective-permute-start.4 = (bf16[2,2,96,2048]{3,2,1,0:T(8,128)(2,1)S(1)}, bf16[2,2,96,2048]{3,2,1,0:T(8,128)(2,1)S(1)}, u32[]{:S(2)}, u32[]{:S(2)}) collective-permute-start(bf16[2,2,96,2048]{3,2,1,0:T(8,128)(2,1)S(1)} %copy-done.1), channel_id=1, source_target_pairs={{0,1},{1,0},{2,3},{3,2},{4,5},{5,4},{6,7},{7,6},{8,9},{9,8},{10,11... | collective-permute-start | bytes 4718600 | tf_op jit(solution)/shard_map/ppermute | solution.py:869
  64.3 43.7 %all-to-all-start.2 = ((bf16[8,768,128]{1,2,0:T(8,128)(2,1)}), bf16[8,768,128]{1,2,0:T(8,128)(2,1)}, u32[]{:S(2)}, u32[]{:S(2)}) async-start(bf16[8,768,128]{1,2,0:T(8,128)(2,1)} %broadcast_in_dim.73), calls=%async_computation.2 | async-start | bytes 3145728 | tf_op jit(solution)/shard_map/all_to_all | solution.py:697
  71.5 32.7 %collective-permute-start.6 = (bf16[1,256,768]{2,1,0:T(8,128)(2,1)}, bf16[1,256,768]{2,1,0:T(8,128)(2,1)S(1)}, u32[]{:S(2)}, u32[]{:S(2)}) collective-permute-start(bf16[1,256,768]{2,1,0:T(8,128)(2,1)} %get-tuple-element.92), channel_id=1, source_target_pairs={{0,8},{1,12},{4,9},{5,13},{8,0},{9,4},{12,1},{13,5},{2,10},{3,14},... | collective-permute-start | bytes 1179656 | tf_op jit(solution)/shard_map/ppermute | solution.py:769
  73.0 31.2 %collective-permute-start.5 = (bf16[1,256,768]{2,1,0:T(8,128)(2,1)}, bf16[1,256,768]{2,1,0:T(8,128)(2,1)S(1)}, u32[]{:S(2)}, u32[]{:S(2)}) collective-permute-start(bf16[1,256,768]{2,1,0:T(8,128)(2,1)} %get-tuple-element.91.refs_1_), channel_id=1, source_target_pairs={{1,4},{4,1},{9,12},{12,9},{3,6},{6,3},{11,14},{14,11},{17,20},{20,... | collective-permute-start | bytes 1179656 | tf_op jit(solution)/shard_map/ppermute | solution.py:768
  138.2 35.7 %all-to-all-start.3 = ((bf16[8,160,768]{2,1,0:T(8,128)(2,1)}), bf16[8,160,768]{2,1,0:T(8,128)(2,1)S(1)}, u32[]{:S(2)}, u32[]{:S(2)}) async-start(bf16[8,160,768]{2,1,0:T(8,128)(2,1)} %get-tuple-element.95), calls=%async_computation.3 | async-start | bytes 3932160 | tf_op jit(solution)/shard_map/all_to_all | solution.py:697
  141.8 48.7 %all-gather.7.cloned.1.call-start = ((), (), s32[]{:S(2)}) async-start(), calls=%async_computation.16 | async-start | bytes 2359296 | tf_op jit(solution)/shard_map/all_gather | solution.py:786
  206.7 32.3 %all-to-all-start.4 = ((bf16[8,160,768]{2,1,0:T(8,128)(2,1)}), bf16[8,160,768]{2,1,0:T(8,128)(2,1)S(1)}, u32[]{:S(2)}, u32[]{:S(2)}) async-start(bf16[8,160,768]{2,1,0:T(8,128)(2,1)} %bitcast.152), calls=%async_computation.4 | async-start | bytes 3932160 | tf_op jit(solution)/shard_map/all_to_all | solution.py:697
  332.5 17.5 %collective-permute-start.11 = (bf16[4,2,96,2048]{3,2,1,0:T(8,128)(2,1)}, bf16[4,2,96,2048]{3,2,1,0:T(8,128)(2,1)}, u32[]{:S(2)}, u32[]{:S(2)}) collective-permute-start(bf16[4,2,96,2048]{3,2,1,0:T(8,128)(2,1)} %get-tuple-element.114), channel_id=1, source_target_pairs={{0,1},{1,0},{2,3},{3,2},{4,5},{5,4},{6,7},{7,6},{8,9},{9,8},{10,11... | collective-permute-start | bytes 9437192 | tf_op jit(solution)/shard_map/ppermute | solution.py:795
  333.0 27.8 %all-to-all-start.6 = ((bf16[8,160,768]{2,1,0:T(8,128)(2,1)}), bf16[8,160,768]{2,1,0:T(8,128)(2,1)S(1)}, u32[]{:S(2)}, u32[]{:S(2)}) async-start(bf16[8,160,768]{2,1,0:T(8,128)(2,1)} %bitcast.151), calls=%async_computation.6 | async-start | bytes 3932160 | tf_op jit(solution)/shard_map/all_to_all | solution.py:697
  336.6 98.4 %reduce-scatter.3.cloned.1.call-start = ((), (), s32[]{:S(2)}) async-start(), calls=%async_computation.13 | async-start | bytes 4718592 | tf_op jit(solution)/shard_map/reduce_scatter | solution.py:801
  371.4 16.0 %all-to-all-start.7 = ((bf16[4,192,512]{2,1,0:T(8,128)(2,1)}), bf16[4,192,512]{2,1,0:T(8,128)(2,1)S(1)}, u32[]{:S(2)}, u32[]{:S(2)}) async-start(bf16[4,192,512]{2,1,0:T(8,128)(2,1)} %get-tuple-element.116), calls=%async_computation.7 | async-start | bytes 1572864 | tf_op jit(solution)/shard_map/all_to_all | solution.py:697
  376.8 121.2 %reduce-scatter.5.cloned.1.call-start = ((), (), s32[]{:S(2)}) async-start(), calls=%async_computation.14 | async-start | bytes 2359296 | tf_op jit(solution)/shard_map/reduce_scatter | solution.py:801
  427.4 17.9 %all-to-all-start.9 = ((bf16[8,4,24,768]{3,2,1,0:T(8,128)(2,1)}), bf16[8,4,24,768]{3,2,1,0:T(8,128)(2,1)S(1)}, u32[]{:S(2)}, u32[]{:S(2)}) async-start(bf16[8,4,24,768]{3,2,1,0:T(8,128)(2,1)} %bitcast.121.refs_14_), calls=%async_computation.10 | async-start | bytes 2359296 | tf_op jit(solution)/shard_map/all_to_all | solution.py:697
  446.3 36.0 %all-to-all-start.8 = ((bf16[8,4,24,640]{3,2,1,0:T(8,128)(2,1)}), bf16[8,4,24,640]{3,2,1,0:T(8,128)(2,1)S(1)}, u32[]{:S(2)}, u32[]{:S(2)}) async-start(bf16[8,4,24,640]{3,2,1,0:T(8,128)(2,1)} %bitcast.122), calls=%async_computation.9 | async-start | bytes 1966080 | tf_op jit(solution)/shard_map/all_to_all | solution.py:697
  454.4 27.9 %collective-permute-start.13 = (bf16[512,768]{1,0:T(8,128)(2,1)}, bf16[512,768]{1,0:T(8,128)(2,1)}, u32[]{:S(2)}, u32[]{:S(2)}) collective-permute-start(bf16[512,768]{1,0:T(8,128)(2,1)} %get-tuple-element.137), channel_id=1, source_target_pairs={{0,2},{1,3},{2,0},{3,1},{4,6},{5,7},{6,4},{7,5},{8,10},{9,11},{10,... | collective-permute-start | bytes 2359304 | tf_op jit(solution)/shard_map/ppermute | solution.py:1191
  457.0 48.4 %collective-permute-start.15 = (bf16[2,96,2048]{2,1,0:T(8,128)(2,1)}, bf16[2,96,2048]{2,1,0:T(8,128)(2,1)S(1)}, u32[]{:S(2)}, u32[]{:S(2)}) collective-permute-start(bf16[2,96,2048]{2,1,0:T(8,128)(2,1)} %get-tuple-element.220), channel_id=1, source_target_pairs={{0,8},{1,12},{4,9},{5,13},{8,0},{9,4},{12,1},{13,5},{2,10},{3,14},... | collective-permute-start | bytes 2359304 | tf_op jit(solution)/shard_map/ppermute | solution.py:1170
  458.8 46.6 %collective-permute-start.14 = (bf16[2,96,2048]{2,1,0:T(8,128)(2,1)S(1)}, bf16[2,96,2048]{2,1,0:T(8,128)(2,1)S(1)}, u32[]{:S(2)}, u32[]{:S(2)}) collective-permute-start(bf16[2,96,2048]{2,1,0:T(8,128)(2,1)S(1)} %get-tuple-element.221), channel_id=1, source_target_pairs={{1,4},{4,1},{9,12},{12,9},{3,6},{6,3},{11,14},{14,11},{17,20},{20,... | collective-permute-start | bytes 2359304 | tf_op jit(solution)/shard_map/ppermute | solution.py:1170
  494.5 27.9 %all-to-all-start.10 = ((bf16[4,24,3200]{2,1,0:T(8,128)(2,1)}), bf16[4,24,3200]{2,1,0:T(8,128)(2,1)S(1)}, u32[]{:S(2)}, u32[]{:S(2)}) async-start(bf16[4,24,3200]{2,1,0:T(8,128)(2,1)} %pad.44), calls=%async_computation.11 | async-start | bytes 1228800 | tf_op jit(solution)/shard_map/all_to_all | solution.py:697
  503.9 16.0 %collective-permute-start.17 = (bf16[1,256,768]{2,1,0:T(8,128)(2,1)}, bf16[1,256,768]{2,1,0:T(8,128)(2,1)}, u32[]{:S(2)}, u32[]{:S(2)}) collective-permute-start(bf16[1,256,768]{2,1,0:T(8,128)(2,1)} %get-tuple-element.225), channel_id=1, source_target_pairs={{0,8},{1,12},{4,9},{5,13},{8,0},{9,4},{12,1},{13,5},{2,10},{3,14},... | collective-permute-start | bytes 1179656 | tf_op jit(solution)/shard_map/ppermute | solution.py:765
  (47 other events, 338.9 us)
Sparse Core Ops, SparseCore 0:
  51.0 77.2 all-gather.4
  145.0 44.9 all-gather.6
  357.1 77.8 reduce-scatter.2
  437.2 42.8 reduce-scatter.4

commit v5 on v4

--- a/solution.py
+++ b/solution.py
@@ -406,8 +406,10 @@
 
 def prepare_kernel(got, win, win_t, gains, wrm, out):
     inner = win.shape[1]
-    out[...] = got[:, got.shape[1] - out.shape[1] :]
-    turned = got[:, : got.shape[1] - out.shape[1]].astype(f32).T
+    split = got.shape[1] - out.shape[2]
+    for k in range(out.shape[0]):
+        out[k] = got[:, split:]
+    turned = got[:, :split].astype(f32).T
     win[...] = got[:, :inner]
     win_t[...] = turned[:inner].astype(bf16)
     gains[0:2] = turned[inner : inner + 2]
@@ -572,7 +574,7 @@
         other[k] = shard[1 - index[0]]
 
 
-def total_kernel(n_small, parts, gin, gout, router, mix, small, vectors):
+def total_kernel(n_small, parts, share, gin, gout, router, mix, small, vectors, loss, gain_first, gain_mid):
     total = jnp.sum(parts[...].astype(f32), 0)
     features = gout.shape[1]
     wide = HEAD * (features // HEAD // 4)
@@ -589,16 +591,31 @@
     wide_both = tail + jnp.concatenate([tail[:, n_small:], tail[:, :n_small]], 1)
     small[...] = exact_dot(unit, wide_both, ((1,), (1,)))
     vectors[...] = small[18:20]
+    loss[...] = small[20:21, 0:1] * share[...]
+    gain_first[...] = small[0:1]
+    gain_mid[...] = small[1:2]
     router[...] = both[:, 2 : 2 + ROUTES]
     mix[...] = both[:, 2 + ROUTES : 6 + ROUTES]
 
 
-def owner_kernel(which, part, alike, unlike, gate, up):
-    mine = part[which[0]]
-    first = jnp.where(which[1] == 1, mine, alike[...])
-    for k, out in enumerate((gate, up)):
-        out[which[0]] = first[k].astype(f32)
-        out[1 - which[0]] = unlike[k].astype(f32)
+def in_sum_kernel(gate, gate_given, up, up_given, out):
+    for k, (own, given) in enumerate(((gate, gate_given), (up, up_given))):
+        out[:, k] = (own[...].astype(f32) + given[...].astype(f32)).astype(bf16)
+
+
+def part_kernel(which, part, same, other):
+    same[...] = part[which[0]]
+    other[...] = part[1 - which[0]]
+
+
+def owner_kernel(which, same, alike, unlike, *outs):
+    mine = jnp.where(which[1] == 1, same[...], alike[...]).astype(f32)
+    theirs = unlike[...].astype(f32)
+    height = outs[0].shape[1]
+    for k, out in enumerate(outs):
+        here = slice(k * height, (k + 1) * height)
+        out[which[0]] = mine[here]
+        out[1 - which[0]] = theirs[here]
 
 
 def cross_kernel(which, same, alike, unlike, out):
@@ -621,13 +638,17 @@
 def expert_hidden_kernel(
     me, rows, near, far, near_other, far_other, gate_part, up_part, hidden, gate, up
 ):
-    x = rows[...]
     parts = (near, far, near_other, far_other)
-    g = nn(x, whole_tile(me, [p[:, 0] for p in parts], gate))
-    u = nn(x, whole_tile(me, [p[:, 1] for p in parts], up))
-    gate_part[...] = g
-    up_part[...] = u
-    hidden[...] = (g / (1.0 + jnp.exp(-g)) * u).astype(bf16)
+    w_gate = whole_tile(me, [p[:, 0] for p in parts], gate)
+    w_up = whole_tile(me, [p[:, 1] for p in parts], up)
+    step = rows.shape[0] // 2
+    for k in range(2):
+        here = slice(k * step, (k + 1) * step)
+        g = nn(rows[here], w_gate)
+        u = nn(rows[here], w_up)
+        gate_part[here] = g
+        up_part[here] = u
+        hidden[here] = (g / (1.0 + jnp.exp(-g)) * u).astype(bf16)
 
 
 def expert_result_kernel(me, hidden, near, far, near_other, far_other, result, down):
@@ -643,9 +664,9 @@
 
 
 def expert_backward_kernel(
-    me, rows, grad, gate_part, up_part, near, far, near_other, far_other,
+    me, grad, gate_part, up_part, near, far, near_other, far_other,
     down_near, down_far, down_near_other, down_far_other,
-    d_own, d_other, result, gate, up, down, parts, acc,
+    d_gate, d_up, result, gate, up, down, acc,
 ):
     f = pl.program_id(0)
 
@@ -654,29 +675,39 @@
         pieces = (down_near, down_far, down_near_other, down_far_other)
         whole_tile(me, [p[...] for p in pieces], down)
 
-    gh = nt(grad[...], down[f // 2, f % 2].reshape(-1, down.shape[-1]))
-    g = gate_part[...]
-    u = up_part[...]
-    sig = 1.0 / (1.0 + jnp.exp(-g))
-    dg = (gh * u * sig * (1.0 + g * (1.0 - sig))).astype(bf16)
-    du = (gh * (g * sig)).astype(bf16)
-    for k, d in enumerate((dg, du)):
-        d_own[:, k], d_other[:, k] = split_tile(me, tn(rows[...], d).astype(bf16), parts)
+    w_down = down[f // 2, f % 2].reshape(-1, down.shape[-1])
     weights = (near, far, near_other, far_other)
-    part = nt(dg, whole_tile(me, [p[:, 0] for p in weights], gate))
-    part = part + nt(du, whole_tile(me, [p[:, 1] for p in weights], up))
+    w_gate = whole_tile(me, [p[:, 0] for p in weights], gate)
+    w_up = whole_tile(me, [p[:, 1] for p in weights], up)
 
     @pl.when(f == 0)
     def _():
-        acc[...] = part
-
-    @pl.when(f > 0)
-    def _():
-        acc[...] += part
+        acc[...] = jnp.zeros_like(acc)
+
+    step = grad.shape[0] // 2
+    for k in range(2):
+        here = slice(k * step, (k + 1) * step)
+        gh = nt(grad[here], w_down)
+        g = gate_part[here]
+        sig = 1.0 / (1.0 + jnp.exp(-g))
+        silu = g * sig
+        dg = (gh * up_part[here] * (sig + silu * (1.0 - sig))).astype(bf16)
+        du = (gh * silu).astype(bf16)
+        d_gate[here] = dg
+        d_up[here] = du
+        acc[here] += nt(dg, w_gate) + nt(du, w_up)
 
     @pl.when(f == pl.num_programs(0) - 1)
     def _():
         result[...] = acc[...].astype(bf16)
+
+
+def in_grad_kernel(me, rows, d, own, other, parts, turned):
+    @pl.when(pl.program_id(0) == 0)
+    def _():
+        turned[...] = rows[...].astype(f32).T.astype(bf16)
+
+    own[...], other[...] = split_tile(me, nn(turned[...], d[...]).astype(bf16), parts)
 
 
 def seq_add_kernel(keep, given, near, far):
@@ -800,8 +831,41 @@
     def far_sum(part):
         return lax.psum_scatter(part, "a", scatter_dimension=0, tiled=False)
 
-    def to_owner(part):
-        return crossed(item(part, b_id), item(part, 1 - b_id)).astype(f32)
+    def to_owner(part, after):
+        _, height, width = part.shape
+        steps = 4 if width % 512 == 0 else 2
+        one = ((height, width // steps), by_col)
+        same, other, done = call(
+            part_kernel,
+            "part",
+            3,
+            (steps,),
+            [(which, None, None), (part, (2, height, width // steps), by_last)],
+            [(sds((height, width), bf16),) + one] * 2,
+            prefetch=1,
+            after=after,
+        )
+        given = [
+            lax.ppermute(same, ("b", "d", "sc"), alike),
+            lax.ppermute(other, ("b", "d", "sc"), unlike),
+        ]
+
+        def kept(count, after):
+            shape = (2, height // count, width)
+            return call(
+                owner_kernel,
+                "owner",
+                4,
+                (steps,),
+                [(which, None, None)] + [(x,) + one for x in [same] + given],
+                [(sds(shape, f32), shape[:2] + (width // steps,), by_last)] * count,
+                prefetch=1,
+                after=after,
+            )
+
+        return kept, done
+
+    slice_rows = expert_gate.shape[1]
 
     def regroup(near, far, near_other, far_other):
         if n_far == 2:
@@ -867,6 +931,7 @@
     in_pair = cross(same_in, other_in, [held[1], start, slot_row])
     in_far = far_pair(in_pair)
     in_other = lax.ppermute(in_pair, "sc", swap)
+
     same_down, other_down, _ = pick([expert_down], [in_pair])
 
     own_cols = (input_proj + picked[0, 0].astype(bf16)).reshape(rows_here, 3, n_seq, wide)
@@ -917,12 +982,11 @@
             (sds((3 * wide, features), bf16), None, None),
             (sds((8, features), f32), None, None),
             (sds((features, ROUTES + 4), f32), None, None),
-            (sds((features, got.shape[1] - inner), bf16), None, None),
+            (sds((n_plane, features, got.shape[1] - inner), bf16), None, None),
         ],
     )
     gain_first, gain_mid, vectors_f = gains[0:1], gains[1:2], gains[2:4]
-    out_part = jnp.broadcast_to(out_cols[None], (n_plane,) + out_cols.shape)
-    full_out = exchange(out_part, PLANE)[:, :, :piece].transpose(1, 0, 2)
+    full_out = exchange(out_cols, PLANE)[:, :, :piece].transpose(1, 0, 2)
     full_out = full_out.reshape(features, features)
 
     seq_inputs, normed_first, attended, attended_t, log_totals, *heads_saved, forward_done = attend_forward(
@@ -1042,6 +1106,67 @@
         [pltpu.VMEM((tokens_here, features), bf16)] * 2,
     )
     grad_recv = exchange(grad_send, ROWS).reshape(-1, features)
+    partial_normed, small_cols, vector_cols, route_done = call(
+        route_kernel,
+        "route",
+        14,
+        steps,
+        [
+            (soft,) + soft_block,
+            (routes,) + pair_block,
+            (stats, (rows_block, 8), by_row),
+            (grad_full,) + wide_block,
+            (normed,) + wide_block,
+            (wrm,) + whole,
+        ],
+        [
+            (tok,) + wide_block,
+            (sds((features, ROUTES + 4), f32),) + whole,
+            (sds((features, ROUTES + 4), f32),) + whole,
+        ],
+    )
+
+    d_gate, d_up, grad_rows, backward_done = call(
+        expert_backward_kernel,
+        "expert_backward",
+        20,
+        tiles,
+        [
+            (me,) + whole,
+            (grad_recv,) + whole,
+            (gate_part,) + h_col,
+            (up_part,) + h_col,
+        ]
+        + in_parts
+        + [(p,) + whole for p in down_parts_w],
+        [(sds((n_rows, hid), bf16),) + h_col] * 2
+        + [(sds((n_rows, features), bf16),) + whole],
+        [w_tile] * 2 + [down_tile, pltpu.VMEM((n_rows, features), f32)],
+        prefetch=1,
+        after=[partial_normed],
+    )
+    grad_back = exchange(grad_rows.reshape(slots_shape), ROWS)
+    def in_grad(name, d, after):
+        shape = (4, piece_rows, tile)
+        out = (sds((4, piece_rows, hid), bf16), shape, by_last)
+        *grads, _ = call(
+            in_grad_kernel,
+            name,
+            8,
+            tiles,
+            [(me,) + whole, (recv_rows,) + whole, (d,) + h_col],
+            [out] * 2,
+            [
+                pltpu.VMEM((4, 2, piece_rows, tile), bf16),
+                pltpu.VMEM((features, n_rows), bf16),
+            ],
+            prefetch=1,
+            after=after,
+        )
+        return grads
+
+    gate_grads = in_grad("gate_grad", d_gate, [grad_rows])
+    up_grads = in_grad("up_grad", d_up, [gate_grads[0]])
     *down_grads, _ = call(
         down_grad_kernel,
         "down_grad",
@@ -1051,57 +1176,27 @@
         [(sds((4, far_rows, features), bf16), (1, far_rows, features), by_first)] * 2,
         [pltpu.VMEM((1, 2, far_rows, features), bf16)],
         prefetch=1,
-    )
-    down_sum = core_sum(*owner_slices(*(p[:, None] for p in down_grads)))
-    part_out = (sds((4, 2, piece_rows, hid), bf16), (4, 2, piece_rows, tile), w_part[1])
-    *in_grads, grad_rows, backward_done = call(
-        expert_backward_kernel,
-        "expert_backward",
-        32,
-        tiles,
-        [
-            (me,) + whole,
-            (recv_rows,) + whole,
-            (grad_recv,) + whole,
-            (gate_part,) + h_col,
-            (up_part,) + h_col,
-        ]
-        + in_parts
-        + [(p,) + whole for p in down_parts_w],
-        [part_out] * 2 + [(sds((n_rows, features), bf16),) + whole],
-        [w_tile] * 2
-        + [
-            down_tile,
-            pltpu.VMEM((4, 2, piece_rows, tile), bf16),
-            pltpu.VMEM((n_rows, features), f32),
-        ],
-        prefetch=1,
-        after=[down_sum],
-    )
-    grad_back = exchange(grad_rows.reshape(slots_shape), ROWS)
-    down_part = far_sum(down_sum)
-    partial_normed, small_cols, vector_cols, route_done = call(
-        route_kernel,
-        "route",
-        14,
-        steps,
-        [
-            (soft,) + soft_block,
-            (routes,) + pair_block,
-            (stats, (rows_block, 8), by_row),
-            (grad_full,) + wide_block,
-            (normed,) + wide_block,
-            (wrm,) + whole,
-        ],
-        [
-            (tok,) + wide_block,
-            (sds((features, ROUTES + 4), f32),) + whole,
-            (sds((features, ROUTES + 4), f32),) + whole,
-        ],
-    )
-
-    in_sum = core_sum(*owner_slices(*in_grads), route_done)
-
+        after=[up_grads[0]],
+    )
+
+    pairs = [owner_slices(*(q[:, None] for q in pair)) for pair in (gate_grads, up_grads)]
+    terms = [x[:, 0] for own, other in pairs for x in (own, lax.ppermute(other, "sc", swap))]
+    in_sum, _ = call(
+        in_sum_kernel,
+        "in_sum",
+        4,
+        (4,),
+        [(x, (n_out // 4, slice_rows, hid), by_first) for x in terms],
+        [
+            (
+                sds((n_out, 2, slice_rows, hid), bf16),
+                (n_out // 4, 2, slice_rows, hid),
+                lambda i, *_: (i, 0, 0, 0),
+            )
+        ],
+        after=[down_grads[0]],
+    )
+    in_part = far_sum(in_sum.reshape(n_far, 2, 2 * slice_rows, hid))
     grad_mid, grad_branch, grad_attended, grad_mixture_gain, join_done = call(
         join_kernel,
         "join",
@@ -1124,14 +1219,17 @@
         ],
         after=[in_sum],
     )
-    grad_output_proj, _ = call(
+    grad_output_proj, out_done = call(
         out_grad_kernel,
         "out_grad",
         3,
         (1,),
         [(attended_tok,) + whole, (grad_branch,) + whole],
         [(sds((features, features), bf16),) + whole],
-    )
+        after=[in_sum],
+    )
+    down_sum = core_sum(*owner_slices(*(p[:, None] for p in down_grads)), out_done)
+    down_part = far_sum(down_sum)[:, 0]
     grad_heads = exchange(grad_attended, SEQ)
 
     def plane_blocks(part):
@@ -1162,14 +1260,8 @@
     small_low = jnp.pad(small_low, ((0, 0), (0, -(3 * wide + 2 * n_small) % 128)))
     keep, sent, last, attention_done = attend_backward(
         chosen, grad_heads, attended_t, log_totals, *heads_saved, start, seq_inputs, normed_first,
-        own_in, small_low, [out_blocks],
-    )
-
-    in_part = far_sum(in_sum) + attention_done[0, 0].astype(bf16)
-    given = [
-        lax.ppermute(item(part, i), ("b", "d", "sc"), pairs)
-        for part, i, pairs in ((in_part, b_id, alike), (in_part, 1 - b_id, unlike))
-    ]
+        own_in, small_low, [out_blocks, down_sum],
+    )
 
     sent = lax.ppermute(sent, SEQ, [(i, i ^ 1) for i in range(n_seq)])
     near, sent, added = call(
@@ -1185,9 +1277,8 @@
             (tok, (tokens_here // 2, features), by_row),
             (sds((tokens_here, features), bf16), (tokens_here // 2, features), by_row),
         ],
-        after=[in_part],
-    )
-    last = exchange(plane_blocks(last + added[0, 0].astype(bf16)), PLANE)
+    )
+    kept_in, parted = to_owner(in_part, [near])
     sent = lax.ppermute(sent, SEQ, [(i, i ^ 2) for i in range(n_seq)])
     grad_input, finished = call(
         finish_kernel,
@@ -1202,37 +1293,28 @@
             (gain_first,) + whole,
         ],
         [(tok,) + wide_block],
-        after=[last],
-    )
-
-    in_shape = (2,) + in_part.shape[2:]
-    in_block = (in_shape[0], in_shape[1], hid // 4)
-    cols_part = ((2,) + in_block, lambda i, *_: (0, 0, 0, i))
-    cols_item = (in_block, by_last)
-    grad_expert_gate, grad_expert_up, _ = call(
-        owner_kernel,
-        "owner",
-        4,
-        (4,),
-        [(which, None, None), (in_part,) + cols_part] + [(x,) + cols_item for x in given],
-        [(sds(in_shape, f32),) + cols_item] * 2,
-        prefetch=1,
-        after=[grad_input],
-    )
+        after=[parted],
+    )
+
+    grad_expert_gate, grad_expert_up, owned = kept_in(2, [])
+    last = last + (finished[0, 0] + owned[0, 0]).astype(bf16)
+    last = exchange(plane_blocks(last), PLANE)
+    kept_down, _ = to_owner(down_part, [grad_expert_gate])
     cols = last[:, :, :, : 3 * wide].reshape(n_in, n_seq, n_out, rows_here, 3 * wide)
-    cols = (jnp.sum(cols.astype(f32), 0) + finished[0, 0]).astype(bf16).transpose(1, 2, 0, 3)
+    cols = jnp.sum(cols.astype(f32), 0).astype(bf16).transpose(1, 2, 0, 3)
     rest = jnp.sum(last[:, :, :, 3 * wide : 3 * wide + 2 * n_small].astype(f32), 0)
     rest = rest[:, :, :n_small] + rest[:, :, n_small:]
     last = jnp.concatenate(
         [cols.reshape(n_out, rows_here, -1), out_grad, two_parts(rest, 2)], 2
     )
     last = jnp.pad(last, ((0, 0), (0, 0), (0, -last.shape[2] % 128)))
-    *last, small_grads, grad_const_vectors, _ = call(
+    loss_share = 1.0 / (2.0 * features * valid_count)
+    *last, _, grad_const_vectors, mean_loss, gain_first_row, gain_mid_row, _ = call(
         functools.partial(total_kernel, n_small),
         "total",
         2,
         (1,),
-        [(exchange(last, OUTER),) + whole],
+        [(exchange(last, OUTER),) + whole, (loss_share.reshape(1, 1),) + whole],
         [
             (sds((rows_here, 3 * features), f32),) + whole,
             (sds((rows_here, features), f32),) + whole,
@@ -1240,19 +1322,21 @@
             (sds((rows_here, 4), f32),) + whole,
             (sds((24, rows_here), f32),) + whole,
             (sds((2, rows_here), f32),) + whole,
-        ],
-    )
-    grad_expert_down = to_owner(down_part + finished[0, 0].astype(bf16))[:, 0]
+            (sds((1, 1), f32),) + whole,
+            (sds((1, rows_here), f32),) + whole,
+            (sds((1, rows_here), f32),) + whole,
+        ],
+    )
+    grad_expert_down, _ = kept_down(1, [mean_loss])
     grad_input_proj, grad_output_proj, grad_router, grad_const_mix = last
-    mean_loss = small_grads[20, 0] / (2.0 * features * valid_count)
     return (
         full_output,
-        mean_loss,
+        mean_loss.reshape(()),
         grad_input,
         grad_input_proj,
         grad_output_proj,
-        small_grads[0],
-        small_grads[1],
+        gain_first_row.reshape(-1),
+        gain_mid_row.reshape(-1),
         grad_router,
         grad_const_mix,
         grad_const_vectors,

time: 549 us -> 540 us (0.984)
  the two profiles are of different devices: /device:TPU:1 before, /device:TPU:2 now
where the time goes in v5:
time: 540 us; the launch traced here: 530 us
  Pallas kernels  236 us (44%)
  waiting for transfers between devices  137 us (25%)
  starting transfers between devices  69.6 us (13%)
  local copies, waits for them, and re-layouts  46 us (9%)
  between operations  22.2 us (4%)
  other arithmetic  18.5 us (3%)
    pallas_call x26, Pallas kernels, call(): pl.pallas_call(ordered, grid_spec=pltpu.PrefetchScalarGridSpec(num_scalar...  236 us
    all_to_all x11, waiting for transfers between devices, exchange(): return lax.all_to_all(blocks, axes, split_axis=0, concat_axis=0, tiled=True)  99.2 us
    all_to_all x11, starting transfers between devices, exchange(): return lax.all_to_all(blocks, axes, split_axis=0, concat_axis=0, tiled=True)  51.6 us
    unnamed x89, local copies, waits for them, and re-layouts  19.9 us
    ppermute x2, waiting for transfers between devices, to_owner(): lax.ppermute(other, ('b', 'd', 'sc'), unlike)  14.7 us
  transfers between devices with their start and end apart: 34, of which 14 were waited for; matrix products, arithmetic and copies ran while one was open for 8% of the time, Pallas kernels for 33%

profile of v5, /device:TPU:2, one launch (start us, length us, event | category | flops | bytes accessed | tf_op | source)
XLA Modules:
  0.0 529.5 jit_solution(4378641960792892840)
XLA Ops:
  23.0 6.7 %all-to-all-start = ((bf16[32,24,768]{2,1,0:T(8,128)(2,1)}), bf16[32,24,768]{2,1,0:T(8,128)(2,1)}, u32[]{:S(2)}, u32[]{:S(2)}) async-start(bf16[32,24,768]{2,1,0:T(8,128)(2,1)} %bitcast.14), calls=%async_computation | async-start | bytes 2359296 | tf_op jit(solution)/shard_map/all_to_all | solution.py:728
  49.6 8.9 %all-to-all-done = bf16[32,24,768]{2,1,0:T(8,128)(2,1)} async-done(((bf16[32,24,768]{2,1,0:T(8,128)(2,1)}), bf16[32,24,768]{2,1,0:T(8,128)(2,1)}, u32[]{:S(2)}, u32[]{:S(2)}) %all-to-all-start) | async-done | bytes 1179680 | tf_op jit(solution)/shard_map/all_to_all | solution.py:728
  72.4 26.5 %attend_forward.1 = (bf16[2048,768]{1,0:T(8,128)(2,1)}, bf16[2048,768]{1,0:T(8,128)(2,1)}, bf16[4,192,512]{2,1,0:T(8,128)(2,1)}, f32[192,2048]{1,0:T(8,128)}, f3...) custom-call(s32[4]{0:T(128)} %copy-done.35, ...), custom_call_target="tpu_custom_call" | custom-call | flops 149500000 | bytes 17673220 | tf_op jit(solution)/shard_map/attend_forward/pallas_call | solution.py:313
  119.2 8.2 %all-gather.5.cloned.1.call-done = bf16[4,2,96,2048]{3,2,1,0:T(8,128)(2,1)} async-done(((bf16[2,2,96,2048]{3,2,1,0:T(8,128)(2,1)}), bf16[4,2,96,2048]{3,2,1,0:T(8,128)(2,1)}) %all-gather.5.cloned.1.call-update) | async-done | bytes 3145744 | tf_op jit(solution)/shard_map/all_gather | solution.py:817
  127.4 10.0 %mid.1 = (f32[512,768]{1,0:T(8,128)}, f32[512,768]{1,0:T(8,128)}, f32[512,16]{1,0:T(8,128)}, bf16[8,160,768]{2,1,0:T(8,128)(2,1)}, f32[1,1]{1,0:T(1,128)}) custom-call(bf16[4,192,512]{2,1,0:T(8,128)(2,1)} %copy-done.9, bf16[512,768]{1,0:T(8,128)(2,1)} %refs_3_.2, bf16[768,768]{1,0:T(8,128)(2,1)} %copy.187.refs_2_.refs_6_, ...), custom_call_target="tpu_custom_call" | custom-call | flops 57500000 | bytes 7998468 | tf_op jit(solution)/shard_map/mid/pallas_call | solution.py:313
  147.4 32.0 %all-to-all-done.3 = bf16[8,160,768]{2,1,0:T(8,128)(2,1)S(1)} async-done(((bf16[8,160,768]{2,1,0:T(8,128)(2,1)}), bf16[8,160,768]{2,1,0:T(8,128)(2,1)S(1)}, u32[]{:S(2)}, u32[]{:S(2)}) %all-to-all-start.3) | async-done | bytes 1966112 | tf_op jit(solution)/shard_map/all_to_all | solution.py:728
  180.7 14.8 %expert_hidden.1 = (f32[1280,2048]{1,0:T(8,128)}, f32[1280,2048]{1,0:T(8,128)}, bf16[1280,2048]{1,0:T(8,128)(2,1)}, f32[1,1]{1,0:T(1,128)}) custom-call(s32[2]{0:T(128)} %pad_add_fusion.refs_0_, bf16[1280,768]{1,0:T(8,128)(2,1)} %bitcast.123, bf16[2,2,96,2048]{3,2,1,0:T(8,128)(2,1)} %get-tuple-element.99.refs_2_.refs_4_, bf16[2,2,96,2048]{3,2,1,0:T(8,128)(2,1)} %copy-done.4, ...), custom_call_target="tpu_custom_call" | custom-call | flops 80500000 | bytes 34471940 | tf_op jit(solution)/shard_map/expert_hidden/pallas_call | solution.py:313
  201.5 9.1 %expert_result.1 = (bf16[1280,768]{1,0:T(8,128)(2,1)}, f32[1,1]{1,0:T(1,128)}) custom-call(s32[2]{0:T(128)} %pad_add_fusion.refs_0_, bf16[1280,2048]{1,0:T(8,128)(2,1)} %get-tuple-element.109.refs_1_, bf16[2,256,768]{2,1,0:T(8,128)(2,1)} %bitcast.133, bf16[2,256,768]{2,1,0:T(8,128)(2,1)} %get-tuple-element.245.refs_3_.refs_9_, ...), custom_call_target="tpu_custom_call" | custom-call | flops 46000000 | bytes 10354692 | tf_op jit(solution)/shard_map/expert_result/pallas_call | solution.py:313
  220.7 20.8 %all-to-all-done.4.refs_0_ = bf16[8,160,768]{2,1,0:T(8,128)(2,1)S(1)} async-done(((bf16[8,160,768]{2,1,0:T(8,128)(2,1)}), bf16[8,160,768]{2,1,0:T(8,128)(2,1)S(1)}, u32[]{:S(2)}, u32[]{:S(2)}) %all-to-all-start.4) | async-done | bytes 1966112 | tf_op jit(solution)/shard_map/all_to_all | solution.py:728
  242.9 11.1 %loss.1 = (bf16[512,768]{1,0:T(8,128)(2,1)}, f32[512,768]{1,0:T(8,128)}, f32[512,8]{1,0:T(8,128)}, bf16[8,160,768]{2,1,0:T(8,128)(2,1)}, f32[1,768]{1,0:T(1,128)}, /*index=5*/f32[1,1]{1,0:T(1,128)}) custom-call(bf16[8,160,768]{2,1,0:T(8,128)(2,1)} %copy-done.8, s32[512,2]{1,0:T(8,128)} %copy-done.13, s32[8,512]{1,0:T(8,128)} %pad.41.clone.refs_6_.refs_2_, ...), custom_call_target="tpu_custom_call" | custom-call | flops 63250000 | bytes 10308616 | tf_op jit(solution)/shard_map/loss/pallas_call | solution.py:313
  258.4 13.4 %route.1 = (f32[512,768]{1,0:T(8,128)}, f32[768,16]{1,0:T(8,128)}, f32[768,16]{1,0:T(8,128)}, f32[1,1]{1,0:T(1,128)}) custom-call(f32[512,16]{1,0:T(8,128)} %get-tuple-element.112.refs_4_.refs_0_, s32[512,2]{1,0:T(8,128)} %copy-done.6, f32[512,8]{1,0:T(8,128)} %get-tuple-element.119.refs_2_, f32[512,768]{1,0:T(8,128)} %get-tuple-element.120.refs_3_.refs_4_, ...), custom_call_target="tpu_custom_call" | custom-call | flops 80500000 | bytes 4919300 | tf_op jit(solution)/shard_map/route/pallas_call | solution.py:313
  271.9 9.6 %all-to-all-done.5 = bf16[8,160,768]{2,1,0:T(8,128)(2,1)S(1)} async-done(((bf16[8,160,768]{2,1,0:T(8,128)(2,1)}), bf16[8,160,768]{2,1,0:T(8,128)(2,1)S(1)}, u32[]{:S(2)}, u32[]{:S(2)}) %all-to-all-start.5) | async-done | bytes 1966112 | tf_op jit(solution)/shard_map/all_to_all | solution.py:728
  282.7 25.5 %expert_backward.1 = (bf16[1280,2048]{1,0:T(8,128)(2,1)}, bf16[1280,2048]{1,0:T(8,128)(2,1)}, bf16[1280,768]{1,0:T(8,128)(2,1)}, f32[1,1]{1,0:T(1,128)}) custom-call(s32[2]{0:T(128)} %pad_add_fusion.refs_0_, bf16[1280,768]{1,0:T(8,128)(2,1)} %bitcast.127, f32[1280,2048]{1,0:T(8,128)} %get-tuple-element.117.refs_2_, f32[1280,2048]{1,0:T(8,128)} %get-tuple-element.118.refs_3_, ...), custom_call_target="tpu_custom_call" | custom-call | flops 115000000 | bytes 44826628 | tf_op jit(solution)/shard_map/expert_backward/pallas_call | solution.py:313
  313.4 9.5 %gate_grad.1 = (bf16[4,96,2048]{2,1,0:T(8,128)(2,1)}, bf16[4,96,2048]{2,1,0:T(8,128)(2,1)}, f32[1,1]{1,0:T(1,128)}) custom-call(s32[2]{0:T(128)} %pad_add_fusion.refs_0_, bf16[1280,768]{1,0:T(8,128)(2,1)} %bitcast.124, bf16[1280,2048]{1,0:T(8,128)(2,1)} %get-tuple-element.123.refs_2_, bf16[1280,768]{1,0:T(8,128)(2,1)} %get-tuple-element.122.refs_3_), custom_call_target="tpu_custom_call" | custom-call | flops 46000000 | bytes 10354692 | tf_op jit(solution)/shard_map/gate_grad/pallas_call | solution.py:313
  322.8 9.5 %up_grad.1 = (bf16[4,96,2048]{2,1,0:T(8,128)(2,1)}, bf16[4,96,2048]{2,1,0:T(8,128)(2,1)}, f32[1,1]{1,0:T(1,128)}) custom-call(s32[2]{0:T(128)} %pad_add_fusion.refs_0_, bf16[1280,768]{1,0:T(8,128)(2,1)} %bitcast.125, bf16[1280,2048]{1,0:T(8,128)(2,1)} %get-tuple-element.126.refs_2_, bf16[4,96,2048]{2,1,0:T(8,128)(2,1)} %get-tuple-element.124.refs_3_.refs_0_), custom_call_target="tpu_custom_call" | custom-call | flops 46000000 | bytes 10354692 | tf_op jit(solution)/shard_map/up_grad/pallas_call | solution.py:313
  332.8 9.0 %down_grad.1 = (bf16[4,256,768]{2,1,0:T(8,128)(2,1)}, bf16[4,256,768]{2,1,0:T(8,128)(2,1)}, f32[1,1]{1,0:T(1,128)}) custom-call(s32[2]{0:T(128)} %pad_add_fusion.refs_0_, bf16[1280,2048]{1,0:T(8,128)(2,1)} %get-tuple-element.109.refs_1_, bf16[1280,768]{1,0:T(8,128)(2,1)} %bitcast.128, bf16[4,96,2048]{2,1,0:T(8,128)(2,1)} %get-tuple-element.127.refs_3_.refs_2_), custom_call_target="tpu_custom_call" | custom-call | flops 46000000 | bytes 10354692 | tf_op jit(solution)/shard_map/down_grad/pallas_call | solution.py:313
  352.4 9.3 %join.1 = (f32[512,768]{1,0:T(8,128)}, bf16[512,768]{1,0:T(8,128)(2,1)}, bf16[4,192,512]{2,1,0:T(8,128)(2,1)}, f32[1,768]{1,0:T(1,128)}, f32[1,1]{1,0:T(1,128)}) custom-call(bf16[8,160,768]{2,1,0:T(8,128)(2,1)} %copy-done.7, s32[512,2]{1,0:T(8,128)} %copy-done.13, f32[512,768]{1,0:T(8,128)} %get-tuple-element.121.refs_12_.refs_2_, ...), custom_call_target="tpu_custom_call" | custom-call | flops 46000000 | bytes 11020292 | tf_op jit(solution)/shard_map/join/pallas_call | solution.py:313
  376.3 37.9 %attend_backward.1 = (f32[2,512,768]{2,1,0:T(8,128)}, bf16[2,512,768]{2,1,0:T(8,128)(2,1)}, bf16[768,640]{1,0:T(8,128)(2,1)}, f32[1,1]{1,0:T(1,128)}) custom-call(s32[4]{0:T(128)} %copy-done.35, bf16[4,192,512]{2,1,0:T(8,128)(2,1)} %copy-done.21, f32[192,2048]{1,0:T(8,128)} %get-tuple-element.132.refs_2_, f32[8,2048]{1,0:T(8,128)} %get-tuple-element.133.refs_3_, ...), custom_call_target="tpu_custom_call" | custom-call | flops 43699998720 | bytes 19341316 | tf_op jit(solution)/shard_map/attend_backward/pallas_call | solution.py:313
  431.8 5.8 %all-to-all-start.9 = ((bf16[8,4,24,768]{3,2,1,0:T(8,128)(2,1)}), bf16[8,4,24,768]{3,2,1,0:T(8,128)(2,1)S(1)}, u32[]{:S(2)}, u32[]{:S(2)}) async-start(bf16[8,4,24,768]{3,2,1,0:T(8,128)(2,1)} %bitcast.115.refs_14_), calls=%async_computation.10 | async-start | bytes 2359296 | tf_op jit(solution)/shard_map/all_to_all | solution.py:728
  437.6 5.4 %collective-permute-done.14.refs_1_ = bf16[512,768]{1,0:T(8,128)(2,1)S(1)} collective-permute-done((bf16[512,768]{1,0:T(8,128)(2,1)}, bf16[512,768]{1,0:T(8,128)(2,1)S(1)}, u32[]{:S(2)}, u32[]{:S(2)}) %collective-permute-start.14) | collective-permute-done | bytes 786464 | tf_op jit(solution)/shard_map/ppermute | solution.py:1282
  443.9 5.2 finish.1
  449.1 14.7 %collective-permute-done.16.refs_3_ = bf16[192,2048]{1,0:T(8,128)(2,1)S(1)} collective-permute-done((bf16[192,2048]{1,0:T(8,128)(2,1)}, bf16[192,2048]{1,0:T(8,128)(2,1)S(1)}, u32[]{:S(2)}, u32[]{:S(2)}) %collective-permute-start.16) | collective-permute-done | bytes 786464 | tf_op jit(solution)/shard_map/ppermute | solution.py:850
  476.6 13.0 %all-to-all-done.8 = bf16[8,4,24,640]{3,2,1,0:T(8,128)(2,1)S(1)} async-done(((bf16[8,4,24,640]{3,2,1,0:T(8,128)(2,1)}), bf16[8,4,24,640]{3,2,1,0:T(8,128)(2,1)S(1)}, u32[]{:S(2)}, u32[]{:S(2)}) %all-to-all-start.8) | async-done | bytes 983072 | tf_op jit(solution)/shard_map/all_to_all | solution.py:728
  501.3 11.2 %all-to-all-done.10.refs_0_ = bf16[4,24,3200]{2,1,0:T(8,128)(2,1)S(1)} async-done(((bf16[4,24,3200]{2,1,0:T(8,128)(2,1)}), bf16[4,24,3200]{2,1,0:T(8,128)(2,1)S(1)}, u32[]{:S(2)}, u32[]{:S(2)}) %all-to-all-start.10) | async-done | bytes 614432 | tf_op jit(solution)/shard_map/all_to_all | solution.py:728
  (251 shorter events, 180.1 us)
Async XLA Ops:
  9.2 21.4 %collective-permute-start = (bf16[1,528,768]{2,1,0:T(8,128)(2,1)S(1)}, bf16[1,528,768]{2,1,0:T(8,128)(2,1)S(1)}, u32[]{:S(2)}, u32[]{:S(2)}) collective-permute-start(bf16[1,528,768]{2,1,0:T(8,128)(2,1)S(1)} %fusion.4), channel_id=1, source_target_pairs={{0,2},{1,3},{2,0},{3,1},{4,6},{5,7},{6,4},{7,5},{8,10},{9,11},{10,... | collective-permute-start | bytes 2433032 | tf_op jit(solution)/shard_map/ppermute | solution.py:740
  12.9 28.6 %collective-permute-start.3 = (bf16[2,96,2048]{2,1,0:T(8,128)(2,1)}, bf16[2,96,2048]{2,1,0:T(8,128)(2,1)}, u32[]{:S(2)}, u32[]{:S(2)}) collective-permute-start(bf16[2,96,2048]{2,1,0:T(8,128)(2,1)} %get-tuple-element.98), channel_id=1, source_target_pairs={{0,8},{1,12},{4,9},{5,13},{8,0},{9,4},{12,1},{13,5},{2,10},{3,14},... | collective-permute-start | bytes 2359304 | tf_op jit(solution)/shard_map/ppermute | solution.py:800
  15.0 26.5 %collective-permute-start.2 = (bf16[2,96,2048]{2,1,0:T(8,128)(2,1)}, bf16[2,96,2048]{2,1,0:T(8,128)(2,1)}, u32[]{:S(2)}, u32[]{:S(2)}) collective-permute-start(bf16[2,96,2048]{2,1,0:T(8,128)(2,1)} %get-tuple-element.97.refs_1_), channel_id=1, source_target_pairs={{1,4},{4,1},{9,12},{12,9},{3,6},{6,3},{11,14},{14,11},{17,20},{20,... | collective-permute-start | bytes 2359304 | tf_op jit(solution)/shard_map/ppermute | solution.py:799
  23.0 35.5 %all-to-all-start = ((bf16[32,24,768]{2,1,0:T(8,128)(2,1)}), bf16[32,24,768]{2,1,0:T(8,128)(2,1)}, u32[]{:S(2)}, u32[]{:S(2)}) async-start(bf16[32,24,768]{2,1,0:T(8,128)(2,1)} %bitcast.14), calls=%async_computation | async-start | bytes 2359296 | tf_op jit(solution)/shard_map/all_to_all | solution.py:728
  29.7 97.8 %all-gather.5.cloned.1.call-start = ((), (), s32[]{:S(2)}) async-start(), calls=%async_computation.15 | async-start | bytes 4718592 | tf_op jit(solution)/shard_map/all_gather | solution.py:817
  47.4 23.8 %collective-permute-start.4 = (bf16[2,2,96,2048]{3,2,1,0:T(8,128)(2,1)S(1)}, bf16[2,2,96,2048]{3,2,1,0:T(8,128)(2,1)S(1)}, u32[]{:S(2)}, u32[]{:S(2)}) collective-permute-start(bf16[2,2,96,2048]{3,2,1,0:T(8,128)(2,1)S(1)} %copy-done.2), channel_id=1, source_target_pairs={{0,1},{1,0},{2,3},{3,2},{4,5},{5,4},{6,7},{7,6},{8,9},{9,8},{10,11... | collective-permute-start | bytes 4718600 | tf_op jit(solution)/shard_map/ppermute | solution.py:933
  62.0 43.3 %all-to-all-start.2 = ((bf16[8,768,128]{2,1,0:T(8,128)(2,1)}), bf16[8,768,128]{2,1,0:T(8,128)(2,1)}, u32[]{:S(2)}, u32[]{:S(2)}) async-start(bf16[8,768,128]{2,1,0:T(8,128)(2,1)} %get-tuple-element.101), calls=%async_computation.2 | async-start | bytes 3145728 | tf_op jit(solution)/shard_map/all_to_all | solution.py:728
  68.7 30.3 %collective-permute-start.6 = (bf16[1,256,768]{2,1,0:T(8,128)(2,1)}, bf16[1,256,768]{2,1,0:T(8,128)(2,1)S(1)}, u32[]{:S(2)}, u32[]{:S(2)}) collective-permute-start(bf16[1,256,768]{2,1,0:T(8,128)(2,1)} %get-tuple-element.104), channel_id=1, source_target_pairs={{0,8},{1,12},{4,9},{5,13},{8,0},{9,4},{12,1},{13,5},{2,10},{3,14},... | collective-permute-start | bytes 1179656 | tf_op jit(solution)/shard_map/ppermute | solution.py:800
  69.1 29.8 %collective-permute-start.5 = (bf16[1,256,768]{2,1,0:T(8,128)(2,1)}, bf16[1,256,768]{2,1,0:T(8,128)(2,1)S(1)}, u32[]{:S(2)}, u32[]{:S(2)}) collective-permute-start(bf16[1,256,768]{2,1,0:T(8,128)(2,1)} %get-tuple-element.103.refs_1_), channel_id=1, source_target_pairs={{1,4},{4,1},{9,12},{12,9},{3,6},{6,3},{11,14},{14,11},{17,20},{20,... | collective-permute-start | bytes 1179656 | tf_op jit(solution)/shard_map/ppermute | solution.py:799
  137.4 42.0 %all-to-all-start.3 = ((bf16[8,160,768]{2,1,0:T(8,128)(2,1)}), bf16[8,160,768]{2,1,0:T(8,128)(2,1)S(1)}, u32[]{:S(2)}, u32[]{:S(2)}) async-start(bf16[8,160,768]{2,1,0:T(8,128)(2,1)} %get-tuple-element.107), calls=%async_computation.3 | async-start | bytes 3932160 | tf_op jit(solution)/shard_map/all_to_all | solution.py:728
  141.6 54.6 %all-gather.7.cloned.1.call-start = ((), (), s32[]{:S(2)}) async-start(), calls=%async_computation.16 | async-start | bytes 2359296 | tf_op jit(solution)/shard_map/all_gather | solution.py:817
  210.6 31.0 %all-to-all-start.4 = ((bf16[8,160,768]{2,1,0:T(8,128)(2,1)}), bf16[8,160,768]{2,1,0:T(8,128)(2,1)S(1)}, u32[]{:S(2)}, u32[]{:S(2)}) async-start(bf16[8,160,768]{2,1,0:T(8,128)(2,1)} %bitcast.146), calls=%async_computation.4 | async-start | bytes 3932160 | tf_op jit(solution)/shard_map/all_to_all | solution.py:728
  254.0 27.5 %all-to-all-start.5 = ((bf16[8,160,768]{2,1,0:T(8,128)(2,1)}), bf16[8,160,768]{2,1,0:T(8,128)(2,1)S(1)}, u32[]{:S(2)}, u32[]{:S(2)}) async-start(bf16[8,160,768]{2,1,0:T(8,128)(2,1)} %get-tuple-element.116), calls=%async_computation.5 | async-start | bytes 3932160 | tf_op jit(solution)/shard_map/all_to_all | solution.py:728
  308.2 42.9 %all-to-all-start.6 = ((bf16[8,160,768]{2,1,0:T(8,128)(2,1)}), bf16[8,160,768]{2,1,0:T(8,128)(2,1)S(1)}, u32[]{:S(2)}, u32[]{:S(2)}) async-start(bf16[8,160,768]{2,1,0:T(8,128)(2,1)} %bitcast.129), calls=%async_computation.6 | async-start | bytes 3932160 | tf_op jit(solution)/shard_map/all_to_all | solution.py:728
  313.4 111.9 %reduce-scatter.3.cloned.1.call-start = ((), (), s32[]{:S(2)}) async-start(), calls=%async_computation.13 | async-start | bytes 4718592 | tf_op jit(solution)/shard_map/reduce_scatter | solution.py:832
  322.8 19.0 %collective-permute-start.10 = (bf16[4,1,96,2048]{3,2,0,1:T(8,128)(2,1)}, bf16[4,1,96,2048]{3,2,0,1:T(8,128)(2,1)}, u32[]{:S(2)}, u32[]{:S(2)}) collective-permute-start(bf16[4,1,96,2048]{3,2,0,1:T(8,128)(2,1)} %bitcast.171), channel_id=1, source_target_pairs={{0,1},{1,0},{2,3},{3,2},{4,5},{5,4},{6,7},{7,6},{8,9},{9,8},{10,11... | collective-permute-start | bytes 4718600 | tf_op jit(solution)/shard_map/ppermute | solution.py:1183
  341.9 31.2 %collective-permute-start.12 = (bf16[4,1,256,768]{3,2,0,1:T(8,128)(2,1)}, bf16[4,1,256,768]{3,2,0,1:T(8,128)(2,1)S(1)}, u32[]{:S(2)}, u32[]{:S(2)}) collective-permute-start(bf16[4,1,256,768]{3,2,0,1:T(8,128)(2,1)} %bitcast.170), channel_id=1, source_target_pairs={{0,1},{1,0},{2,3},{3,2},{4,5},{5,4},{6,7},{7,6},{8,9},{9,8},{10,11... | collective-permute-start | bytes 4718600 | tf_op jit(solution)/shard_map/ppermute | solution.py:826
  365.3 130.4 %reduce-scatter.5.cloned.1.call-start = ((), (), s32[]{:S(2)}) async-start(), calls=%async_computation.14 | async-start | bytes 2359296 | tf_op jit(solution)/shard_map/reduce_scatter | solution.py:832
  422.4 20.6 %collective-permute-start.14 = (bf16[512,768]{1,0:T(8,128)(2,1)}, bf16[512,768]{1,0:T(8,128)(2,1)S(1)}, u32[]{:S(2)}, u32[]{:S(2)}) collective-permute-start(bf16[512,768]{1,0:T(8,128)(2,1)} %get-tuple-element.152), channel_id=1, source_target_pairs={{0,2},{1,3},{2,0},{3,1},{4,6},{5,7},{6,4},{7,5},{8,10},{9,11},{10,... | collective-permute-start | bytes 2359304 | tf_op jit(solution)/shard_map/ppermute | solution.py:1282
  429.6 34.2 %collective-permute-start.16 = (bf16[192,2048]{1,0:T(8,128)(2,1)}, bf16[192,2048]{1,0:T(8,128)(2,1)S(1)}, u32[]{:S(2)}, u32[]{:S(2)}) collective-permute-start(bf16[192,2048]{1,0:T(8,128)(2,1)} %get-tuple-element.157), channel_id=1, source_target_pairs={{0,8},{1,12},{4,9},{5,13},{8,0},{9,4},{12,1},{13,5},{2,10},{3,14},... | collective-permute-start | bytes 2359304 | tf_op jit(solution)/shard_map/ppermute | solution.py:850
  430.3 33.5 %collective-permute-start.15 = (bf16[192,2048]{1,0:T(8,128)(2,1)}, bf16[192,2048]{1,0:T(8,128)(2,1)}, u32[]{:S(2)}, u32[]{:S(2)}) collective-permute-start(bf16[192,2048]{1,0:T(8,128)(2,1)} %get-tuple-element.156.refs_1_), channel_id=1, source_target_pairs={{1,4},{4,1},{9,12},{12,9},{3,6},{6,3},{11,14},{14,11},{17,20},{20,... | collective-permute-start | bytes 2359304 | tf_op jit(solution)/shard_map/ppermute | solution.py:849
  431.8 40.1 %all-to-all-start.9 = ((bf16[8,4,24,768]{3,2,1,0:T(8,128)(2,1)}), bf16[8,4,24,768]{3,2,1,0:T(8,128)(2,1)S(1)}, u32[]{:S(2)}, u32[]{:S(2)}) async-start(bf16[8,4,24,768]{3,2,1,0:T(8,128)(2,1)} %bitcast.115.refs_14_), calls=%async_computation.10 | async-start | bytes 2359296 | tf_op jit(solution)/shard_map/all_to_all | solution.py:728
  492.0 20.5 %all-to-all-start.10 = ((bf16[4,24,3200]{2,1,0:T(8,128)(2,1)}), bf16[4,24,3200]{2,1,0:T(8,128)(2,1)S(1)}, u32[]{:S(2)}, u32[]{:S(2)}) async-start(bf16[4,24,3200]{2,1,0:T(8,128)(2,1)} %pad.44), calls=%async_computation.11 | async-start | bytes 1228800 | tf_op jit(solution)/shard_map/all_to_all | solution.py:728
  498.3 19.7 %collective-permute-start.18 = (bf16[256,768]{1,0:T(8,128)(2,1)}, bf16[256,768]{1,0:T(8,128)(2,1)S(1)}, u32[]{:S(2)}, u32[]{:S(2)}) collective-permute-start(bf16[256,768]{1,0:T(8,128)(2,1)} %get-tuple-element.171), channel_id=1, source_target_pairs={{0,8},{1,12},{4,9},{5,13},{8,0},{9,4},{12,1},{13,5},{2,10},{3,14},... | collective-permute-start | bytes 1179656 | tf_op jit(solution)/shard_map/ppermute | solution.py:850
  (50 other events, 347.9 us)
Sparse Core Ops, SparseCore 0:
  46.1 81.2 all-gather.4
  144.0 45.0 all-gather.6
  347.1 78.1 reduce-scatter.2
  428.0 42.8 reduce-scatter.4

commit v6 on v5

--- a/solution.py
+++ b/solution.py
@@ -1000,7 +1000,7 @@
     down_other = lax.ppermute(down_pair, "sc", swap)
 
     whole = (None, None)
-    rows_block = 128
+    rows_block = 256
     steps = (tokens_here // rows_block,)
     wide_block = ((rows_block, features), by_row)
     soft_block = ((rows_block, ROUTES + 4), by_row)
@@ -1060,12 +1060,12 @@
     down_parts_w = [p[:, 0] for p in regroup(down_pair, down_far, down_other, down_far_other)]
     far_rows = down_parts_w[0].shape[1]
     down_tile = pltpu.VMEM((2, 2, 2, far_rows, features), bf16)
-    row_tile = n_rows // 4
+    row_tile = n_rows // 2
     result_rows, _ = call(
         expert_result_kernel,
         "expert_result",
         8,
-        (4,),
+        (2,),
         [
             (me,) + whole,
             (hidden, (row_tile, hid), by_row),

time: 540 us -> 538 us (level)
  no operation moved by 1% of the time
where the time goes in v6:
time: 538 us; the launch traced here: 528 us
  Pallas kernels  232 us (43%)
  waiting for transfers between devices  141 us (26%)
  starting transfers between devices  68.8 us (13%)
  local copies, waits for them, and re-layouts  46 us (9%)
  between operations  21.9 us (4%)
  other arithmetic  18.5 us (3%)
    pallas_call x26, Pallas kernels, call(): pl.pallas_call(ordered, grid_spec=pltpu.PrefetchScalarGridSpec(num_scalar...  232 us
    all_to_all x11, waiting for transfers between devices, exchange(): return lax.all_to_all(blocks, axes, split_axis=0, concat_axis=0, tiled=True)  101 us
    all_to_all x11, starting transfers between devices, exchange(): return lax.all_to_all(blocks, axes, split_axis=0, concat_axis=0, tiled=True)  51.7 us
    unnamed x89, local copies, waits for them, and re-layouts  19.9 us
    ppermute x2, waiting for transfers between devices, to_owner(): lax.ppermute(other, ('b', 'd', 'sc'), unlike)  16.1 us
  transfers between devices with their start and end apart: 34, of which 14 were waited for; matrix products, arithmetic and copies ran while one was open for 8% of the time, Pallas kernels for 33%

profile of v6, /device:TPU:2, one launch (start us, length us, event | category | flops | bytes accessed | tf_op | source)
XLA Modules:
  0.0 528.4 jit_solution(10241551030468125113)
XLA Ops:
  23.0 6.7 %all-to-all-start = ((bf16[32,24,768]{2,1,0:T(8,128)(2,1)}), bf16[32,24,768]{2,1,0:T(8,128)(2,1)}, u32[]{:S(2)}, u32[]{:S(2)}) async-start(bf16[32,24,768]{2,1,0:T(8,128)(2,1)} %bitcast.14), calls=%async_computation | async-start | bytes 2359296 | tf_op jit(solution)/shard_map/all_to_all | solution.py:728
  49.6 8.9 %all-to-all-done = bf16[32,24,768]{2,1,0:T(8,128)(2,1)} async-done(((bf16[32,24,768]{2,1,0:T(8,128)(2,1)}), bf16[32,24,768]{2,1,0:T(8,128)(2,1)}, u32[]{:S(2)}, u32[]{:S(2)}) %all-to-all-start) | async-done | bytes 1179680 | tf_op jit(solution)/shard_map/all_to_all | solution.py:728
  72.4 26.5 %attend_forward.1 = (bf16[2048,768]{1,0:T(8,128)(2,1)}, bf16[2048,768]{1,0:T(8,128)(2,1)}, bf16[4,192,512]{2,1,0:T(8,128)(2,1)}, f32[192,2048]{1,0:T(8,128)}, f3...) custom-call(s32[4]{0:T(128)} %copy-done.35, ...), custom_call_target="tpu_custom_call" | custom-call | flops 149500000 | bytes 17673220 | tf_op jit(solution)/shard_map/attend_forward/pallas_call | solution.py:313
  119.2 8.2 %all-gather.5.cloned.1.call-done = bf16[4,2,96,2048]{3,2,1,0:T(8,128)(2,1)} async-done(((bf16[2,2,96,2048]{3,2,1,0:T(8,128)(2,1)}), bf16[4,2,96,2048]{3,2,1,0:T(8,128)(2,1)}) %all-gather.5.cloned.1.call-update) | async-done | bytes 3145744 | tf_op jit(solution)/shard_map/all_gather | solution.py:817
  127.4 9.7 %mid.1 = (f32[512,768]{1,0:T(8,128)}, f32[512,768]{1,0:T(8,128)}, f32[512,16]{1,0:T(8,128)}, bf16[8,160,768]{2,1,0:T(8,128)(2,1)}, f32[1,1]{1,0:T(1,128)}) custom-call(bf16[4,192,512]{2,1,0:T(8,128)(2,1)} %copy-done.9, bf16[512,768]{1,0:T(8,128)(2,1)} %refs_3_.2, bf16[768,768]{1,0:T(8,128)(2,1)} %copy.187.refs_2_.refs_6_, ...), custom_call_target="tpu_custom_call" | custom-call | flops 57500000 | bytes 7998468 | tf_op jit(solution)/shard_map/mid/pallas_call | solution.py:313
  147.2 32.0 %all-to-all-done.3 = bf16[8,160,768]{2,1,0:T(8,128)(2,1)S(1)} async-done(((bf16[8,160,768]{2,1,0:T(8,128)(2,1)}), bf16[8,160,768]{2,1,0:T(8,128)(2,1)S(1)}, u32[]{:S(2)}, u32[]{:S(2)}) %all-to-all-start.3) | async-done | bytes 1966112 | tf_op jit(solution)/shard_map/all_to_all | solution.py:728
  180.5 14.8 %expert_hidden.1 = (f32[1280,2048]{1,0:T(8,128)}, f32[1280,2048]{1,0:T(8,128)}, bf16[1280,2048]{1,0:T(8,128)(2,1)}, f32[1,1]{1,0:T(1,128)}) custom-call(s32[2]{0:T(128)} %pad_add_fusion.refs_0_, bf16[1280,768]{1,0:T(8,128)(2,1)} %bitcast.123, bf16[2,2,96,2048]{3,2,1,0:T(8,128)(2,1)} %get-tuple-element.99.refs_2_.refs_4_, bf16[2,2,96,2048]{3,2,1,0:T(8,128)(2,1)} %copy-done.4, ...), custom_call_target="tpu_custom_call" | custom-call | flops 80500000 | bytes 34471940 | tf_op jit(solution)/shard_map/expert_hidden/pallas_call | solution.py:313
  201.3 8.9 %expert_result.1 = (bf16[1280,768]{1,0:T(8,128)(2,1)}, f32[1,1]{1,0:T(1,128)}) custom-call(s32[2]{0:T(128)} %pad_add_fusion.refs_0_, bf16[1280,2048]{1,0:T(8,128)(2,1)} %get-tuple-element.109.refs_1_, bf16[2,256,768]{2,1,0:T(8,128)(2,1)} %bitcast.133, bf16[2,256,768]{2,1,0:T(8,128)(2,1)} %get-tuple-element.245.refs_3_.refs_9_, ...), custom_call_target="tpu_custom_call" | custom-call | flops 46000000 | bytes 10354692 | tf_op jit(solution)/shard_map/expert_result/pallas_call | solution.py:313
  220.3 20.8 %all-to-all-done.4.refs_0_ = bf16[8,160,768]{2,1,0:T(8,128)(2,1)S(1)} async-done(((bf16[8,160,768]{2,1,0:T(8,128)(2,1)}), bf16[8,160,768]{2,1,0:T(8,128)(2,1)S(1)}, u32[]{:S(2)}, u32[]{:S(2)}) %all-to-all-start.4) | async-done | bytes 1966112 | tf_op jit(solution)/shard_map/all_to_all | solution.py:728
  242.4 10.6 %loss.1 = (bf16[512,768]{1,0:T(8,128)(2,1)}, f32[512,768]{1,0:T(8,128)}, f32[512,8]{1,0:T(8,128)}, bf16[8,160,768]{2,1,0:T(8,128)(2,1)}, f32[1,768]{1,0:T(1,128)}, /*index=5*/f32[1,1]{1,0:T(1,128)}) custom-call(bf16[8,160,768]{2,1,0:T(8,128)(2,1)} %copy-done.8, s32[512,2]{1,0:T(8,128)} %copy-done.13, s32[8,512]{1,0:T(8,128)} %pad.41.clone.refs_6_.refs_2_, ...), custom_call_target="tpu_custom_call" | custom-call | flops 63250000 | bytes 10308616 | tf_op jit(solution)/shard_map/loss/pallas_call | solution.py:313
  257.7 11.9 %route.1 = (f32[512,768]{1,0:T(8,128)}, f32[768,16]{1,0:T(8,128)}, f32[768,16]{1,0:T(8,128)}, f32[1,1]{1,0:T(1,128)}) custom-call(f32[512,16]{1,0:T(8,128)} %get-tuple-element.112.refs_4_.refs_0_, s32[512,2]{1,0:T(8,128)} %copy-done.6, f32[512,8]{1,0:T(8,128)} %get-tuple-element.119.refs_2_, f32[512,768]{1,0:T(8,128)} %get-tuple-element.120.refs_3_.refs_4_, ...), custom_call_target="tpu_custom_call" | custom-call | flops 80500000 | bytes 4919300 | tf_op jit(solution)/shard_map/route/pallas_call | solution.py:313
  269.6 11.1 %all-to-all-done.5 = bf16[8,160,768]{2,1,0:T(8,128)(2,1)S(1)} async-done(((bf16[8,160,768]{2,1,0:T(8,128)(2,1)}), bf16[8,160,768]{2,1,0:T(8,128)(2,1)S(1)}, u32[]{:S(2)}, u32[]{:S(2)}) %all-to-all-start.5) | async-done | bytes 1966112 | tf_op jit(solution)/shard_map/all_to_all | solution.py:728
  282.1 25.5 %expert_backward.1 = (bf16[1280,2048]{1,0:T(8,128)(2,1)}, bf16[1280,2048]{1,0:T(8,128)(2,1)}, bf16[1280,768]{1,0:T(8,128)(2,1)}, f32[1,1]{1,0:T(1,128)}) custom-call(s32[2]{0:T(128)} %pad_add_fusion.refs_0_, bf16[1280,768]{1,0:T(8,128)(2,1)} %bitcast.127, f32[1280,2048]{1,0:T(8,128)} %get-tuple-element.117.refs_2_, f32[1280,2048]{1,0:T(8,128)} %get-tuple-element.118.refs_3_, ...), custom_call_target="tpu_custom_call" | custom-call | flops 115000000 | bytes 44826628 | tf_op jit(solution)/shard_map/expert_backward/pallas_call | solution.py:313
  307.6 5.1 all-to-all-start.6
  312.7 9.5 %gate_grad.1 = (bf16[4,96,2048]{2,1,0:T(8,128)(2,1)}, bf16[4,96,2048]{2,1,0:T(8,128)(2,1)}, f32[1,1]{1,0:T(1,128)}) custom-call(s32[2]{0:T(128)} %pad_add_fusion.refs_0_, bf16[1280,768]{1,0:T(8,128)(2,1)} %bitcast.124, bf16[1280,2048]{1,0:T(8,128)(2,1)} %get-tuple-element.123.refs_2_, bf16[1280,768]{1,0:T(8,128)(2,1)} %get-tuple-element.122.refs_3_), custom_call_target="tpu_custom_call" | custom-call | flops 46000000 | bytes 10354692 | tf_op jit(solution)/shard_map/gate_grad/pallas_call | solution.py:313
  322.2 9.5 %up_grad.1 = (bf16[4,96,2048]{2,1,0:T(8,128)(2,1)}, bf16[4,96,2048]{2,1,0:T(8,128)(2,1)}, f32[1,1]{1,0:T(1,128)}) custom-call(s32[2]{0:T(128)} %pad_add_fusion.refs_0_, bf16[1280,768]{1,0:T(8,128)(2,1)} %bitcast.125, bf16[1280,2048]{1,0:T(8,128)(2,1)} %get-tuple-element.126.refs_2_, bf16[4,96,2048]{2,1,0:T(8,128)(2,1)} %get-tuple-element.124.refs_3_.refs_0_), custom_call_target="tpu_custom_call" | custom-call | flops 46000000 | bytes 10354692 | tf_op jit(solution)/shard_map/up_grad/pallas_call | solution.py:313
  332.2 9.0 %down_grad.1 = (bf16[4,256,768]{2,1,0:T(8,128)(2,1)}, bf16[4,256,768]{2,1,0:T(8,128)(2,1)}, f32[1,1]{1,0:T(1,128)}) custom-call(s32[2]{0:T(128)} %pad_add_fusion.refs_0_, bf16[1280,2048]{1,0:T(8,128)(2,1)} %get-tuple-element.109.refs_1_, bf16[1280,768]{1,0:T(8,128)(2,1)} %bitcast.128, bf16[4,96,2048]{2,1,0:T(8,128)(2,1)} %get-tuple-element.127.refs_3_.refs_2_), custom_call_target="tpu_custom_call" | custom-call | flops 46000000 | bytes 10354692 | tf_op jit(solution)/shard_map/down_grad/pallas_call | solution.py:313
  351.8 8.6 %join.1 = (f32[512,768]{1,0:T(8,128)}, bf16[512,768]{1,0:T(8,128)(2,1)}, bf16[4,192,512]{2,1,0:T(8,128)(2,1)}, f32[1,768]{1,0:T(1,128)}, f32[1,1]{1,0:T(1,128)}) custom-call(bf16[8,160,768]{2,1,0:T(8,128)(2,1)} %copy-done.7, s32[512,2]{1,0:T(8,128)} %copy-done.13, f32[512,768]{1,0:T(8,128)} %get-tuple-element.121.refs_12_.refs_2_, ...), custom_call_target="tpu_custom_call" | custom-call | flops 46000000 | bytes 11020292 | tf_op jit(solution)/shard_map/join/pallas_call | solution.py:313
  374.8 37.9 %attend_backward.1 = (f32[2,512,768]{2,1,0:T(8,128)}, bf16[2,512,768]{2,1,0:T(8,128)(2,1)}, bf16[768,640]{1,0:T(8,128)(2,1)}, f32[1,1]{1,0:T(1,128)}) custom-call(s32[4]{0:T(128)} %copy-done.35, bf16[4,192,512]{2,1,0:T(8,128)(2,1)} %copy-done.21, f32[192,2048]{1,0:T(8,128)} %get-tuple-element.132.refs_2_, f32[8,2048]{1,0:T(8,128)} %get-tuple-element.133.refs_3_, ...), custom_call_target="tpu_custom_call" | custom-call | flops 43699998720 | bytes 19341316 | tf_op jit(solution)/shard_map/attend_backward/pallas_call | solution.py:313
  430.5 5.8 %all-to-all-start.9 = ((bf16[8,4,24,768]{3,2,1,0:T(8,128)(2,1)}), bf16[8,4,24,768]{3,2,1,0:T(8,128)(2,1)S(1)}, u32[]{:S(2)}, u32[]{:S(2)}) async-start(bf16[8,4,24,768]{3,2,1,0:T(8,128)(2,1)} %bitcast.115.refs_14_), calls=%async_computation.10 | async-start | bytes 2359296 | tf_op jit(solution)/shard_map/all_to_all | solution.py:728
  436.3 5.4 %collective-permute-done.14.refs_1_ = bf16[512,768]{1,0:T(8,128)(2,1)S(1)} collective-permute-done((bf16[512,768]{1,0:T(8,128)(2,1)}, bf16[512,768]{1,0:T(8,128)(2,1)S(1)}, u32[]{:S(2)}, u32[]{:S(2)}) %collective-permute-start.14) | collective-permute-done | bytes 786464 | tf_op jit(solution)/shard_map/ppermute | solution.py:1282
  446.8 16.1 %collective-permute-done.16.refs_3_ = bf16[192,2048]{1,0:T(8,128)(2,1)S(1)} collective-permute-done((bf16[192,2048]{1,0:T(8,128)(2,1)}, bf16[192,2048]{1,0:T(8,128)(2,1)S(1)}, u32[]{:S(2)}, u32[]{:S(2)}) %collective-permute-start.16) | collective-permute-done | bytes 786464 | tf_op jit(solution)/shard_map/ppermute | solution.py:850
  475.7 13.0 %all-to-all-done.8 = bf16[8,4,24,640]{3,2,1,0:T(8,128)(2,1)S(1)} async-done(((bf16[8,4,24,640]{3,2,1,0:T(8,128)(2,1)}), bf16[8,4,24,640]{3,2,1,0:T(8,128)(2,1)S(1)}, u32[]{:S(2)}, u32[]{:S(2)}) %all-to-all-start.8) | async-done | bytes 983072 | tf_op jit(solution)/shard_map/all_to_all | solution.py:728
  499.9 11.7 %all-to-all-done.10.refs_0_ = bf16[4,24,3200]{2,1,0:T(8,128)(2,1)S(1)} async-done(((bf16[4,24,3200]{2,1,0:T(8,128)(2,1)}), bf16[4,24,3200]{2,1,0:T(8,128)(2,1)S(1)}, u32[]{:S(2)}, u32[]{:S(2)}) %all-to-all-start.10) | async-done | bytes 614432 | tf_op jit(solution)/shard_map/all_to_all | solution.py:728
  (251 shorter events, 179.1 us)
Async XLA Ops:
  9.2 21.4 %collective-permute-start = (bf16[1,528,768]{2,1,0:T(8,128)(2,1)S(1)}, bf16[1,528,768]{2,1,0:T(8,128)(2,1)S(1)}, u32[]{:S(2)}, u32[]{:S(2)}) collective-permute-start(bf16[1,528,768]{2,1,0:T(8,128)(2,1)S(1)} %fusion.4), channel_id=1, source_target_pairs={{0,2},{1,3},{2,0},{3,1},{4,6},{5,7},{6,4},{7,5},{8,10},{9,11},{10,... | collective-permute-start | bytes 2433032 | tf_op jit(solution)/shard_map/ppermute | solution.py:740
  12.9 28.6 %collective-permute-start.3 = (bf16[2,96,2048]{2,1,0:T(8,128)(2,1)}, bf16[2,96,2048]{2,1,0:T(8,128)(2,1)}, u32[]{:S(2)}, u32[]{:S(2)}) collective-permute-start(bf16[2,96,2048]{2,1,0:T(8,128)(2,1)} %get-tuple-element.98), channel_id=1, source_target_pairs={{0,8},{1,12},{4,9},{5,13},{8,0},{9,4},{12,1},{13,5},{2,10},{3,14},... | collective-permute-start | bytes 2359304 | tf_op jit(solution)/shard_map/ppermute | solution.py:800
  15.0 26.5 %collective-permute-start.2 = (bf16[2,96,2048]{2,1,0:T(8,128)(2,1)}, bf16[2,96,2048]{2,1,0:T(8,128)(2,1)}, u32[]{:S(2)}, u32[]{:S(2)}) collective-permute-start(bf16[2,96,2048]{2,1,0:T(8,128)(2,1)} %get-tuple-element.97.refs_1_), channel_id=1, source_target_pairs={{1,4},{4,1},{9,12},{12,9},{3,6},{6,3},{11,14},{14,11},{17,20},{20,... | collective-permute-start | bytes 2359304 | tf_op jit(solution)/shard_map/ppermute | solution.py:799
  23.0 35.5 %all-to-all-start = ((bf16[32,24,768]{2,1,0:T(8,128)(2,1)}), bf16[32,24,768]{2,1,0:T(8,128)(2,1)}, u32[]{:S(2)}, u32[]{:S(2)}) async-start(bf16[32,24,768]{2,1,0:T(8,128)(2,1)} %bitcast.14), calls=%async_computation | async-start | bytes 2359296 | tf_op jit(solution)/shard_map/all_to_all | solution.py:728
  29.7 97.8 %all-gather.5.cloned.1.call-start = ((), (), s32[]{:S(2)}) async-start(), calls=%async_computation.15 | async-start | bytes 4718592 | tf_op jit(solution)/shard_map/all_gather | solution.py:817
  47.4 23.8 %collective-permute-start.4 = (bf16[2,2,96,2048]{3,2,1,0:T(8,128)(2,1)S(1)}, bf16[2,2,96,2048]{3,2,1,0:T(8,128)(2,1)S(1)}, u32[]{:S(2)}, u32[]{:S(2)}) collective-permute-start(bf16[2,2,96,2048]{3,2,1,0:T(8,128)(2,1)S(1)} %copy-done.2), channel_id=1, source_target_pairs={{0,1},{1,0},{2,3},{3,2},{4,5},{5,4},{6,7},{7,6},{8,9},{9,8},{10,11... | collective-permute-start | bytes 4718600 | tf_op jit(solution)/shard_map/ppermute | solution.py:933
  62.0 43.3 %all-to-all-start.2 = ((bf16[8,768,128]{2,1,0:T(8,128)(2,1)}), bf16[8,768,128]{2,1,0:T(8,128)(2,1)}, u32[]{:S(2)}, u32[]{:S(2)}) async-start(bf16[8,768,128]{2,1,0:T(8,128)(2,1)} %get-tuple-element.101), calls=%async_computation.2 | async-start | bytes 3145728 | tf_op jit(solution)/shard_map/all_to_all | solution.py:728
  68.7 30.3 %collective-permute-start.6 = (bf16[1,256,768]{2,1,0:T(8,128)(2,1)}, bf16[1,256,768]{2,1,0:T(8,128)(2,1)S(1)}, u32[]{:S(2)}, u32[]{:S(2)}) collective-permute-start(bf16[1,256,768]{2,1,0:T(8,128)(2,1)} %get-tuple-element.104), channel_id=1, source_target_pairs={{0,8},{1,12},{4,9},{5,13},{8,0},{9,4},{12,1},{13,5},{2,10},{3,14},... | collective-permute-start | bytes 1179656 | tf_op jit(solution)/shard_map/ppermute | solution.py:800
  69.1 29.8 %collective-permute-start.5 = (bf16[1,256,768]{2,1,0:T(8,128)(2,1)}, bf16[1,256,768]{2,1,0:T(8,128)(2,1)S(1)}, u32[]{:S(2)}, u32[]{:S(2)}) collective-permute-start(bf16[1,256,768]{2,1,0:T(8,128)(2,1)} %get-tuple-element.103.refs_1_), channel_id=1, source_target_pairs={{1,4},{4,1},{9,12},{12,9},{3,6},{6,3},{11,14},{14,11},{17,20},{20,... | collective-permute-start | bytes 1179656 | tf_op jit(solution)/shard_map/ppermute | solution.py:799
  137.2 42.0 %all-to-all-start.3 = ((bf16[8,160,768]{2,1,0:T(8,128)(2,1)}), bf16[8,160,768]{2,1,0:T(8,128)(2,1)S(1)}, u32[]{:S(2)}, u32[]{:S(2)}) async-start(bf16[8,160,768]{2,1,0:T(8,128)(2,1)} %get-tuple-element.107), calls=%async_computation.3 | async-start | bytes 3932160 | tf_op jit(solution)/shard_map/all_to_all | solution.py:728
  141.4 54.6 %all-gather.7.cloned.1.call-start = ((), (), s32[]{:S(2)}) async-start(), calls=%async_computation.16 | async-start | bytes 2359296 | tf_op jit(solution)/shard_map/all_gather | solution.py:817
  210.2 30.9 %all-to-all-start.4 = ((bf16[8,160,768]{2,1,0:T(8,128)(2,1)}), bf16[8,160,768]{2,1,0:T(8,128)(2,1)S(1)}, u32[]{:S(2)}, u32[]{:S(2)}) async-start(bf16[8,160,768]{2,1,0:T(8,128)(2,1)} %bitcast.146), calls=%async_computation.4 | async-start | bytes 3932160 | tf_op jit(solution)/shard_map/all_to_all | solution.py:728
  253.0 27.7 %all-to-all-start.5 = ((bf16[8,160,768]{2,1,0:T(8,128)(2,1)}), bf16[8,160,768]{2,1,0:T(8,128)(2,1)S(1)}, u32[]{:S(2)}, u32[]{:S(2)}) async-start(bf16[8,160,768]{2,1,0:T(8,128)(2,1)} %get-tuple-element.116), calls=%async_computation.5 | async-start | bytes 3932160 | tf_op jit(solution)/shard_map/all_to_all | solution.py:728
  307.6 42.9 %all-to-all-start.6 = ((bf16[8,160,768]{2,1,0:T(8,128)(2,1)}), bf16[8,160,768]{2,1,0:T(8,128)(2,1)S(1)}, u32[]{:S(2)}, u32[]{:S(2)}) async-start(bf16[8,160,768]{2,1,0:T(8,128)(2,1)} %bitcast.129), calls=%async_computation.6 | async-start | bytes 3932160 | tf_op jit(solution)/shard_map/all_to_all | solution.py:728
  312.7 111.9 %reduce-scatter.3.cloned.1.call-start = ((), (), s32[]{:S(2)}) async-start(), calls=%async_computation.13 | async-start | bytes 4718592 | tf_op jit(solution)/shard_map/reduce_scatter | solution.py:832
  322.2 19.0 %collective-permute-start.10 = (bf16[4,1,96,2048]{3,2,0,1:T(8,128)(2,1)}, bf16[4,1,96,2048]{3,2,0,1:T(8,128)(2,1)}, u32[]{:S(2)}, u32[]{:S(2)}) collective-permute-start(bf16[4,1,96,2048]{3,2,0,1:T(8,128)(2,1)} %bitcast.171), channel_id=1, source_target_pairs={{0,1},{1,0},{2,3},{3,2},{4,5},{5,4},{6,7},{7,6},{8,9},{9,8},{10,11... | collective-permute-start | bytes 4718600 | tf_op jit(solution)/shard_map/ppermute | solution.py:1183
  341.2 30.5 %collective-permute-start.12 = (bf16[4,1,256,768]{3,2,0,1:T(8,128)(2,1)}, bf16[4,1,256,768]{3,2,0,1:T(8,128)(2,1)S(1)}, u32[]{:S(2)}, u32[]{:S(2)}) collective-permute-start(bf16[4,1,256,768]{3,2,0,1:T(8,128)(2,1)} %bitcast.170), channel_id=1, source_target_pairs={{0,1},{1,0},{2,3},{3,2},{4,5},{5,4},{6,7},{7,6},{8,9},{9,8},{10,11... | collective-permute-start | bytes 4718600 | tf_op jit(solution)/shard_map/ppermute | solution.py:826
  363.9 130.7 %reduce-scatter.5.cloned.1.call-start = ((), (), s32[]{:S(2)}) async-start(), calls=%async_computation.14 | async-start | bytes 2359296 | tf_op jit(solution)/shard_map/reduce_scatter | solution.py:832
  421.0 20.6 %collective-permute-start.14 = (bf16[512,768]{1,0:T(8,128)(2,1)}, bf16[512,768]{1,0:T(8,128)(2,1)S(1)}, u32[]{:S(2)}, u32[]{:S(2)}) collective-permute-start(bf16[512,768]{1,0:T(8,128)(2,1)} %get-tuple-element.152), channel_id=1, source_target_pairs={{0,2},{1,3},{2,0},{3,1},{4,6},{5,7},{6,4},{7,5},{8,10},{9,11},{10,... | collective-permute-start | bytes 2359304 | tf_op jit(solution)/shard_map/ppermute | solution.py:1282
  429.0 33.9 %collective-permute-start.16 = (bf16[192,2048]{1,0:T(8,128)(2,1)}, bf16[192,2048]{1,0:T(8,128)(2,1)S(1)}, u32[]{:S(2)}, u32[]{:S(2)}) collective-permute-start(bf16[192,2048]{1,0:T(8,128)(2,1)} %get-tuple-element.157), channel_id=1, source_target_pairs={{0,8},{1,12},{4,9},{5,13},{8,0},{9,4},{12,1},{13,5},{2,10},{3,14},... | collective-permute-start | bytes 2359304 | tf_op jit(solution)/shard_map/ppermute | solution.py:850
  429.0 33.9 %collective-permute-start.15 = (bf16[192,2048]{1,0:T(8,128)(2,1)}, bf16[192,2048]{1,0:T(8,128)(2,1)}, u32[]{:S(2)}, u32[]{:S(2)}) collective-permute-start(bf16[192,2048]{1,0:T(8,128)(2,1)} %get-tuple-element.156.refs_1_), channel_id=1, source_target_pairs={{1,4},{4,1},{9,12},{12,9},{3,6},{6,3},{11,14},{14,11},{17,20},{20,... | collective-permute-start | bytes 2359304 | tf_op jit(solution)/shard_map/ppermute | solution.py:849
  430.5 40.5 %all-to-all-start.9 = ((bf16[8,4,24,768]{3,2,1,0:T(8,128)(2,1)}), bf16[8,4,24,768]{3,2,1,0:T(8,128)(2,1)S(1)}, u32[]{:S(2)}, u32[]{:S(2)}) async-start(bf16[8,4,24,768]{3,2,1,0:T(8,128)(2,1)} %bitcast.115.refs_14_), calls=%async_computation.10 | async-start | bytes 2359296 | tf_op jit(solution)/shard_map/all_to_all | solution.py:728
  491.1 20.5 %all-to-all-start.10 = ((bf16[4,24,3200]{2,1,0:T(8,128)(2,1)}), bf16[4,24,3200]{2,1,0:T(8,128)(2,1)S(1)}, u32[]{:S(2)}, u32[]{:S(2)}) async-start(bf16[4,24,3200]{2,1,0:T(8,128)(2,1)} %pad.44), calls=%async_computation.11 | async-start | bytes 1228800 | tf_op jit(solution)/shard_map/all_to_all | solution.py:728
  497.2 19.9 %collective-permute-start.18 = (bf16[256,768]{1,0:T(8,128)(2,1)}, bf16[256,768]{1,0:T(8,128)(2,1)S(1)}, u32[]{:S(2)}, u32[]{:S(2)}) collective-permute-start(bf16[256,768]{1,0:T(8,128)(2,1)} %get-tuple-element.171), channel_id=1, source_target_pairs={{0,8},{1,12},{4,9},{5,13},{8,0},{9,4},{12,1},{13,5},{2,10},{3,14},... | collective-permute-start | bytes 1179656 | tf_op jit(solution)/shard_map/ppermute | solution.py:850
  (50 other events, 349.7 us)
Sparse Core Ops, SparseCore 0:
  46.1 81.2 all-gather.4
  143.8 45.0 all-gather.6
  346.5 78.1 reduce-scatter.2
  427.4 42.8 reduce-scatter.4
